TPU v7x, 128 devices: a whole 4x4x4 slice. The times are simulated.
128 devices in a mesh: dom: 8 (over y, core), order: 16 (over z, x).
Axes of the slice: x: 4, y: 4, z: 4, core: 2. Of those that a mesh axis runs over, the one named last changes fastest.
Arguments:
- ssh: float32 [8192, 16, 256], P(('dom', 'order')), may hold values from -6 to 6
- cell_count: int32 [8192], P(('dom', 'order')), may hold values from 1 to 256, 1572864 in all
- remap_index: int32 [8192, 4, 256], P(('dom', 'order')), may hold values from 0 to 255
- remap_weight: float32 [8192, 4, 256], P(('dom', 'order')), may hold values from 0.1 to 0.6
- block_tile: int32 [8192], P(('dom', 'order')), may hold values from 0 to 32767, as said below
- gauss_weight: float32 [1024], replicated, may hold values from 0.2 to 2
- love: float32 [1024], replicated, may hold values from 0.3 to 3
- legendre: bfloat16 [1024, 1024, 1024], P(('dom', 'order')), may hold values from -0.1875 to 0.1875
Outputs:
- sal: float32 [8192, 16, 256], P(('dom', 'order'))
Inputs may be any that keep to these rules, and one draw needn't show every extreme that they name: Block rows p * 64 to (p + 1) * 64 - 1 name tiles whose owner block_tile // 256 is p - 1, p or p + 1; exactly 32 of them name owner p, and at most 32 name each of the other two.
All inputs are finite; a program needn't handle non-finite values. No bound on the sum of `cell_count` on one device may be relied on, other than what follows from the above.
Results may differ from a plain program's by a relative error of at most 0.006.
Values may be sent and summed in bfloat16 or wider, within the bound.
No kernel may reach another device: no remote copies, remote signals or barrier semaphores. Data moves between devices by JAX's collectives and lax.ppermute only.
A program may use at most 192 MiB of HBM per device.

v0:
```python
import math

import jax
import jax.numpy as jnp
from jax import lax
from jax.sharding import PartitionSpec as P

NLON = 4096
ORDERS = 1024
BLOCK = 256
LAT_DEV = 16
CAP = 32
TILE_DEV = 256


def from_behind(value, axis, steps):
    count = lax.axis_size(axis)
    leading, last = (max(0, -steps), min(count, count - steps))
    return lax.ppermute(value, axis, [(source, source + steps) for source in range(leading, last)])


def cell_matrix(remap_index, remap_weight, cell_count):
    block_count, point_count, num_cells = remap_index.shape
    points = lax.broadcasted_iota(jnp.int32, (1, 1, num_cells), 2)
    cell_idx = lax.broadcasted_iota(jnp.int32, (block_count, num_cells), 1)
    live_mask = (cell_idx < cell_count[:, None]).astype(jnp.float32)
    matrix = jnp.zeros((block_count, num_cells, num_cells), jnp.float32)
    for kpoint in range(point_count):
        hit_mask = remap_index[:, kpoint, :, None] == points
        matrix = matrix + jnp.where(hit_mask, remap_weight[:, kpoint, :, None], jnp.float32(0.0))
    return matrix * live_mask[:, :, None]


def fourier_tables(circle_len, order_count, tile_len):
    spots = lax.broadcasted_iota(jnp.int32, (circle_len, order_count), 0)
    waves = lax.broadcasted_iota(jnp.int32, (circle_len, order_count), 1)
    phase_idx = spots * waves % circle_len
    angles = phase_idx.astype(jnp.float32) * jnp.float32(2.0 * math.pi / circle_len)
    cosine = jnp.cos(angles)
    sine_part = jnp.sin(angles)
    forward = jnp.stack([cosine, -sine_part], axis=1) / jnp.float32(circle_len)
    forward = forward.reshape(circle_len // tile_len, tile_len, 2, order_count)
    factor = jnp.where(waves == 0, jnp.float32(1.0), jnp.float32(2.0))
    inverse = jnp.stack([cosine * factor, -sine_part * factor], axis=0)
    inverse = inverse.reshape(2, circle_len // tile_len, tile_len, order_count)
    return (forward, inverse)


def split_table(table):
    upper_part = table.astype(jnp.bfloat16)
    lower_part = (table - upper_part.astype(jnp.float32)).astype(jnp.bfloat16)
    return (upper_part, lower_part)


def slot_select(offset, local_tile, direction, capacity):
    is_target = (offset == direction).astype(jnp.int32)
    position = jnp.cumsum(is_target) - 1
    slot_idx = lax.broadcasted_iota(jnp.int32, (capacity, offset.shape[0]), 0)
    chosen = (is_target[None, :] == 1) & (position[None, :] == slot_idx)
    tile_ids = jnp.sum(jnp.where(chosen, local_tile[None, :], 0), axis=1)
    tile_ids = jnp.where(jnp.any(chosen, axis=1), tile_ids, -1)
    return (chosen.astype(jnp.float32), tile_ids)


def tile_onehot(tile_ids, tile_count):
    columns = lax.broadcasted_iota(jnp.int32, (tile_ids.shape[0], tile_count), 1)
    return (tile_ids[:, None] == columns).astype(jnp.float32)


def legendre_local(tables, by_order, gauss_weight, love, first_order):
    order_count, half_lats, degree_count = tables.shape
    north_rows = by_order[:, :half_lats, :].astype(jnp.float32)
    south_rows = jnp.flip(by_order[:, half_lats:, :], axis=1).astype(jnp.float32)
    weights_col = gauss_weight[None, :, None]
    even_in = ((north_rows + south_rows) * weights_col).astype(jnp.bfloat16)
    odd_in = ((north_rows - south_rows) * weights_col).astype(jnp.bfloat16)
    even_coef = jnp.einsum("ojl,ojc->olc", tables, even_in, preferred_element_type=jnp.float32)
    odd_coef = jnp.einsum("ojl,ojc->olc", tables, odd_in, preferred_element_type=jnp.float32)
    degree = lax.broadcasted_iota(jnp.int32, (order_count, degree_count, 1), 1)
    order_ids = first_order + lax.broadcasted_iota(jnp.int32, (order_count, degree_count, 1), 0)
    is_even = (degree + order_ids) % 2 == 0
    coefficient = jnp.where(
        degree < order_ids, jnp.float32(0.0), jnp.where(is_even, even_coef, odd_coef)
    )
    coefficient = (coefficient * love[None, :, None]).astype(jnp.bfloat16)
    even_part = jnp.where(is_even, coefficient, jnp.zeros_like(coefficient))
    odd_part = jnp.where(is_even, jnp.zeros_like(coefficient), coefficient)
    even_out = jnp.einsum("ojl,olc->ojc", tables, even_part, preferred_element_type=jnp.float32)
    odd_out = jnp.einsum("ojl,olc->ojc", tables, odd_part, preferred_element_type=jnp.float32)
    upper_rows = even_out + odd_out
    lower_rows = jnp.flip(even_out - odd_out, axis=1)
    return jnp.concatenate([upper_rows, lower_rows], axis=1).astype(jnp.bfloat16)


def on_device(ssh, cell_count, remap_index, remap_weight, block_tile, gauss_weight, love, legendre):
    highest = lax.Precision.HIGHEST
    order_local, half_lats, degree_count = legendre.shape
    lat_total = 2 * half_lats
    rank_here = lax.axis_index(("dom", "order"))
    field_count = ssh.shape[1]
    matrix = cell_matrix(remap_index, remap_weight, cell_count)
    spread = jnp.einsum("bfc,bcp->bfp", ssh, matrix, precision=highest)
    owner_rank = block_tile // TILE_DEV
    local_tile = block_tile % TILE_DEV
    offset = owner_rank - rank_here
    own_onehot = tile_onehot(jnp.where(offset == 0, local_tile, -1), TILE_DEV)
    select_up, ids_up = slot_select(offset, local_tile, 1, CAP)
    select_down, ids_down = slot_select(offset, local_tile, -1, CAP)
    buffer_up = jnp.einsum("sb,bfp->sfp", select_up, spread, precision=highest)
    buffer_down = jnp.einsum("sb,bfp->sfp", select_down, spread, precision=highest)
    from_lower, lower_ids = from_behind((buffer_up, ids_up), ("dom", "order"), 1)
    from_upper, upper_ids = from_behind((buffer_down, ids_down), ("dom", "order"), -1)
    lower_onehot = tile_onehot(lower_ids, TILE_DEV)
    upper_onehot = tile_onehot(upper_ids, TILE_DEV)
    grid_tiles = jnp.einsum("bt,bfp->tfp", own_onehot, spread, precision=highest)
    grid_tiles = grid_tiles + jnp.einsum("st,sfp->tfp", lower_onehot, from_lower, precision=highest)
    grid_tiles = grid_tiles + jnp.einsum("st,sfp->tfp", upper_onehot, from_upper, precision=highest)
    grid_vals = grid_tiles.reshape(LAT_DEV, NLON // BLOCK, field_count, BLOCK)
    forward, inverse = fourier_tables(NLON, ORDERS, BLOCK)
    fourier = jnp.einsum(
        "rsfb,sbcm->rfcm", grid_vals, forward, precision=lax.Precision.HIGH
    ).astype(jnp.bfloat16)
    lat_major = lax.all_to_all(fourier, ("dom", "order"), split_axis=3, concat_axis=0, tiled=True)
    by_order = lat_major.transpose(3, 0, 1, 2).reshape(order_local, lat_total, field_count * 2)
    synth = legendre_local(legendre, by_order, gauss_weight, love, rank_here * order_local)
    synth_lats = synth.reshape(order_local, lat_total, field_count, 2).transpose(1, 2, 3, 0)
    returned = lax.all_to_all(synth_lats, ("dom", "order"), split_axis=0, concat_axis=3, tiled=True)
    inv_upper, inv_lower = split_table(inverse)
    load_grid = jnp.einsum(
        "rfcm,csbm->rsfb", returned, inv_upper, preferred_element_type=jnp.float32
    )
    load_grid = load_grid + jnp.einsum(
        "rfcm,csbm->rsfb", returned, inv_lower, preferred_element_type=jnp.float32
    )
    load_tiles = load_grid.reshape(TILE_DEV, field_count, BLOCK)
    values_lower = jnp.einsum("st,tfp->sfp", lower_onehot, load_tiles, precision=highest)
    values_upper = jnp.einsum("st,tfp->sfp", upper_onehot, load_tiles, precision=highest)
    back_up = from_behind(values_lower, ("dom", "order"), -1)
    back_down = from_behind(values_upper, ("dom", "order"), 1)
    block_vals = jnp.einsum("bt,tfp->bfp", own_onehot, load_tiles, precision=highest)
    block_vals = block_vals + jnp.einsum("sb,sfp->bfp", select_up, back_up, precision=highest)
    block_vals = block_vals + jnp.einsum("sb,sfp->bfp", select_down, back_down, precision=highest)
    return jnp.einsum("bcp,bfp->bfc", matrix, block_vals, precision=highest)


def solution(mesh):
    return jax.shard_map(
        on_device,
        mesh=mesh,
        in_specs=(
            P(("dom", "order"), None, None),
            P(("dom", "order")),
            P(("dom", "order"), None, None),
            P(("dom", "order"), None, None),
            P(("dom", "order")),
            P(),
            P(),
            P(("dom", "order"), None, None),
        ),
        out_specs=P(("dom", "order"), None, None),
        check_vma=False,
    )
```

profile of v0, /device:TPU:1, one launch (start us, length us, event | category | flops | bytes accessed | tf_op | source)
XLA Modules:
  0.0 546.0 jit_solution(16333014757575452161)
XLA Ops:
  0.0 1.5 fusion.153
  1.6 1.7 fusion.152
  3.2 0.7 fusion.99
  4.0 0.7 fusion.141
  4.7 0.1 copy.106
  4.8 0.1 reduce-window.16
  4.8 0.1 add_reduce_fusion.1
  5.1 36.3 %fusion.67 = f32[64,16,256]{2,1,0:T(8,128)S(1)} fusion(f32[64,16,256]{2,1,0:T(8,128)S(1)} %copy-done, f32[64,256]{1,0:T(8,128)S(1)} %fusion.99, f32[64,256]{1,0:T(8,128)S(1)} %get-tuple-element.30, s32[64,256]{1,0:T(8,128)S(1)} %get-tuple-element.34, f32[64,256]{1,0:T(8,128)S(1)} %get-tuple-element.31, s32[64,256]{1,0:T(8,128)S(1)} %get-tuple-element.35, ...), kind=kOutput, calls=%fused_computation.81 | convolution fusion | flops 855638016 | bytes 2686976 | tf_op jit(solution)/shard_map/bfc,bcp->bfp/dot_general | solution.py:102
  41.4 1.1 fusion.76
  42.5 4.0 collective-permute-start.1
  46.5 0.1 fusion.120
  46.6 0.1 copy.108
  46.7 0.1 reduce-window.17
  46.8 0.1 add_reduce_fusion
  47.0 0.1 select_reduce_fusion
  47.1 3.1 collective-permute-start
  50.2 1.1 fusion.74
  51.3 6.0 %collective-permute-start.3 = (f32[32,16,256]{2,0,1:T(8,128)S(1)}, f32[32,16,256]{2,0,1:T(8,128)S(1)}, u32[]{:S(2)}, u32[]{:S(2)}) collective-permute-start(f32[32,16,256]{2,0,1:T(8,128)S(1)} %fusion.74), channel_id=1, source_target_pairs={{1,0},{2,1},{3,2},{4,3},{5,4},{6,5},{7,6},{8,7},{9,8},{10,9},{11,1... | collective-permute-start | bytes 1572872 | tf_op jit(solution)/shard_map/ppermute | solution.py:19
  57.4 0.1 fusion.123
  57.5 4.2 collective-permute-start.2
  61.7 69.8 %fusion.26 = (f32[16,256,1,1024]{3,1,0,2:T(8,128)}, f32[16,256,1,1024]{3,1,0,2:T(8,128)}) fusion(s32[16,256]{1,0:T(8,128)S(1)} %multiply_add_fusion), kind=kLoop, calls=%fused_computation.42 | loop fusion | flops 62914560 | bytes 33570816 | tf_op jit(solution)/shard_map/cos | solution.py:39
  131.6 2.4 fusion.78
  134.0 1.9 fusion.109
  135.9 4.5 add_add_fusion
  140.4 25.6 %bitcast_convert_fusion = bf16[16,16,2,1024]{3,1,2,0:T(8,128)(2,1)S(1)} fusion(f32[16,256,1,1024]{3,1,0,2:T(8,128)} %get-tuple-element.22, f32[16,256,1,1024]{3,1,0,2:T(8,128)} %get-tuple-element.21, f32[16,16,16,256,1]{3,1,0,2,4:T(8,128)} %bitcast.140), kind=kOutput, calls=%fused_computation.75 | convolution fusion | flops 12902203392 | bytes 38797312 | tf_op jit(solution)/shard_map/rsfb,sbcm->rfcm/dot_general | solution.py:120
  166.0 15.0 %copy.111 = bf16[16,16,2,1024]{1,2,0,3:T(2,128)(2,1)} copy(bf16[16,16,2,1024]{3,1,2,0:T(8,128)(2,1)S(1)} %bitcast_convert_fusion) | data formatting | bytes 2097152 | tf_op jit(solution)/shard_map/convert_element_type | solution.py:122
  181.0 24.0 %reshape.359 = bf16[128,2,2048]{2,1,0:T(2,128)(2,1)} reshape(bf16[1024,16,2,16]{3,2,1,0:T(2,128)(2,1)} %bitcast.134) | data formatting | bytes 2097152
  205.0 7.0 %all-to-all-start = ((bf16[128,2,2048]{2,1,0:T(2,128)(2,1)}), bf16[128,2,2048]{2,1,0:T(2,128)(2,1)S(1)}, u32[]{:S(2)}, u32[]{:S(2)}) async-start(bf16[128,2,2048]{2,1,0:T(2,128)(2,1)} %reshape.359), calls=%async_computation | async-start | bytes 2097152 | tf_op jit(solution)/shard_map/all_to_all | solution.py:123
  212.0 69.4 %cosine_multiply_fusion = (f32[1,16,256,1024]{3,2,0,1:T(8,128)}, f32[1,16,256,1024]{3,2,0,1:T(8,128)}) fusion(f32[1024]{0:T(1024)S(1)} %fusion.136), kind=kLoop, calls=%fused_computation.34 | loop fusion | flops 79691776 | bytes 33558528 | tf_op jit(solution)/shard_map/mul | solution.py:44
  281.4 0.1 iota_compare_fusion.8
  281.5 7.5 %reshape.360 = bf16[1024,16,2,16]{3,2,1,0:T(2,128)(2,1)} reshape(bf16[128,2,2048]{2,1,0:T(2,128)(2,1)S(1)} %all-to-all-done) | data formatting | bytes 2097152
  289.0 9.9 %copy.197 = bf16[16,16,2,1024]{1,3,2,0:T(8,128)(2,1)} copy(bf16[16,16,2,1024]{1,2,0,3:T(2,128)(2,1)} %bitcast.135) | data formatting | bytes 2097152 | tf_op jit(solution)/shard_map/all_to_all | solution.py:123
  298.8 20.8 %copy.113 = bf16[128,16,16,2,8]{1,0,4,3,2:T(8,128)(2,1)} copy(bf16[128,16,16,2,8]{2,4,0,3,1:T(8,128)(2,1)} %bitcast.136) | data formatting | bytes 2097152 | tf_op jit(solution)/shard_map/all_to_all | solution.py:123
  319.6 15.1 %all_to_all.29 = bf16[2048,16,2,8]{0,3,2,1:T(8,128)(2,1)S(1)} reshape(bf16[128,16,16,2,8]{1,0,4,3,2:T(8,128)(2,1)} %copy.113) | data formatting | bytes 2097152 | tf_op jit(solution)/shard_map/all_to_all | solution.py:123
  334.8 0.3 copy.150
  335.1 1.4 rev.8
  336.6 8.9 %fusion.82 = f32[8,32,1024]{2,1,0:T(8,128)S(1)} fusion(bf16[8,1024,1024]{2,1,0:T(8,128)(2,1)} %param.15, bf16[8,1024,32]{1,2,0:T(8,128)(2,1)S(1)} %rev.8, f32[1024]{0:T(1024)S(1)} %copy-done.8, bf16[8,1024,32]{1,0,2:T(8,128)(2,1)S(1)} %get-tuple-element.11), kind=kOutput, calls=%fused_computation.99 | convolution fusion | flops 538181632 | bytes 18878464 | tf_op jit(solution)/shard_map/ojl,ojc->olc/dot_general | solution.py:77
  345.5 9.0 %fusion.68 = bf16[8,32,1024]{2,1,0:T(8,128)(2,1)S(1)} fusion(f32[8,32,1024]{2,1,0:T(8,128)S(1)} %fusion.82, bf16[8,1024,1024]{2,1,0:T(8,128)(2,1)} %param.15, bf16[8,1024,32]{1,2,0:T(8,128)(2,1)S(1)} %rev.8, f32[1024]{0:T(1024)S(1)} %copy-done.9, f32[1024]{0:T(1024)S(1)} %copy-done.8, pred[8,1024]{1,0:T(8,128)(4,1)S(1)} %get-tuple-element.26, ...), kind=kOutput, calls=%fused_computation.84 | convolution fusion | flops 539230208 | bytes 19423232 | tf_op jit(solution)/shard_map/ojl,ojc->olc/dot_general | solution.py:78
  354.5 10.8 %fusion.84 = f32[8,32,1024]{2,1,0:T(8,128)S(1)} fusion(bf16[8,1024,1024]{2,1,0:T(8,128)(2,1)} %param.15, bf16[8,32,1024]{2,1,0:T(8,128)(2,1)S(1)} %fusion.68, pred[8,1024]{1,0:T(8,128)(4,1)S(1)} %get-tuple-element.26), kind=kOutput, calls=%fused_computation.100 | convolution fusion | flops 537133056 | bytes 18358272 | tf_op jit(solution)/shard_map/ojl,olc->ojc/dot_general | solution.py:89
  365.3 11.0 %fusion.86 = f32[8,32,1024]{2,1,0:T(8,128)S(1)} fusion(bf16[8,1024,1024]{2,1,0:T(8,128)(2,1)} %param.15, bf16[8,32,1024]{2,1,0:T(8,128)(2,1)S(1)} %fusion.68, pred[8,1024]{1,0:T(8,128)(4,1)S(1)} %get-tuple-element.26), kind=kOutput, calls=%fused_computation.102 | convolution fusion | flops 537133056 | bytes 18358272 | tf_op jit(solution)/shard_map/ojl,olc->ojc/dot_general | solution.py:88
  376.3 0.2 fusion.80
  376.4 0.2 subtract_bitcast_fusion
  376.7 0.2 concatenate.11
  376.9 4.8 copy.116
  381.7 1.0 rev.9
  382.8 0.2 concatenate.12
  383.0 4.8 copy.117
  387.8 9.4 %fusion.154 = bf16[2048,2,8,16]{3,2,1,0:T(8,128)(2,1)} fusion(bf16[8,1024,16,2]{2,0,3,1:T(8,128)(2,1)} %copy.117, bf16[8,1024,16,2]{2,0,3,1:T(8,128)(2,1)} %copy.116), kind=kLoop, calls=%fused_computation.194 | loop fusion | flops 524288 | bytes 2097152
  397.2 12.5 %reshape.361 = bf16[128,2,2048]{2,1,0:T(2,128)(2,1)} reshape(bf16[2048,2,8,16]{3,2,1,0:T(8,128)(2,1)} %fusion.154) | data formatting | bytes 2097152
  409.6 9.8 %all-to-all-start.1 = ((bf16[128,2,2048]{2,1,0:T(2,128)(2,1)}), bf16[128,2,2048]{2,1,0:T(2,128)(2,1)S(1)}, u32[]{:S(2)}, u32[]{:S(2)}) async-start(bf16[128,2,2048]{2,1,0:T(2,128)(2,1)} %reshape.361), calls=%async_computation.1 | async-start | bytes 2097152 | tf_op jit(solution)/shard_map/all_to_all | solution.py:127
  419.4 23.5 %add_multiply_fusion.9 = f32[64,256,256]{2,1,0:T(8,128)} fusion(f32[64,256]{1,0:T(8,128)S(1)} %fusion.99, f32[64,256]{1,0:T(8,128)S(1)} %get-tuple-element.30, s32[64,256]{1,0:T(8,128)S(1)} %get-tuple-element.34, f32[64,256]{1,0:T(8,128)S(1)} %get-tuple-element.31, s32[64,256]{1,0:T(8,128)S(1)} %copy-done.3, ...), kind=kLoop, calls=%fused_computation.28.clone.clone.1 | loop fusion | flops 50331648 | bytes 17367040 | tf_op jit(solution)/shard_map/bcp,bfp->bfc/dot_general | solution.py:143
  442.9 7.5 %reshape.362 = bf16[2048,2,8,16]{3,2,1,0:T(8,128)(2,1)} reshape(bf16[128,2,2048]{2,1,0:T(2,128)(2,1)S(1)} %all-to-all-done.1) | data formatting | bytes 2097152
  450.4 18.8 %fusion.7 = f32[16,256,16,16,1]{1,3,4,2,0:T(8,128)} fusion(f32[1,16,256,1024]{3,2,0,1:T(8,128)} %get-tuple-element.24, f32[1,16,256,1024]{3,2,0,1:T(8,128)} %get-tuple-element.23, bf16[16,16,2,128,8]{1,4,2,0,3:T(8,128)(2,1)} %bitcast.137), kind=kOutput, calls=%fused_computation.15 | convolution fusion | flops 4328521728 | bytes 38797312 | tf_op jit(solution)/shard_map/rfcm,csbm->rsfb/dot_general | solution.py:129
  469.2 19.6 %fusion.49 = f32[16,16,16,256]{3,2,0,1:T(8,128)} fusion(f32[16,256,16,16,1]{1,3,4,2,0:T(8,128)} %fusion.7, bf16[16,16,2,128,8]{1,4,2,0,3:T(8,128)(2,1)} %bitcast.138, f32[1,16,256,1024]{3,2,0,1:T(8,128)} %get-tuple-element.24, f32[1,16,256,1024]{3,2,0,1:T(8,128)} %get-tuple-element.23), kind=kOutput, calls=%fused_computation.66 | convolution fusion | flops 4337958912 | bytes 42991616 | tf_op jit(solution)/shard_map/rfcm,csbm->rsfb/dot_general | solution.py:132
  488.8 2.8 copy.122
  491.6 4.0 fusion.53
  495.7 7.6 %collective-permute-start.4 = (f32[32,16,256]{2,0,1:T(8,128)S(1)}, f32[32,16,256]{2,0,1:T(8,128)S(1)}, u32[]{:S(2)}, u32[]{:S(2)}) collective-permute-start(f32[32,16,256]{2,0,1:T(8,128)S(1)} %fusion.53), channel_id=1, source_target_pairs={{1,0},{2,1},{3,2},{4,3},{5,4},{6,5},{7,6},{8,7},{9,8},{10,9},{11,1... | collective-permute-start | bytes 1572872 | tf_op jit(solution)/shard_map/ppermute | solution.py:19
  503.2 4.0 fusion.51
  507.3 2.1 collective-permute-start.5
  509.4 4.2 fusion.55
  513.7 0.6 convolution_add_fusion.1
  514.3 12.2 %collective-permute-done.5 = f32[32,16,256]{2,0,1:T(8,128)S(1)} collective-permute-done((f32[32,16,256]{2,0,1:T(8,128)S(1)}, f32[32,16,256]{2,0,1:T(8,128)S(1)}, u32[]{:S(2)}, u32[]{:S(2)}) %collective-permute-start.5) | collective-permute-done | bytes 524320 | tf_op jit(solution)/shard_map/ppermute | solution.py:19
  526.5 0.7 convolution_add_fusion
  527.1 18.4 %fusion.22 = f32[64,16,256]{2,1,0:T(8,128)} fusion(f32[64,16,256]{2,0,1:T(8,128)S(1)} %convolution_add_fusion, f32[64,256,256]{2,1,0:T(8,128)} %add_multiply_fusion.9), kind=kOutput, calls=%fused_computation.36 | convolution fusion | flops 805306368 | bytes 18874368 | tf_op jit(solution)/shard_map/bcp,bfp->bfc/dot_general | solution.py:143
  (61 shorter events, 0.3 us)
Async XLA Ops:
  0.0 5.1 copy-start
  4.6 52.7 %copy-start.14 = (pred[64]{0:T(512)(128)(4,1)}, pred[64]{0:T(512)(128)(4,1)S(1)}, u32[]{:S(2)}) copy-start(pred[64]{0:T(512)(128)(4,1)S(1)} %get-tuple-element.7) | copy-start | bytes 196
  4.6 42.3 %copy-start.16 = (pred[64]{0:T(512)(128)(4,1)}, pred[64]{0:T(512)(128)(4,1)S(1)}, u32[]{:S(2)}) copy-start(pred[64]{0:T(512)(128)(4,1)S(1)} %get-tuple-element.29) | copy-start | bytes 196
  5.0 42.0 %copy-start.10 = (s32[64]{0:T(128)}, s32[64]{0:T(128)S(1)}, u32[]{:S(2)}) copy-start(s32[64]{0:T(128)S(1)} %add_reduce_fusion.1) | copy-start | bytes 772
  5.0 36.4 %copy-start.2 = (s32[64,256]{1,0:T(8,128)}, s32[64,256]{1,0:T(8,128)S(1)}, u32[]{:S(2)}) copy-start(s32[64,256]{1,0:T(8,128)S(1)} %get-tuple-element.35) | copy-start | bytes 196612
  5.1 36.3 %copy-start.4 = (s32[64,256]{1,0:T(8,128)}, s32[64,256]{1,0:T(8,128)S(1)}, u32[]{:S(2)}) copy-start(s32[64,256]{1,0:T(8,128)S(1)} %get-tuple-element.36) | copy-start | bytes 196612
  5.1 36.3 %copy-start.6 = (s32[64,256]{1,0:T(8,128)}, s32[64,256]{1,0:T(8,128)S(1)}, u32[]{:S(2)}) copy-start(s32[64,256]{1,0:T(8,128)S(1)} %get-tuple-element.37) | copy-start | bytes 196612
  5.1 41.4 %copy-start.20 = (s32[64]{0:T(128)S(1)}, s32[64]{0:T(128)}, u32[]{:S(2)}) copy-start(s32[64]{0:T(128)} %param.12) | copy-start | bytes 772
  42.5 91.5 %collective-permute-start.1 = (f32[32,16,256]{2,0,1:T(8,128)S(1)}, f32[32,16,256]{2,0,1:T(8,128)S(1)}, u32[]{:S(2)}, u32[]{:S(2)}) collective-permute-start(f32[32,16,256]{2,0,1:T(8,128)S(1)} %fusion.76), channel_id=1, source_target_pairs={{0,1},{1,2},{2,3},{3,4},{4,5},{5,6},{6,7},{7,8},{8,9},{9,10},{10,1... | collective-permute-start | bytes 1572872 | tf_op jit(solution)/shard_map/ppermute | solution.py:19
  46.5 85.1 %copy-start.18 = (s32[64]{0:T(128)}, s32[64]{0:T(128)S(1)}, u32[]{:S(2)}) copy-start(s32[64]{0:T(128)S(1)} %get-tuple-element.9) | copy-start | bytes 772
  46.9 10.6 %copy-start.12 = (s32[64]{0:T(128)}, s32[64]{0:T(128)S(1)}, u32[]{:S(2)}) copy-start(s32[64]{0:T(128)S(1)} %add_reduce_fusion) | copy-start | bytes 772
  47.1 86.9 %collective-permute-start = (s32[32]{0:T(128)S(1)}, s32[32]{0:T(128)S(1)}, u32[]{:S(2)}, u32[]{:S(2)}) collective-permute-start(s32[32]{0:T(128)S(1)} %broadcast_select_fusion.1), channel_id=1, source_target_pairs={{0,1},{1,2},{2,3},{3,4},{4,5},{5,6},{6,7},{7,8},{8,9},{9,10},{10,1... | collective-permute-start | bytes 392 | tf_op jit(solution)/shard_map/ppermute | solution.py:19
  51.3 84.6 %collective-permute-start.3 = (f32[32,16,256]{2,0,1:T(8,128)S(1)}, f32[32,16,256]{2,0,1:T(8,128)S(1)}, u32[]{:S(2)}, u32[]{:S(2)}) collective-permute-start(f32[32,16,256]{2,0,1:T(8,128)S(1)} %fusion.74), channel_id=1, source_target_pairs={{1,0},{2,1},{3,2},{4,3},{5,4},{6,5},{7,6},{8,7},{9,8},{10,9},{11,1... | collective-permute-start | bytes 1572872 | tf_op jit(solution)/shard_map/ppermute | solution.py:19
  57.5 78.4 %collective-permute-start.2 = (s32[32]{0:T(128)S(1)}, s32[32]{0:T(128)S(1)}, u32[]{:S(2)}, u32[]{:S(2)}) collective-permute-start(s32[32]{0:T(128)S(1)} %broadcast_select_fusion), channel_id=1, source_target_pairs={{1,0},{2,1},{3,2},{4,3},{5,4},{6,5},{7,6},{8,7},{9,8},{10,9},{11,1... | collective-permute-start | bytes 392 | tf_op jit(solution)/shard_map/ppermute | solution.py:19
  205.0 76.5 %all-to-all-start = ((bf16[128,2,2048]{2,1,0:T(2,128)(2,1)}), bf16[128,2,2048]{2,1,0:T(2,128)(2,1)S(1)}, u32[]{:S(2)}, u32[]{:S(2)}) async-start(bf16[128,2,2048]{2,1,0:T(2,128)(2,1)} %reshape.359), calls=%async_computation | async-start | bytes 2097152 | tf_op jit(solution)/shard_map/all_to_all | solution.py:123
  298.8 37.7 %copy-start.8 = (f32[1024]{0:T(1024)S(1)}, f32[1024]{0:T(1024)}, u32[]{:S(2)}) copy-start(f32[1024]{0:T(1024)} %param.13) | copy-start | bytes 12292
  319.6 25.9 %copy-start.9 = (f32[1024]{0:T(1024)S(1)}, f32[1024]{0:T(1024)}, u32[]{:S(2)}) copy-start(f32[1024]{0:T(1024)} %param.14) | copy-start | bytes 12292
  382.7 36.7 %copy-start.3 = (s32[64,256]{1,0:T(8,128)S(1)}, s32[64,256]{1,0:T(8,128)}, u32[]{:S(2)}) copy-start(s32[64,256]{1,0:T(8,128)} %copy-done.2) | copy-start | bytes 196612
  382.7 36.7 %copy-start.5 = (s32[64,256]{1,0:T(8,128)S(1)}, s32[64,256]{1,0:T(8,128)}, u32[]{:S(2)}) copy-start(s32[64,256]{1,0:T(8,128)} %copy-done.4) | copy-start | bytes 196612
  382.7 36.7 %copy-start.7 = (s32[64,256]{1,0:T(8,128)S(1)}, s32[64,256]{1,0:T(8,128)}, u32[]{:S(2)}) copy-start(s32[64,256]{1,0:T(8,128)} %copy-done.6) | copy-start | bytes 196612
  409.6 33.3 %all-to-all-start.1 = ((bf16[128,2,2048]{2,1,0:T(2,128)(2,1)}), bf16[128,2,2048]{2,1,0:T(2,128)(2,1)S(1)}, u32[]{:S(2)}, u32[]{:S(2)}) async-start(bf16[128,2,2048]{2,1,0:T(2,128)(2,1)} %reshape.361), calls=%async_computation.1 | async-start | bytes 2097152 | tf_op jit(solution)/shard_map/all_to_all | solution.py:127
  488.8 20.6 %copy-start.19 = (s32[64]{0:T(128)S(1)}, s32[64]{0:T(128)}, u32[]{:S(2)}) copy-start(s32[64]{0:T(128)} %copy-done.18) | copy-start | bytes 772
  488.8 24.9 %copy-start.11 = (s32[64]{0:T(128)S(1)}, s32[64]{0:T(128)}, u32[]{:S(2)}) copy-start(s32[64]{0:T(128)} %copy-done.10) | copy-start | bytes 772
  488.8 24.9 %copy-start.17 = (pred[64]{0:T(512)(128)(4,1)S(1)}, pred[64]{0:T(512)(128)(4,1)}, u32[]{:S(2)}) copy-start(pred[64]{0:T(512)(128)(4,1)} %copy-done.16) | copy-start | bytes 196
  488.8 37.7 %copy-start.13 = (s32[64]{0:T(128)S(1)}, s32[64]{0:T(128)}, u32[]{:S(2)}) copy-start(s32[64]{0:T(128)} %copy-done.12) | copy-start | bytes 772
  488.8 37.7 %copy-start.15 = (pred[64]{0:T(512)(128)(4,1)S(1)}, pred[64]{0:T(512)(128)(4,1)}, u32[]{:S(2)}) copy-start(pred[64]{0:T(512)(128)(4,1)} %copy-done.14) | copy-start | bytes 196
  491.6 53.9 %copy-start.1 = (f32[64,16,256]{2,1,0:T(8,128)S(1)}, f32[64,16,256]{2,1,0:T(8,128)}, u32[]{:S(2)}) copy-start(f32[64,16,256]{2,1,0:T(8,128)} %param.8) | copy-start | bytes 3145732
  495.7 18.0 %collective-permute-start.4 = (f32[32,16,256]{2,0,1:T(8,128)S(1)}, f32[32,16,256]{2,0,1:T(8,128)S(1)}, u32[]{:S(2)}, u32[]{:S(2)}) collective-permute-start(f32[32,16,256]{2,0,1:T(8,128)S(1)} %fusion.53), channel_id=1, source_target_pairs={{1,0},{2,1},{3,2},{4,3},{5,4},{6,5},{7,6},{8,7},{9,8},{10,9},{11,1... | collective-permute-start | bytes 1572872 | tf_op jit(solution)/shard_map/ppermute | solution.py:19
  507.3 19.2 %collective-permute-start.5 = (f32[32,16,256]{2,0,1:T(8,128)S(1)}, f32[32,16,256]{2,0,1:T(8,128)S(1)}, u32[]{:S(2)}, u32[]{:S(2)}) collective-permute-start(f32[32,16,256]{2,0,1:T(8,128)S(1)} %fusion.51), channel_id=1, source_target_pairs={{0,1},{1,2},{2,3},{3,4},{4,5},{5,6},{6,7},{7,8},{8,9},{9,10},{10,1... | collective-permute-start | bytes 1572872 | tf_op jit(solution)/shard_map/ppermute | solution.py:19
where the time goes:
time: 550 us; the launch traced here: 546 us
  matrix products  183 us (33%)
  other arithmetic  175 us (32%)
  local copies, waits for them, and re-layouts  131 us (24%)
  starting transfers between devices  43.8 us (8%)
  waiting for transfers between devices  12.2 us (2%)
    cos x1, other arithmetic, fourier_tables(): cosine = jnp.cos(angles)  69.8 us
    mul x1, other arithmetic, fourier_tables(): inverse = jnp.stack([cosine * factor, -sine_part * factor], axis=0)  69.4 us
    unnamed x47, local copies, waits for them, and re-layouts  51.8 us
    all_to_all x3, local copies, waits for them, and re-layouts, on_device(): lax.all_to_all(fourier, ('dom', 'order'), split_axis=3, concat_axis=0, ti...  45.8 us
    dot_general x1, matrix products, on_device(): spread = jnp.einsum('bfc,bcp->bfp', ssh, matrix, precision=highest)  36.3 us
    ppermute x6, starting transfers between devices, from_behind(): lax.ppermute(value, axis, [(source, source + steps) for source in range(l...  27 us
    dot_general x1, matrix products, on_device(): jnp.einsum('rsfb,sbcm->rfcm', grid_vals, forward, precision=lax.Precision...  25.6 us
    dot_general x1, other arithmetic, on_device(): return jnp.einsum('bcp,bfp->bfc', matrix, block_vals, precision=highest)  23.5 us
  transfers between devices with their start and end apart: 8, of which 1 were waited for; matrix products, arithmetic and copies ran while one was open for 33% of the time, Pallas kernels for 0%

commit v1 on v0

v1 whole, which is shorter than its diff:
```python
import functools
import math

import jax
import jax.numpy as jnp
import numpy as np
from jax import lax
from jax.experimental import pallas as pl
from jax.experimental.pallas import tpu as pltpu
from jax.sharding import PartitionSpec as P

AXES = ("dom", "order")
DEVS = 128
NF = 16
BLOCK = 256
BLK = 64
HALF_BLK = 32
TILES = 256
LAT = 16
ORD = 8
NLAT = 1024
NDEG = 1024
RADIX = 16
NQ = 64
STEP = 8
F32 = jnp.float32
BF16 = jnp.bfloat16
MIB = 1 << 20

SMEM = pltpu.SMEM
VMEM = pltpu.VMEM


def hi_lo(table):
    table = np.asarray(table, np.float32)
    hi = table.astype(jnp.bfloat16)
    lo = (table - hi.astype(np.float32)).astype(jnp.bfloat16)
    return hi, lo


def make_tables():
    tiles = np.arange(RADIX)
    comps = []
    for u in range(9):
        comps.append(np.cos(2 * np.pi * ((u * tiles) % RADIX) / RADIX))
    for u in range(1, 8):
        comps.append(-np.sin(2 * np.pi * ((u * tiles) % RADIX) / RADIX))
    first = np.kron(np.stack(comps), np.eye(NF))
    f_hi, f_lo = hi_lo(first / 4096.0)
    i_hi, i_lo = hi_lo(2.0 * first.T)
    points = np.arange(BLOCK)
    angle = 2 * np.pi * ((np.arange(NQ)[:, None] * points[None, :]) % BLOCK) / BLOCK
    cos, sin = np.cos(angle), np.sin(angle)
    second = np.concatenate(
        [np.concatenate([cos, sin], axis=1), np.concatenate([-sin, cos], axis=1)], axis=0
    )
    s_hi, s_lo = hi_lo(second)
    twist = 2 * np.pi * (tiles[:, None] * points[None, :]) / 4096.0
    return dict(
        first=np.concatenate([f_hi, f_lo], axis=0),
        last=np.concatenate([i_hi, i_lo], axis=1),
        second=np.concatenate([s_hi, s_lo], axis=0),
        twc=np.cos(twist).astype(np.float32),
        tws=np.sin(twist).astype(np.float32),
    )


def vmem_spec():
    return pl.BlockSpec(memory_space=VMEM)


def smem_spec():
    return pl.BlockSpec(memory_space=SMEM)


def params(mib):
    return pltpu.CompilerParams(vmem_limit_bytes=mib * MIB)


def lists_kernel(me_ref, tile_ref, own_b, own_t, oth_b, oth_t):
    me = me_ref[0]

    def step(b, counts):
        own_n, oth_n = counts
        tile = tile_ref[b]
        own = (lax.shift_right_logical(tile, 8) == me).astype(jnp.int32)
        own_b[own_n] = b
        own_t[own_n] = tile
        oth_b[oth_n] = b
        oth_t[oth_n] = tile
        return own_n + own, oth_n + 1 - own

    lax.fori_loop(0, BLK, step, (jnp.int32(0), jnp.int32(0)))


def make_lists(me, block_tile):
    shape = jax.ShapeDtypeStruct((HALF_BLK + 1,), jnp.int32)
    return pl.pallas_call(
        lists_kernel,
        out_shape=(shape,) * 4,
        in_specs=[smem_spec()] * 2,
        out_specs=(smem_spec(),) * 4,
    )(me, block_tile)


def spread_kernel(pick, count, ssh, index, weight, wt_out, out):
    base = pl.program_id(0) * STEP
    lanes = lax.broadcasted_iota(jnp.int32, (4, BLOCK), 1)
    points = lax.broadcasted_iota(jnp.int32, (BLOCK, BLOCK), 0)

    def step(i, carry):
        b = pick[base + i]
        idx = index[b]
        wgt = jnp.where(lanes < count[b], weight[b], 0.0)
        mat = jnp.where(points == idx[0:1], wgt[0:1], 0.0)
        for k in range(1, 4):
            mat = mat + jnp.where(points == idx[k : k + 1], wgt[k : k + 1], 0.0)
        mat = mat.astype(BF16)
        wt_out[i] = mat
        heights = ssh[b]
        hi = heights.astype(BF16)
        lo = (heights - hi.astype(F32)).astype(BF16)
        both = lax.dot_general(
            jnp.concatenate([hi, lo], axis=0),
            mat,
            (((1,), (1,)), ((), ())),
            preferred_element_type=F32,
        )
        out[i] = (both[:NF] + both[NF:]).astype(out.dtype)
        return carry

    lax.fori_loop(0, STEP, step, 0, unroll=2)


def spread_half(pick, count, ssh, index, weight, dtype):
    return pl.pallas_call(
        spread_kernel,
        grid=(HALF_BLK // STEP,),
        out_shape=(
            jax.ShapeDtypeStruct((HALF_BLK, BLOCK, BLOCK), BF16),
            jax.ShapeDtypeStruct((HALF_BLK, NF, BLOCK), dtype),
        ),
        in_specs=[smem_spec(), smem_spec(), vmem_spec(), vmem_spec(), vmem_spec()],
        out_specs=(
            pl.BlockSpec((STEP, BLOCK, BLOCK), lambda i: (i, 0, 0)),
            pl.BlockSpec((STEP, NF, BLOCK), lambda i: (i, 0, 0)),
        ),
        compiler_params=params(24),
        cost_estimate=pl.CostEstimate(
            flops=2 * HALF_BLK * NF * BLOCK * BLOCK * 8, bytes_accessed=6 * MIB, transcendentals=0
        ),
    )(pick, count, ssh, index, weight)


def comp_re(u):
    return min(u, RADIX - u)


def comp_im(u):
    return 8 + min(u, RADIX - u)


def forward_kernel(
    me_ref, own_t, low_t, upp_t, own, low, upp, first, second, twc, tws, out, grid, mid, wide
):
    me = me_ref[0]
    flip = jnp.where(me >= DEVS // 2, 0xF0, 0)
    grid[...] = jnp.zeros_like(grid)

    def add_own(i, carry):
        tile = (own_t[i] & 255) ^ flip
        grid[tile] = grid[tile] + own[i]
        return carry

    lax.fori_loop(0, HALF_BLK, add_own, 0, unroll=2)

    def add_other(tiles, values):
        def body(i, carry):
            tile = tiles[i]
            mine = lax.shift_right_logical(tile, 8) == me
            spot = jnp.where(mine, (tile & 255) ^ flip, TILES)
            grid[spot] = grid[spot] + values[i].astype(F32)
            return carry

        lax.fori_loop(0, HALF_BLK, body, 0, unroll=2)

    add_other(low_t, low)
    add_other(upp_t, upp)

    def circle(r, carry):
        rows = grid[pl.ds(r * RADIX, RADIX)].reshape(RADIX * NF, BLOCK)
        hi = rows.astype(BF16)
        lo = (rows - hi.astype(F32)).astype(BF16)
        part = jnp.dot(first[...], hi, preferred_element_type=F32)
        comps = part[:256] + part[256:]
        comps = comps + jnp.dot(first[0:256], lo, preferred_element_type=F32)
        for u in range(RADIX):
            a = comps[comp_re(u) * NF : comp_re(u) * NF + NF]
            cu = twc[u : u + 1]
            su = tws[u : u + 1]
            if u == 0:
                re, im = a, jnp.zeros_like(a)
            elif u == 8:
                re, im = a * cu, -(a * su)
            else:
                b = comps[comp_im(u) * NF : comp_im(u) * NF + NF]
                if u < 8:
                    re, im = a * cu + b * su, b * cu - a * su
                else:
                    re, im = a * cu - b * su, -(b * cu + a * su)
            mid[u * NF : u * NF + NF, 0:BLOCK] = re.astype(BF16)
            mid[u * NF : u * NF + NF, BLOCK : 2 * BLOCK] = im.astype(BF16)
        res = lax.dot_general(
            second[...], mid[...], (((1,), (1,)), ((), ())), preferred_element_type=F32
        )
        res = res[:128] + res[128:]
        for c in range(2):
            for uh in range(2):
                wide[pl.ds(uh * 32 + c * 16 + r, NQ, stride=64), :] = res[
                    c * NQ : c * NQ + NQ, uh * 128 : uh * 128 + 128
                ]
        return carry

    lax.fori_loop(0, LAT, circle, 0)
    out[...] = wide[...].astype(BF16).reshape(out.shape)


def forward(me, own_t, low_t, upp_t, own, low, upp, tables):
    return pl.pallas_call(
        forward_kernel,
        out_shape=jax.ShapeDtypeStruct((DEVS, 32, 128), BF16),
        in_specs=[smem_spec()] * 4 + [vmem_spec()] * 7,
        out_specs=vmem_spec(),
        scratch_shapes=[
            VMEM((TILES + 1, NF, BLOCK), F32),
            VMEM((RADIX * NF, 2 * BLOCK), BF16),
            VMEM((DEVS * 32, 128), F32),
        ],
        compiler_params=params(32),
    )(
        me,
        own_t,
        low_t,
        upp_t,
        own,
        low,
        upp,
        tables["first"],
        tables["second"],
        tables["twc"],
        tables["tws"],
    )


def legendre_kernel(me_ref, table, data, gauss, love, out, ins, outs):
    k = pl.program_id(0)

    @pl.when(k == 0)
    def _():
        gw = gauss[...]
        for c in range(2):
            north = jnp.concatenate([data[i, c * 16 : c * 16 + 16] for i in range(64)], axis=0)
            south = jnp.concatenate(
                [data[127 - i, c * 16 : c * 16 + 16] for i in range(64)], axis=0
            )
            north = north.astype(F32).T
            south = south.astype(F32).T
            even = ((north + south) * gw).astype(BF16)
            odd = ((north - south) * gw).astype(BF16)
            ins[:, c * 16 : c * 16 + 16, :] = even.reshape(ORD, NF, NLAT)
            ins[:, 32 + c * 16 : 32 + c * 16 + 16, :] = odd.reshape(ORD, NF, NLAT)

    tab = table[0]
    both = jnp.dot(ins[k], tab, preferred_element_type=F32)
    order = me_ref[0] * ORD + k
    degree = lax.broadcasted_iota(jnp.int32, (32, NDEG), 1)
    is_even = ((degree + order) & 1) == 0
    coef = jnp.where(is_even, both[:32], both[32:])
    coef = jnp.where(degree < order, 0.0, coef)
    coef = coef * love[...]
    parts = jnp.concatenate(
        [jnp.where(is_even, coef, 0.0), jnp.where(is_even, 0.0, coef)], axis=0
    ).astype(BF16)
    res = lax.dot_general(parts, tab, (((1,), (1,)), ((), ())), preferred_element_type=F32)
    upper = res[:32] + res[32:]
    lower = res[:32] - res[32:]
    spot = pl.ds(pl.multiple_of(k * NF, NF), NF)
    for c in range(2):
        outs[c, 0, spot, :] = upper[c * 16 : c * 16 + 16]
        outs[c, 1, spot, :] = lower[c * 16 : c * 16 + 16]

    @pl.when(k == ORD - 1)
    def _():
        for c in range(2):
            up = outs[c, 0].T.astype(BF16)
            dn = outs[c, 1].T.astype(BF16)
            for i in range(64):
                out[i, c * 16 : c * 16 + 16] = up[i * 16 : i * 16 + 16]
                out[127 - i, c * 16 : c * 16 + 16] = dn[i * 16 : i * 16 + 16]


def legendre_both(me, table, data, gauss, love):
    return pl.pallas_call(
        legendre_kernel,
        grid=(ORD,),
        out_shape=jax.ShapeDtypeStruct((DEVS, 32, 128), BF16),
        in_specs=[
            smem_spec(),
            pl.BlockSpec((1, NLAT, NDEG), lambda k: (k, 0, 0)),
            vmem_spec(),
            vmem_spec(),
            vmem_spec(),
        ],
        out_specs=pl.BlockSpec((DEVS, 32, 128), lambda k: (0, 0, 0)),
        scratch_shapes=[VMEM((ORD, 64, NLAT), BF16), VMEM((2, 2, 128, NLAT), F32)],
        compiler_params=params(40),
    )(me, table, data, gauss.reshape(1, NLAT), love.reshape(1, NDEG))


def inverse_kernel(
    me_ref, own_t, low_t, upp_t, data, second, last, twc, tws, own, low, upp, wide, tiles, mid
):
    me = me_ref[0]
    flip = jnp.where(me >= DEVS // 2, 0xF0, 0)
    wide[...] = data[...].astype(F32).reshape(wide.shape)
    row = lax.broadcasted_iota(jnp.int32, (NQ, 128), 0)
    lane = lax.broadcasted_iota(jnp.int32, (NQ, 128), 1)
    zonal = jnp.where((row == 0) & (lane < NF), 0.5, 1.0)

    def circle(r, carry):
        parts = []
        for c in range(2):
            left = wide[pl.ds(c * 16 + r, NQ, stride=64), :] * zonal
            right = wide[pl.ds(32 + c * 16 + r, NQ, stride=64), :]
            parts.append(jnp.concatenate([left, right], axis=1))
        spectrum = jnp.concatenate(parts, axis=0).T.astype(BF16)
        spectrum = jnp.concatenate([spectrum, spectrum], axis=1)
        waves = jnp.dot(spectrum, second[...], preferred_element_type=F32)
        res, ims = {}, {}
        for u in range(RADIX):
            a = waves[u * NF : u * NF + NF, 0:BLOCK]
            b = waves[u * NF : u * NF + NF, BLOCK : 2 * BLOCK]
            cu = twc[u : u + 1]
            su = tws[u : u + 1]
            res[u] = a * cu - b * su if u else a
            if u not in (0, 8):
                ims[u] = a * su + b * cu
        for u in range(9):
            val = res[u] if u in (0, 8) else res[u] + res[RADIX - u]
            mid[u * NF : u * NF + NF] = val.astype(BF16)
        for u in range(1, 8):
            val = ims[u] - ims[RADIX - u]
            mid[(8 + u) * NF : (8 + u) * NF + NF] = val.astype(BF16)
        comps = mid[...]
        load = jnp.dot(last[:, 0:256], comps, preferred_element_type=F32)
        load = load + jnp.dot(last[:, 256:512], comps, preferred_element_type=F32)
        tiles[pl.ds(r * RADIX, RADIX)] = load.reshape(RADIX, NF, BLOCK)
        return carry

    lax.fori_loop(0, LAT, circle, 0)

    def gather(i, carry):
        own[i] = tiles[(own_t[i] & 255) ^ flip]
        low[i] = tiles[(low_t[i] & 255) ^ flip].astype(BF16)
        upp[i] = tiles[(upp_t[i] & 255) ^ flip].astype(BF16)
        return carry

    lax.fori_loop(0, HALF_BLK, gather, 0, unroll=2)


def inverse(me, own_t, low_t, upp_t, data, tables):
    return pl.pallas_call(
        inverse_kernel,
        out_shape=(
            jax.ShapeDtypeStruct((HALF_BLK, NF, BLOCK), F32),
            jax.ShapeDtypeStruct((HALF_BLK, NF, BLOCK), BF16),
            jax.ShapeDtypeStruct((HALF_BLK, NF, BLOCK), BF16),
        ),
        in_specs=[smem_spec()] * 4 + [vmem_spec()] * 5,
        out_specs=(vmem_spec(),) * 3,
        scratch_shapes=[
            VMEM((DEVS * 32, 128), F32),
            VMEM((TILES, NF, BLOCK), F32),
            VMEM((RADIX * NF, BLOCK), BF16),
        ],
        compiler_params=params(32),
    )(
        me,
        own_t,
        low_t,
        upp_t,
        data,
        tables["second"],
        tables["last"],
        tables["twc"],
        tables["tws"],
    )


def own_kernel(values, wt, out):
    for i in range(STEP):
        val = values[i]
        hi = val.astype(BF16)
        lo = (val - hi.astype(F32)).astype(BF16)
        both = jnp.dot(jnp.concatenate([hi, lo], axis=0), wt[i], preferred_element_type=F32)
        out[i] = both[:NF] + both[NF:]


def own_cells(values, wt):
    return pl.pallas_call(
        own_kernel,
        grid=(HALF_BLK // STEP,),
        out_shape=jax.ShapeDtypeStruct((HALF_BLK, NF, BLOCK), F32),
        in_specs=[
            pl.BlockSpec((STEP, NF, BLOCK), lambda i: (i, 0, 0)),
            pl.BlockSpec((STEP, BLOCK, BLOCK), lambda i: (i, 0, 0)),
        ],
        out_specs=pl.BlockSpec((STEP, NF, BLOCK), lambda i: (i, 0, 0)),
        compiler_params=params(16),
        cost_estimate=pl.CostEstimate(
            flops=2 * HALF_BLK * NF * BLOCK * BLOCK * 4, bytes_accessed=5 * MIB, transcendentals=0
        ),
    )(values, wt)


def cells_kernel(me_ref, own_b, oth_b, oth_t, own, low, upp, wt, out):
    me = me_ref[0]
    step_id = pl.program_id(0)

    @pl.when(step_id == 0)
    def _():
        def copy(i, carry):
            out[own_b[i]] = own[i]
            return carry

        lax.fori_loop(0, HALF_BLK, copy, 0, unroll=2)

    for i in range(STEP):
        slot = step_id * STEP + i
        above = lax.shift_right_logical(oth_t[slot], 8) > me
        val = jnp.where(above, upp[slot], low[slot])
        out[oth_b[slot]] = jnp.dot(val, wt[i], preferred_element_type=F32)


def all_cells(me, own_b, oth_b, oth_t, own, low, upp, wt):
    return pl.pallas_call(
        cells_kernel,
        grid=(HALF_BLK // STEP,),
        out_shape=jax.ShapeDtypeStruct((BLK, NF, BLOCK), F32),
        in_specs=[smem_spec()] * 4
        + [vmem_spec()] * 3
        + [pl.BlockSpec((STEP, BLOCK, BLOCK), lambda i: (i, 0, 0))],
        out_specs=pl.BlockSpec((BLK, NF, BLOCK), lambda i: (0, 0, 0)),
        compiler_params=params(16),
    )(me, own_b, oth_b, oth_t, own, low, upp, wt)


def shift(value, steps):
    pairs = [(source, (source + steps) % DEVS) for source in range(DEVS)]
    return lax.ppermute(value, AXES, pairs)


def on_device(
    tables, ssh, cell_count, remap_index, remap_weight, block_tile, gauss_weight, love, legendre
):
    rank = lax.axis_index(AXES).astype(jnp.int32)
    me = rank.reshape(1)
    own_b, own_t, oth_b, oth_t = make_lists(me, block_tile)
    low_t = shift(oth_t, 1)
    upp_t = shift(oth_t, -1)
    wt_oth, oth = spread_half(oth_b, cell_count, ssh, remap_index, remap_weight, BF16)
    low = shift(oth, 1)
    upp = shift(oth, -1)
    wt_own, own = spread_half(own_b, cell_count, ssh, remap_index, remap_weight, F32)
    fourier = forward(me, own_t, low_t, upp_t, own, low, upp, tables)
    by_order = lax.all_to_all(fourier, AXES, split_axis=0, concat_axis=0, tiled=True)
    synth = legendre_both(me, legendre, by_order, gauss_weight, love)
    by_lat = lax.all_to_all(synth, AXES, split_axis=0, concat_axis=0, tiled=True)
    own_v, low_v, upp_v = inverse(me, own_t, low_t, upp_t, by_lat, tables)
    from_low = shift(upp_v, 1)
    from_upp = shift(low_v, -1)
    own_cell = own_cells(own_v, wt_own)
    return all_cells(me, own_b, oth_b, oth_t, own_cell, from_low, from_upp, wt_oth)


def solution(mesh):
    tables = {name: jnp.asarray(table) for name, table in make_tables().items()}
    return jax.shard_map(
        functools.partial(on_device, tables),
        mesh=mesh,
        in_specs=(
            P(AXES, None, None),
            P(AXES),
            P(AXES, None, None),
            P(AXES, None, None),
            P(AXES),
            P(),
            P(),
            P(AXES, None, None),
        ),
        out_specs=P(AXES, None, None),
        check_vma=False,
    )
```

time: 550 us -> 145 us (0.26)
  matrix products: 183 us -> 0 us
  other arithmetic: 175 us -> 0 us
  local copies, waits for them, and re-layouts: 131 us -> 9.08 us
  Pallas kernels: 0 us -> 56.7 us
  blocking collectives: 0 us -> 54.6 us
  starting transfers between devices: 43.8 us -> 17.6 us
  waiting for transfers between devices: 12.2 us -> 6.01 us
    dot_general x19 -> x0, matrix products: 183 us -> none  [the longest x1 36.3 us: on_device(): spread = jnp.einsum('bfc,bcp->bfp', ssh, matrix, precision=highest)]
    cos x1 -> x0, other arithmetic: 69.8 us -> none  [fourier_tables(): cosine = jnp.cos(angles)]
    mul x1 -> x0, other arithmetic: 69.4 us -> none  [fourier_tables(): inverse = jnp.stack([cosine * factor, -sine_part * factor], axis=0)]
    pallas_call x0 -> x8, Pallas kernels: none -> 56.7 us  [the longest x1 13.6 us: forward(): pl.pallas_call(forward_kernel, out_shape=jax.ShapeDtypeStruct((DEVS, 32,...]
    all_to_all x0 -> x2, blocking collectives: none -> 54.6 us  [the longest x1 31.6 us: on_device(): lax.all_to_all(fourier, AXES, split_axis=0, concat_axis=0, tiled=True)]
    all_to_all x3 -> x0, local copies, waits for them, and re-layouts: 45.8 us -> none  [on_device(): lax.all_to_all(fourier, ('dom', 'order'), split_axis=3, concat_axis=0, ti...]
    unnamed x47 -> x42, local copies, waits for them, and re-layouts: 51.8 us -> 9.08 us
    dot_general x1 -> x0, other arithmetic: 23.5 us -> none  [on_device(): return jnp.einsum('bcp,bfp->bfc', matrix, block_vals, precision=highest)]
  transfers between devices with their start and end apart: 8 -> 6, of which waited for: 1 -> 1; matrix products, arithmetic and copies ran while one was open for 33% -> 0% of each run, Pallas kernels for 0% -> 5%
where the time goes in v1:
time: 145 us; the launch traced here: 144 us
  Pallas kernels  56.7 us (39%)
  blocking collectives  54.6 us (38%)
  starting transfers between devices  17.6 us (12%)
  local copies, waits for them, and re-layouts  9.08 us (6%)
  waiting for transfers between devices  6.01 us (4%)
    all_to_all x1, blocking collectives, on_device(): lax.all_to_all(fourier, AXES, split_axis=0, concat_axis=0, tiled=True)  31.6 us
    all_to_all x1, blocking collectives, on_device(): lax.all_to_all(synth, AXES, split_axis=0, concat_axis=0, tiled=True)  23 us
    ppermute x6, starting transfers between devices, shift(): return lax.ppermute(value, AXES, pairs)  17.6 us
    pallas_call x1, Pallas kernels, forward(): pl.pallas_call(forward_kernel, out_shape=jax.ShapeDtypeStruct((DEVS, 32,...  13.6 us
    pallas_call x1, Pallas kernels, legendre_both(): pl.pallas_call(legendre_kernel, grid=(ORD,), out_shape=jax.ShapeDtypeStru...  13.2 us
    pallas_call x2, Pallas kernels, spread_half(): pl.pallas_call(spread_kernel, grid=(HALF_BLK // STEP,), out_shape=(jax.Sh...  13.1 us
    pallas_call x1, Pallas kernels, inverse(): pl.pallas_call(inverse_kernel, out_shape=(jax.ShapeDtypeStruct((HALF_BLK,...  11.3 us
    unnamed x42, local copies, waits for them, and re-layouts  9.08 us
  transfers between devices with their start and end apart: 6, of which 1 were waited for; matrix products, arithmetic and copies ran while one was open for 0% of the time, Pallas kernels for 5%

profile of v1, /device:TPU:1, one launch (start us, length us, event | category | flops | bytes accessed | tf_op | source)
XLA Modules:
  0.0 144.2 jit_solution(3210885136695414086)
XLA Ops:
  0.0 1.7 %shard_map.127 = (s32[33]{0:T(128)}, s32[33]{0:T(128)}, s32[33]{0:T(128)}, s32[33]{0:T(128)}) custom-call(s32[1]{0:T(128)} %bitcast.me_ref, s32[64]{0:T(128)} %tile_ref.1), custom_call_target="tpu_custom_call" | custom-call | tf_op jit(solution)/shard_map/pallas_call | solution.py:98
  1.7 0.0 copy-start.14
  1.7 0.6 copy-done.14
  2.3 0.0 copy-start.17
  2.3 1.2 copy-done.17
  3.5 0.0 copy-start.18
  3.5 0.9 copy-done.18
  4.5 0.0 copy-start.19
  4.5 0.9 copy-done.19
  5.4 0.0 copy-start.20
  5.4 0.7 copy-done.20
  6.1 0.0 copy-start.8
  6.1 0.0 copy-start.9
  6.1 6.5 %shard_map.129 = (bf16[32,256,256]{2,1,0:T(8,128)(2,1)S(1)}, bf16[32,16,256]{2,1,0:T(8,128)(2,1)S(1)}) custom-call(s32[33]{0:T(128)S(1)} %copy-done.14, s32[64]{0:T(128)S(1)} %copy-done.20, f32[64,16,256]{2,1,0:T(8,128)S(1)} %copy-done.17, s32[64,4,256]{2,1,0:T(4,128)S(1)} %copy-done.18, f32[64,4,256]{2,1,0:T(4,128)S(1)} %copy-done.19), custom_call_target="tpu_custom_call" | custom-call | flops 536870912 | bytes 6291456 | tf_op jit(solution)/shard_map/pallas_call | solution.py:136
  12.7 7.4 %collective-permute-start.3 = (bf16[32,16,256]{2,1,0:T(8,128)(2,1)S(1)}, bf16[32,16,256]{2,1,0:T(8,128)(2,1)S(1)}, u32[]{:S(2)}, u32[]{:S(2)}) collective-permute-start(bf16[32,16,256]{2,1,0:T(8,128)(2,1)S(1)} %get-tuple-element.21), channel_id=1, source_target_pairs={{0,127},{1,0},{2,1},{3,2},{4,3},{5,4},{6,5},{7,6},{8,7},{9,8},{10,... | collective-permute-start | bytes 786440 | tf_op jit(solution)/shard_map/ppermute | solution.py:460
  20.0 0.0 collective-permute-start.2
  20.0 5.1 %collective-permute-start.1 = (s32[33]{0:T(128)}, s32[33]{0:T(128)S(1)}, u32[]{:S(2)}, u32[]{:S(2)}) collective-permute-start(s32[33]{0:T(128)} %get-tuple-element.18.oth_t), channel_id=1, source_target_pairs={{0,127},{1,0},{2,1},{3,2},{4,3},{5,4},{6,5},{7,6},{8,7},{9,8},{10,... | collective-permute-start | bytes 404 | tf_op jit(solution)/shard_map/ppermute | solution.py:460
  25.1 0.0 collective-permute-start
  25.1 0.0 copy-start.12
  25.1 0.7 copy-done.12
  25.7 6.5 %shard_map.128 = (bf16[32,256,256]{2,1,0:T(8,128)(2,1)S(1)}, f32[32,16,256]{2,1,0:T(8,128)S(1)}) custom-call(s32[33]{0:T(128)S(1)} %copy-done.12, s32[64]{0:T(128)S(1)} %copy-done.20, f32[64,16,256]{2,1,0:T(8,128)S(1)} %copy-done.17, s32[64,4,256]{2,1,0:T(4,128)S(1)} %copy-done.18, f32[64,4,256]{2,1,0:T(4,128)S(1)} %copy-done.19), custom_call_target="tpu_custom_call" | custom-call | flops 536870912 | bytes 6291456 | tf_op jit(solution)/shard_map/pallas_call | solution.py:136
  32.3 0.0 collective-permute-done.1.upp_t
  32.3 0.0 collective-permute-done.low_t
  32.3 0.0 collective-permute-done.3.upp
  32.3 0.0 collective-permute-done.2.low
  32.3 0.0 copy-start
  32.3 0.9 copy-done
  33.3 0.0 copy-start.3
  33.3 0.9 copy-done.3
  34.2 0.0 copy-start.4
  34.2 0.7 copy-done.4
  34.9 0.0 copy-start.6
  34.9 0.7 copy-done.6
  35.6 0.0 copy-start.10
  35.6 0.7 copy-done.10
  36.3 13.6 %shard_map.130 = bf16[128,32,128]{2,1,0:T(8,128)(2,1)S(1)} custom-call(s32[1]{0:T(128)} %bitcast.me_ref, s32[33]{0:T(128)S(1)} %copy-done.10, s32[33]{0:T(128)S(1)} %collective-permute-done.low_t, s32[33]{0:T(128)S(1)} %collective-permute-done.1.upp_t, f32[32,16,256]{2,1,0:T(8,128)S(1)} %get-tuple-element.20.own, ...), custom_call_target="tpu_custom_call" | custom-call | tf_op jit(solution)/shard_map/pallas_call | solution.py:229
  50.0 31.6 %all_to_all.10.data = bf16[128,32,128]{2,1,0:T(8,128)(2,1)S(1)} all-to-all(bf16[128,32,128]{2,1,0:T(8,128)(2,1)S(1)} %shard_map.130), channel_id=1, replica_groups=mesh['dom'=8,'order'=16] {'dom','order'}, dimensions={0} | all-to-all | bytes 2097152 | tf_op jit(solution)/shard_map/all_to_all | solution.py:476
  81.5 0.0 copy-done.8
  81.5 0.0 copy-done.9
  81.5 0.0 copy-start.1
  81.5 0.0 copy-start.2
  81.5 0.0 copy-start.5
  81.5 0.0 copy-start.7
  81.6 0.0 copy-start.11
  81.6 13.2 %shard_map.131 = bf16[128,32,128]{2,1,0:T(8,128)(2,1)S(1)} custom-call(s32[1]{0:T(128)} %bitcast.me_ref, bf16[8,1024,1024]{2,1,0:T(8,128)(2,1)} %table.1, bf16[128,32,128]{2,1,0:T(8,128)(2,1)S(1)} %all_to_all.10.data, f32[1,1024]{1,0:T(1,128)S(1)} %bitcast.3, f32[1,1024]{1,0:T(1,128)S(1)} %bitcast.4), custom_call_target="tpu_custom_call" | custom-call | tf_op jit(solution)/shard_map/pallas_call | solution.py:303
  94.8 0.0 copy-start.13
  94.8 0.0 copy-start.15
  94.8 0.0 copy-start.16
  94.8 23.0 %all_to_all.11.data = bf16[128,32,128]{2,1,0:T(8,128)(2,1)S(1)} all-to-all(bf16[128,32,128]{2,1,0:T(8,128)(2,1)S(1)} %shard_map.131), channel_id=1, replica_groups=mesh['dom'=8,'order'=16] {'dom','order'}, dimensions={0} | all-to-all | bytes 2097152 | tf_op jit(solution)/shard_map/all_to_all | solution.py:478
  117.9 0.0 copy-done.1
  117.9 0.0 copy-done.2
  117.9 0.0 copy-done.5
  117.9 0.0 copy-done.7
  117.9 0.0 copy-done.11
  117.9 11.3 %shard_map.132 = (f32[32,16,256]{2,1,0:T(8,128)S(1)}, bf16[32,16,256]{2,1,0:T(8,128)(2,1)S(1)}, bf16[32,16,256]{2,1,0:T(8,128)(2,1)S(1)}) custom-call(s32[1]{0:T(128)} %bitcast.me_ref, s32[33]{0:T(128)S(1)} %copy-done.11, s32[33]{0:T(128)S(1)} %collective-permute-done.low_t, s32[33]{0:T(128)S(1)} %collective-permute-done.1.upp_t, ...), custom_call_target="tpu_custom_call" | custom-call | tf_op jit(solution)/shard_map/pallas_call | solution.py:372
  129.2 0.6 collective-permute-start.4
  129.7 4.6 %collective-permute-start.5 = (bf16[32,16,256]{2,1,0:T(8,128)(2,1)S(1)}, bf16[32,16,256]{2,1,0:T(8,128)(2,1)S(1)}, u32[]{:S(2)}, u32[]{:S(2)}) collective-permute-start(bf16[32,16,256]{2,1,0:T(8,128)(2,1)S(1)} %get-tuple-element.25), channel_id=1, source_target_pairs={{0,127},{1,0},{2,1},{3,2},{4,3},{5,4},{6,5},{7,6},{8,7},{9,8},{10,... | collective-permute-start | bytes 786440 | tf_op jit(solution)/shard_map/ppermute | solution.py:460
  134.3 1.2 shard_map.133.own
  135.5 6.0 %collective-permute-done.4.low = bf16[32,16,256]{2,1,0:T(8,128)(2,1)S(1)} collective-permute-done((bf16[32,16,256]{2,1,0:T(8,128)(2,1)S(1)}, bf16[32,16,256]{2,1,0:T(8,128)(2,1)S(1)}, u32[]{:S(2)}, u32[]{:S(2)}) %collective-permute-start.4) | collective-permute-done | bytes 262176 | tf_op jit(solution)/shard_map/ppermute | solution.py:460
  141.5 0.0 collective-permute-done.5.upp
  141.5 0.0 copy-done.13
  141.5 0.0 copy-done.15
  141.5 0.0 copy-done.16
  141.5 2.7 %shard_map.134 = f32[64,16,256]{2,1,0:T(8,128)} custom-call(s32[1]{0:T(128)} %bitcast.me_ref, s32[33]{0:T(128)S(1)} %copy-done.13, s32[33]{0:T(128)S(1)} %copy-done.15, s32[33]{0:T(128)S(1)} %copy-done.16, f32[32,16,256]{2,1,0:T(8,128)S(1)} %shard_map.133.own, bf16[32,16,256]{2,1,0:T(8,128)(2,1)S(1)} %collective-permute-done.4.low, ...), custom_call_target="tpu_custom_call" | custom-call | tf_op jit(solution)/shard_map/pallas_call | solution.py:446
Async XLA Ops:
  1.7 0.6 copy-start.14
  2.3 1.2 copy-start.17
  3.5 0.9 copy-start.18
  4.5 0.9 copy-start.19
  5.4 0.7 copy-start.20
  6.1 75.4 %copy-start.8 = (f32[1024]{0:T(1024)S(1)}, f32[1024]{0:T(1024)}, u32[]{:S(2)}) copy-start(f32[1024]{0:T(1024)} %param.18) | copy-start | bytes 12292
  6.1 75.4 %copy-start.9 = (f32[1024]{0:T(1024)S(1)}, f32[1024]{0:T(1024)}, u32[]{:S(2)}) copy-start(f32[1024]{0:T(1024)} %param.19) | copy-start | bytes 12292
  12.7 19.6 %collective-permute-start.3 = (bf16[32,16,256]{2,1,0:T(8,128)(2,1)S(1)}, bf16[32,16,256]{2,1,0:T(8,128)(2,1)S(1)}, u32[]{:S(2)}, u32[]{:S(2)}) collective-permute-start(bf16[32,16,256]{2,1,0:T(8,128)(2,1)S(1)} %get-tuple-element.21), channel_id=1, source_target_pairs={{0,127},{1,0},{2,1},{3,2},{4,3},{5,4},{6,5},{7,6},{8,7},{9,8},{10,... | collective-permute-start | bytes 786440 | tf_op jit(solution)/shard_map/ppermute | solution.py:460
  20.0 12.3 %collective-permute-start.2 = (bf16[32,16,256]{2,1,0:T(8,128)(2,1)S(1)}, bf16[32,16,256]{2,1,0:T(8,128)(2,1)S(1)}, u32[]{:S(2)}, u32[]{:S(2)}) collective-permute-start(bf16[32,16,256]{2,1,0:T(8,128)(2,1)S(1)} %get-tuple-element.21), channel_id=1, source_target_pairs={{0,1},{1,2},{2,3},{3,4},{4,5},{5,6},{6,7},{7,8},{8,9},{9,10},{10,1... | collective-permute-start | bytes 786440 | tf_op jit(solution)/shard_map/ppermute | solution.py:460
  20.0 12.3 %collective-permute-start.1 = (s32[33]{0:T(128)}, s32[33]{0:T(128)S(1)}, u32[]{:S(2)}, u32[]{:S(2)}) collective-permute-start(s32[33]{0:T(128)} %get-tuple-element.18.oth_t), channel_id=1, source_target_pairs={{0,127},{1,0},{2,1},{3,2},{4,3},{5,4},{6,5},{7,6},{8,7},{9,8},{10,... | collective-permute-start | bytes 404 | tf_op jit(solution)/shard_map/ppermute | solution.py:460
  25.1 7.2 %collective-permute-start = (s32[33]{0:T(128)}, s32[33]{0:T(128)S(1)}, u32[]{:S(2)}, u32[]{:S(2)}) collective-permute-start(s32[33]{0:T(128)} %get-tuple-element.18.oth_t), channel_id=1, source_target_pairs={{0,1},{1,2},{2,3},{3,4},{4,5},{5,6},{6,7},{7,8},{8,9},{9,10},{10,1... | collective-permute-start | bytes 404 | tf_op jit(solution)/shard_map/ppermute | solution.py:460
  25.1 0.7 copy-start.12
  32.3 1.0 copy-start
  33.3 0.9 copy-start.3
  34.2 0.7 copy-start.4
  34.9 0.7 copy-start.6
  35.6 0.7 copy-start.10
  81.5 36.3 %copy-start.1 = (bf16[256,512]{1,0:T(8,128)(2,1)S(1)}, bf16[256,512]{1,0:T(8,128)(2,1)}, u32[]{:S(2)}) copy-start(bf16[256,512]{1,0:T(8,128)(2,1)} %constant.22.clone.second) | copy-start | bytes 786436
  81.5 36.3 %copy-start.2 = (bf16[256,512]{1,0:T(8,128)(2,1)S(1)}, bf16[256,512]{1,0:T(8,128)(2,1)}, u32[]{:S(2)}) copy-start(bf16[256,512]{1,0:T(8,128)(2,1)} %constant.25.clone.last) | copy-start | bytes 786436
  81.5 36.3 %copy-start.5 = (f32[16,256]{1,0:T(8,128)S(1)}, f32[16,256]{1,0:T(8,128)}, u32[]{:S(2)}) copy-start(f32[16,256]{1,0:T(8,128)} %constant.24.clone.tws) | copy-start | bytes 49156
  81.5 36.3 %copy-start.7 = (f32[16,256]{1,0:T(8,128)S(1)}, f32[16,256]{1,0:T(8,128)}, u32[]{:S(2)}) copy-start(f32[16,256]{1,0:T(8,128)} %constant.23.clone.twc) | copy-start | bytes 49156
  81.6 36.3 %copy-start.11 = (s32[33]{0:T(128)S(1)}, s32[33]{0:T(128)}, u32[]{:S(2)}) copy-start(s32[33]{0:T(128)} %get-tuple-element.19.own_t) | copy-start | bytes 400
  94.8 46.7 %copy-start.13 = (s32[33]{0:T(128)S(1)}, s32[33]{0:T(128)}, u32[]{:S(2)}) copy-start(s32[33]{0:T(128)} %get-tuple-element.16.pick.own_b) | copy-start | bytes 400
  94.8 46.7 %copy-start.15 = (s32[33]{0:T(128)S(1)}, s32[33]{0:T(128)}, u32[]{:S(2)}) copy-start(s32[33]{0:T(128)} %get-tuple-element.17.pick.oth_b) | copy-start | bytes 400
  94.8 46.7 %copy-start.16 = (s32[33]{0:T(128)S(1)}, s32[33]{0:T(128)}, u32[]{:S(2)}) copy-start(s32[33]{0:T(128)} %get-tuple-element.18.oth_t) | copy-start | bytes 400
  129.2 12.3 %collective-permute-start.4 = (bf16[32,16,256]{2,1,0:T(8,128)(2,1)S(1)}, bf16[32,16,256]{2,1,0:T(8,128)(2,1)S(1)}, u32[]{:S(2)}, u32[]{:S(2)}) collective-permute-start(bf16[32,16,256]{2,1,0:T(8,128)(2,1)S(1)} %get-tuple-element.24), channel_id=1, source_target_pairs={{0,1},{1,2},{2,3},{3,4},{4,5},{5,6},{6,7},{7,8},{8,9},{9,10},{10,1... | collective-permute-start | bytes 786440 | tf_op jit(solution)/shard_map/ppermute | solution.py:460
  129.7 11.8 %collective-permute-start.5 = (bf16[32,16,256]{2,1,0:T(8,128)(2,1)S(1)}, bf16[32,16,256]{2,1,0:T(8,128)(2,1)S(1)}, u32[]{:S(2)}, u32[]{:S(2)}) collective-permute-start(bf16[32,16,256]{2,1,0:T(8,128)(2,1)S(1)} %get-tuple-element.25), channel_id=1, source_target_pairs={{0,127},{1,0},{2,1},{3,2},{4,3},{5,4},{6,5},{7,6},{8,7},{9,8},{10,... | collective-permute-start | bytes 786440 | tf_op jit(solution)/shard_map/ppermute | solution.py:460

commit v2 on v1

v2 whole, which is shorter than its diff:
```python
import functools
import math

import jax
import jax.numpy as jnp
import numpy as np
from jax import lax
from jax.experimental import pallas as pl
from jax.experimental.pallas import tpu as pltpu
from jax.sharding import PartitionSpec as P

AXES = ("dom", "order")
DEVS = 128
NF = 16
BLOCK = 256
BLK = 64
HALF_BLK = 32
TILES = 256
LAT = 16
ORD = 8
NLAT = 1024
NDEG = 1024
RADIX = 16
NQ = 64
STEP = 8
F32 = jnp.float32
BF16 = jnp.bfloat16
MIB = 1 << 20

SMEM = pltpu.SMEM
VMEM = pltpu.VMEM


def hi_lo(table):
    table = np.asarray(table, np.float32)
    hi = table.astype(jnp.bfloat16)
    lo = (table - hi.astype(np.float32)).astype(jnp.bfloat16)
    return hi, lo


def make_tables():
    points = np.arange(BLOCK)
    angle = 2 * np.pi * ((np.arange(NQ)[:, None] * points[None, :]) % BLOCK) / BLOCK
    cos, sin = np.cos(angle), np.sin(angle)
    second = np.concatenate(
        [np.concatenate([cos, sin], axis=1), np.concatenate([-sin, cos], axis=1)], axis=0
    )
    s_hi, s_lo = hi_lo(second)
    twist = 2 * np.pi * (np.arange(RADIX)[:, None] * points[None, :]) / 4096.0
    return dict(
        second=np.concatenate([s_hi, s_lo], axis=0),
        twc=np.cos(twist).astype(np.float32),
        tws=np.sin(twist).astype(np.float32),
    )


ROOT = math.sqrt(0.5)
COS1 = math.cos(math.pi / 8)
SIN1 = math.sin(math.pi / 8)


def real_dft16(g):
    e = [g[s] + g[s + 8] for s in range(8)]
    o = [g[s] - g[s + 8] for s in range(8)]
    re, im = [None] * 9, [None] * 9
    ee = [e[s] + e[s + 4] for s in range(4)]
    eo = [e[s] - e[s + 4] for s in range(4)]
    x, y = ee[0] + ee[2], ee[1] + ee[3]
    re[0], re[8] = x + y, x - y
    re[4], im[4] = ee[0] - ee[2], ee[3] - ee[1]

    def odd4(p):
        d, s = (p[1] - p[3]) * ROOT, (p[1] + p[3]) * ROOT
        return (p[0] + d, -(s + p[2])), (p[0] - d, p[2] - s)

    (re[2], im[2]), (re[6], im[6]) = odd4(eo)
    a1, a3 = odd4(o[0::2])
    b1, b3 = odd4(o[1::2])
    t = (b1[0] * COS1 + b1[1] * SIN1, b1[1] * COS1 - b1[0] * SIN1)
    re[1], im[1] = a1[0] + t[0], a1[1] + t[1]
    re[7], im[7] = a1[0] - t[0], t[1] - a1[1]
    t = (b3[0] * SIN1 + b3[1] * COS1, b3[1] * SIN1 - b3[0] * COS1)
    re[3], im[3] = a3[0] + t[0], a3[1] + t[1]
    re[5], im[5] = a3[0] - t[0], t[1] - a3[1]
    return re, im


def real_idft16(a, b):
    x, z = a[0] + a[8], a[0] - a[8]
    q = [x + a[4], z - b[4], x - a[4], z + b[4]]

    def odd4(p1, p3):
        d, s = (p1[0] - p3[0]) * ROOT, (p1[1] + p3[1]) * ROOT
        return [p1[0] + p3[0], d - s, p3[1] - p1[1], -(d + s)]

    w = odd4((a[2], b[2]), (a[6], b[6]))
    even = [q[t] + w[t] for t in range(4)] + [q[t] - w[t] for t in range(4)]
    p1, q1 = (a[1] + a[7], b[1] - b[7]), (a[1] - a[7], b[1] + b[7])
    p3, q3 = (a[3] + a[5], b[3] - b[5]), (a[3] - a[5], b[3] + b[5])
    q1 = (q1[0] * COS1 - q1[1] * SIN1, q1[0] * SIN1 + q1[1] * COS1)
    q3 = (q3[0] * SIN1 - q3[1] * COS1, q3[0] * COS1 + q3[1] * SIN1)
    oe, oo = odd4(p1, p3), odd4(q1, q3)
    odd = [oe[s // 2] if s % 2 == 0 else oo[s // 2] for s in range(8)]
    return [even[s] + odd[s] for s in range(8)] + [even[s] - odd[s] for s in range(8)]


def vmem_spec():
    return pl.BlockSpec(memory_space=VMEM)


def smem_spec():
    return pl.BlockSpec(memory_space=SMEM)


def plain_spec():
    return pl.BlockSpec()


def cost(micros):
    return pl.CostEstimate(flops=micros * 10**9, bytes_accessed=4 * MIB, transcendentals=0)


def params(mib):
    return pltpu.CompilerParams(vmem_limit_bytes=mib * MIB)


OWN_B, OWN_T, OTH_B, OTH_T, COUNT, LISTS = 0, 40, 80, 120, 160, 224


def make_lists(tile_ref, count_ref, lists):
    me = lax.axis_index(AXES)

    def step(b, counts):
        own_n, oth_n = counts
        tile = tile_ref[b]
        own = (lax.shift_right_logical(tile, 8) == me).astype(jnp.int32)
        lists[OWN_B + own_n] = b
        lists[OWN_T + own_n] = tile
        lists[OTH_B + oth_n] = b
        lists[OTH_T + oth_n] = tile
        lists[COUNT + b] = count_ref[b]
        return own_n + own, oth_n + 1 - own

    lax.fori_loop(0, BLK, step, (jnp.int32(0), jnp.int32(0)), unroll=4)


def spread_blocks(first, lists, ssh, index, weight, wt_out, out):
    base = pl.program_id(0) * STEP
    lanes = lax.broadcasted_iota(jnp.int32, (4, BLOCK), 1)
    points = lax.broadcasted_iota(jnp.int32, (BLOCK, BLOCK), 0).astype(F32).astype(BF16)
    zero = jnp.bfloat16(0)
    for i in range(STEP):
        b = lists[first + base + i]
        idx = index[b].astype(F32).astype(BF16)
        wgt = jnp.where(lanes < lists[COUNT + b], weight[b], 0.0).astype(BF16)
        mat = jnp.where(points == idx[0:1], wgt[0:1], zero)
        for k in range(1, 4):
            mat = mat + jnp.where(points == idx[k : k + 1], wgt[k : k + 1], zero)
        wt_out[i] = mat
        heights = ssh[b]
        hi = heights.astype(BF16)
        lo = (heights - hi.astype(F32)).astype(BF16)
        both = lax.dot_general(
            jnp.concatenate([hi, lo], axis=0),
            mat,
            (((1,), (1,)), ((), ())),
            preferred_element_type=F32,
        )
        out[i] = (both[:NF] + both[NF:]).astype(out.dtype)


def other_kernel(
    tile_hbm, count_hbm, ssh_hbm, index_hbm, weight_hbm, lists, wt_out, out,
    tile_ref, count_ref, ssh, index, weight, sems
):
    @pl.when(pl.program_id(0) == 0)
    def _():
        pairs = [
            (tile_hbm, tile_ref),
            (count_hbm, count_ref),
            (index_hbm, index),
            (weight_hbm, weight),
            (ssh_hbm, ssh),
        ]
        copies = [pltpu.make_async_copy(s, d, sems.at[i]) for i, (s, d) in enumerate(pairs)]
        for copy in copies:
            copy.start()
        copies[0].wait()
        copies[1].wait()
        make_lists(tile_ref, count_ref, lists)
        for copy in copies[2:]:
            copy.wait()

    spread_blocks(OTH_B, lists, ssh, index, weight, wt_out, out)


def own_spread_kernel(lists, ssh, index, weight, wt_out, out):
    spread_blocks(OWN_B, lists, ssh, index, weight, wt_out, out)


def whole(shape):
    return pl.BlockSpec(shape, lambda i: (0,) * len(shape))


def spread_half(scalars, ssh, index, weight, dtype, with_lists):
    shapes = (
        jax.ShapeDtypeStruct((HALF_BLK, BLOCK, BLOCK), BF16),
        jax.ShapeDtypeStruct((HALF_BLK, NF, BLOCK), dtype),
    )
    specs = (
        pl.BlockSpec((STEP, BLOCK, BLOCK), lambda i: (i, 0, 0)),
        pl.BlockSpec((STEP, NF, BLOCK), lambda i: (i, 0, 0)),
    )
    if with_lists:
        shapes = (jax.ShapeDtypeStruct((LISTS,), jnp.int32),) + shapes
        specs = (smem_spec(),) + specs
        in_specs = [pl.BlockSpec(memory_space=pltpu.HBM)] * 5
        scratch = [
            SMEM((BLK,), jnp.int32),
            SMEM((BLK,), jnp.int32),
            VMEM((BLK, NF, BLOCK), F32),
            VMEM((BLK, 4, BLOCK), jnp.int32),
            VMEM((BLK, 4, BLOCK), F32),
            pltpu.SemaphoreType.DMA((5,)),
        ]
    else:
        in_specs = [
            smem_spec(),
            whole((BLK, NF, BLOCK)),
            whole((BLK, 4, BLOCK)),
            whole((BLK, 4, BLOCK)),
        ]
        scratch = []
    return pl.pallas_call(
        other_kernel if with_lists else own_spread_kernel,
        grid=(HALF_BLK // STEP,),
        out_shape=shapes,
        in_specs=in_specs,
        out_specs=specs,
        scratch_shapes=scratch,
        compiler_params=params(14),
        cost_estimate=cost(5),
    )(*scalars, ssh, index, weight)


def forward_kernel(lists, low_t, upp_t, own, low, upp, second, twc, tws, out, grid, mid, wide):
    me = lax.axis_index(AXES)
    flip = jnp.where(me >= DEVS // 2, 0xF0, 0)
    grid[...] = jnp.zeros_like(grid)

    def add_own(i, carry):
        tile = (lists[OWN_T + i] & 255) ^ flip
        grid[tile] = grid[tile] + own[i]
        return carry

    lax.fori_loop(0, HALF_BLK, add_own, 0, unroll=4)

    def add_other(tiles, values):
        def body(i, carry):
            tile = tiles[OTH_T + i]
            mine = lax.shift_right_logical(tile, 8) == me
            spot = jnp.where(mine, (tile & 255) ^ flip, TILES)
            grid[spot] = grid[spot] + values[i].astype(F32)
            return carry

        lax.fori_loop(0, HALF_BLK, body, 0, unroll=4)

    add_other(low_t, low)
    add_other(upp_t, upp)

    def circle(r, carry):
        for h in range(2):
            lanes = slice(h * 128, h * 128 + 128)
            re, im = real_dft16([grid[r * RADIX + s, :, lanes] for s in range(RADIX)])
            for u in range(RADIX):
                v = min(u, RADIX - u)
                cu, su = twc[u : u + 1, lanes], tws[u : u + 1, lanes]
                if u == 0:
                    x, y = re[0], jnp.zeros_like(re[0])
                elif u == 8:
                    x, y = re[8] * cu, -(re[8] * su)
                elif u < 8:
                    x, y = re[v] * cu + im[v] * su, im[v] * cu - re[v] * su
                else:
                    x, y = re[v] * cu - im[v] * su, -(im[v] * cu + re[v] * su)
                rows = slice(u * NF, u * NF + NF)
                mid[r, rows, h * 128 : h * 128 + 128] = x.astype(BF16)
                mid[r, rows, 256 + h * 128 : 256 + h * 128 + 128] = y.astype(BF16)
        return carry

    lax.fori_loop(0, LAT, circle, 0, unroll=2)
    for r in range(LAT):
        res = lax.dot_general(
            second[...], mid[r], (((1,), (1,)), ((), ())), preferred_element_type=F32
        )
        res = (res[:128] + res[128:]) * (1.0 / 4096.0)
        for c in range(2):
            for uh in range(2):
                wide[pl.ds(uh * 32 + c * 16 + r, NQ, stride=64), :] = res[
                    c * NQ : c * NQ + NQ, uh * 128 : uh * 128 + 128
                ]
    out[...] = wide[...].astype(BF16).reshape(out.shape)


def forward(lists, low_t, upp_t, own, low, upp, tables):
    return pl.pallas_call(
        forward_kernel,
        out_shape=jax.ShapeDtypeStruct((DEVS, 32, 128), BF16),
        in_specs=[smem_spec()] * 3 + [vmem_spec()] * 3 + [plain_spec()] * 3,
        out_specs=vmem_spec(),
        scratch_shapes=[
            VMEM((TILES + 1, NF, BLOCK), F32),
            VMEM((LAT, RADIX * NF, 2 * BLOCK), BF16),
            VMEM((DEVS * 32, 128), F32),
        ],
        compiler_params=params(18),
        cost_estimate=cost(8),
    )(lists, low_t, upp_t, own, low, upp, tables["second"], tables["twc"], tables["tws"])


def legendre_kernel(table, data, gauss, love, out, ins, outs):
    first_order = lax.axis_index(AXES) * ORD
    gw = gauss[...]
    for c in range(2):
        north = jnp.concatenate([data[i, c * 16 : c * 16 + 16] for i in range(64)], axis=0)
        south = jnp.concatenate([data[127 - i, c * 16 : c * 16 + 16] for i in range(64)], axis=0)
        north = north.astype(F32).T
        south = south.astype(F32).T
        even = ((north + south) * gw).astype(BF16)
        odd = ((north - south) * gw).astype(BF16)
        ins[:, c * 16 : c * 16 + 16, :] = even.reshape(ORD, NF, NLAT)
        ins[:, 32 + c * 16 : 32 + c * 16 + 16, :] = odd.reshape(ORD, NF, NLAT)
    degree = lax.broadcasted_iota(jnp.int32, (32, NDEG), 1)
    for k in range(ORD):
        both = jnp.dot(ins[k], table[k], preferred_element_type=F32)
        order = first_order + k
        is_even = ((degree + order) & 1) == 0
        coef = jnp.where(is_even, both[:32], both[32:])
        coef = jnp.where(degree < order, 0.0, coef)
        coef = coef * love[...]
        parts = jnp.concatenate(
            [jnp.where(is_even, coef, 0.0), jnp.where(is_even, 0.0, coef)], axis=0
        ).astype(BF16)
        res = lax.dot_general(
            parts, table[k], (((1,), (1,)), ((), ())), preferred_element_type=F32
        )
        upper = res[:32] + res[32:]
        lower = res[:32] - res[32:]
        for c in range(2):
            outs[c, 0, k * NF : k * NF + NF, :] = upper[c * 16 : c * 16 + 16]
            outs[c, 1, k * NF : k * NF + NF, :] = lower[c * 16 : c * 16 + 16]
    for c in range(2):
        up = outs[c, 0].T.astype(BF16)
        dn = outs[c, 1].T.astype(BF16)
        for i in range(64):
            out[i, c * 16 : c * 16 + 16] = up[i * 16 : i * 16 + 16]
            out[127 - i, c * 16 : c * 16 + 16] = dn[i * 16 : i * 16 + 16]


def legendre_both(table, data, gauss, love):
    return pl.pallas_call(
        legendre_kernel,
        out_shape=jax.ShapeDtypeStruct((DEVS, 32, 128), BF16),
        in_specs=[plain_spec(), vmem_spec(), plain_spec(), plain_spec()],
        out_specs=vmem_spec(),
        scratch_shapes=[VMEM((ORD, 64, NLAT), BF16), VMEM((2, 2, 128, NLAT), F32)],
        compiler_params=params(12),
        cost_estimate=cost(11),
    )(table, data, gauss.reshape(1, NLAT), love.reshape(1, NDEG))


def inverse_kernel(
    lists, low_t, upp_t, data, second, twc, tws, own, low, upp, wide, tiles, waves
):
    me = lax.axis_index(AXES)
    flip = jnp.where(me >= DEVS // 2, 0xF0, 0)
    wide[...] = data[...].astype(F32).reshape(wide.shape)
    row = lax.broadcasted_iota(jnp.int32, (NQ, 128), 0)
    lane = lax.broadcasted_iota(jnp.int32, (NQ, 128), 1)
    zonal = jnp.where((row == 0) & (lane < NF), 1.0, 2.0)
    for r in range(LAT):
        parts = []
        for c in range(2):
            left = wide[pl.ds(c * 16 + r, NQ, stride=64), :] * zonal
            right = wide[pl.ds(32 + c * 16 + r, NQ, stride=64), :] * 2.0
            parts.append(jnp.concatenate([left, right], axis=1))
        spectrum = jnp.concatenate(parts, axis=0).T.astype(BF16)
        spectrum = jnp.concatenate([spectrum, spectrum], axis=1)
        waves[r] = jnp.dot(spectrum, second[...], preferred_element_type=F32)

    def circle(r, carry):
        for h in range(2):
            lanes = slice(h * 128, h * 128 + 128)
            re, im = {}, {}
            for u in range(RADIX):
                rows = slice(u * NF, u * NF + NF)
                x = waves[r, rows, h * 128 : h * 128 + 128]
                y = waves[r, rows, 256 + h * 128 : 256 + h * 128 + 128]
                cu, su = twc[u : u + 1, lanes], tws[u : u + 1, lanes]
                re[u] = x * cu - y * su if u else x
                if u not in (0, 8):
                    im[u] = x * su + y * cu
            a = [re[0]] + [re[u] + re[RADIX - u] for u in range(1, 8)] + [re[8]]
            b = [None] + [im[u] - im[RADIX - u] for u in range(1, 8)]
            values = real_idft16(a, b)
            for s in range(RADIX):
                tiles[r * RADIX + s, :, lanes] = values[s]
        return carry

    lax.fori_loop(0, LAT, circle, 0)

    def gather(i, carry):
        own[i] = tiles[(lists[OWN_T + i] & 255) ^ flip]
        low[i] = tiles[(low_t[OTH_T + i] & 255) ^ flip].astype(BF16)
        upp[i] = tiles[(upp_t[OTH_T + i] & 255) ^ flip].astype(BF16)
        return carry

    lax.fori_loop(0, HALF_BLK, gather, 0, unroll=4)


def inverse(lists, low_t, upp_t, data, tables):
    return pl.pallas_call(
        inverse_kernel,
        out_shape=(
            jax.ShapeDtypeStruct((HALF_BLK, NF, BLOCK), F32),
            jax.ShapeDtypeStruct((HALF_BLK, NF, BLOCK), BF16),
            jax.ShapeDtypeStruct((HALF_BLK, NF, BLOCK), BF16),
        ),
        in_specs=[smem_spec()] * 3 + [vmem_spec()] + [plain_spec()] * 3,
        out_specs=(vmem_spec(),) * 3,
        scratch_shapes=[
            VMEM((DEVS * 32, 128), F32),
            VMEM((TILES, NF, BLOCK), F32),
            VMEM((LAT, RADIX * NF, 2 * BLOCK), F32),
        ],
        compiler_params=params(20),
        cost_estimate=cost(7),
    )(lists, low_t, upp_t, data, tables["second"], tables["twc"], tables["tws"])


def own_kernel(values, wt, out):
    for i in range(STEP):
        val = values[i]
        hi = val.astype(BF16)
        lo = (val - hi.astype(F32)).astype(BF16)
        both = jnp.dot(jnp.concatenate([hi, lo], axis=0), wt[i], preferred_element_type=F32)
        out[i] = both[:NF] + both[NF:]


def own_cells(values, wt):
    return pl.pallas_call(
        own_kernel,
        grid=(HALF_BLK // STEP,),
        out_shape=jax.ShapeDtypeStruct((HALF_BLK, NF, BLOCK), F32),
        in_specs=[
            pl.BlockSpec((STEP, NF, BLOCK), lambda i: (i, 0, 0)),
            pl.BlockSpec((STEP, BLOCK, BLOCK), lambda i: (i, 0, 0)),
        ],
        out_specs=pl.BlockSpec((STEP, NF, BLOCK), lambda i: (i, 0, 0)),
        compiler_params=params(8),
        cost_estimate=cost(2),
    )(values, wt)


def cells_kernel(lists, own, low, upp, wt, out):
    me = lax.axis_index(AXES)
    step_id = pl.program_id(0)

    @pl.when(step_id == 0)
    def _():
        def copy(i, carry):
            out[lists[OWN_B + i]] = own[i]
            return carry

        lax.fori_loop(0, HALF_BLK, copy, 0, unroll=2)

    for i in range(STEP):
        slot = step_id * STEP + i
        above = lax.shift_right_logical(lists[OTH_T + slot], 8) > me
        val = jnp.where(above, upp[slot], low[slot])
        out[lists[OTH_B + slot]] = jnp.dot(val, wt[i], preferred_element_type=F32)


def all_cells(lists, own, low, upp, wt):
    return pl.pallas_call(
        cells_kernel,
        grid=(HALF_BLK // STEP,),
        out_shape=jax.ShapeDtypeStruct((BLK, NF, BLOCK), F32),
        in_specs=[smem_spec()]
        + [vmem_spec()] * 3
        + [pl.BlockSpec((STEP, BLOCK, BLOCK), lambda i: (i, 0, 0))],
        out_specs=pl.BlockSpec((BLK, NF, BLOCK), lambda i: (0, 0, 0)),
        compiler_params=params(8),
        cost_estimate=cost(4),
    )(lists, own, low, upp, wt)


def shift(value, steps):
    pairs = [(source, (source + steps) % DEVS) for source in range(DEVS)]
    return lax.ppermute(value, AXES, pairs)


def on_device(
    tables, ssh, cell_count, remap_index, remap_weight, block_tile, gauss_weight, love, legendre
):
    lists, wt_oth, oth = spread_half(
        (block_tile, cell_count), ssh, remap_index, remap_weight, BF16, True
    )
    low_t = shift(lists, 1)
    upp_t = shift(lists, -1)
    low = shift(oth, 1)
    upp = shift(oth, -1)
    wt_own, own = spread_half((lists,), ssh, remap_index, remap_weight, F32, False)
    fourier = forward(lists, low_t, upp_t, own, low, upp, tables)
    by_order = lax.all_to_all(fourier, AXES, split_axis=0, concat_axis=0, tiled=True)
    synth = legendre_both(legendre, by_order, gauss_weight, love)
    by_lat = lax.all_to_all(synth, AXES, split_axis=0, concat_axis=0, tiled=True)
    own_v, low_v, upp_v = inverse(lists, low_t, upp_t, by_lat, tables)
    from_low = shift(upp_v, 1)
    from_upp = shift(low_v, -1)
    own_cell = own_cells(own_v, wt_own)
    return all_cells(lists, own_cell, from_low, from_upp, wt_oth)


def solution(mesh):
    tables = {name: jnp.asarray(table) for name, table in make_tables().items()}
    return jax.shard_map(
        functools.partial(on_device, tables),
        mesh=mesh,
        in_specs=(
            P(AXES, None, None),
            P(AXES),
            P(AXES, None, None),
            P(AXES, None, None),
            P(AXES),
            P(),
            P(),
            P(AXES, None, None),
        ),
        out_specs=P(AXES, None, None),
        check_vma=False,
    )
```

time: 145 us -> 116 us (0.80)
  Pallas kernels: 56.7 us -> 29.8 us
  waiting for transfers between devices: 6.01 us -> 13.9 us
  blocking collectives: 54.6 us -> 49.9 us
  local copies, waits for them, and re-layouts: 9.08 us -> 4.49 us
    pallas_call x4 -> x3, Pallas kernels: 28 us -> 15.2 us  [the longest x1 8.53 us: legendre_both(): pl.pallas_call(legendre_kernel, out_shape=jax.ShapeDtypeStruct((DEVS, 32,...]
    pallas_call x1, Pallas kernels: 13.6 us -> 5.64 us  [forward(): pl.pallas_call(forward_kernel, out_shape=jax.ShapeDtypeStruct((DEVS, 32,...]
    ppermute x6, waiting for transfers between devices: 6.01 us -> 13.9 us  [shift(): return lax.ppermute(value, AXES, pairs)]
    pallas_call x1, Pallas kernels: 11.3 us -> 5.08 us  [inverse(): pl.pallas_call(inverse_kernel, out_shape=(jax.ShapeDtypeStruct((HALF_BLK,...]
    all_to_all x1, blocking collectives: 31.6 us -> 26.9 us  [on_device(): lax.all_to_all(fourier, AXES, split_axis=0, concat_axis=0, tiled=True)]
    unnamed x42 -> x34, local copies, waits for them, and re-layouts: 9.08 us -> 4.49 us
  transfers between devices with their start and end apart: 6 -> 6, of which waited for: 1 -> 3; matrix products, arithmetic and copies ran while one was open for 0% -> 0% of each run, Pallas kernels for 5% -> 4%
where the time goes in v2:
time: 116 us
  blocking collectives  49.9 us (43%)
  Pallas kernels  29.8 us (26%)
  starting transfers between devices  17.6 us (15%)
  waiting for transfers between devices  13.9 us (12%)
  local copies, waits for them, and re-layouts  4.49 us (4%)
    all_to_all x1, blocking collectives, on_device(): lax.all_to_all(fourier, AXES, split_axis=0, concat_axis=0, tiled=True)  26.9 us
    all_to_all x1, blocking collectives, on_device(): lax.all_to_all(synth, AXES, split_axis=0, concat_axis=0, tiled=True)  23 us
    ppermute x6, starting transfers between devices, shift(): return lax.ppermute(value, AXES, pairs)  17.6 us
    ppermute x6, waiting for transfers between devices, shift(): return lax.ppermute(value, AXES, pairs)  13.9 us
    pallas_call x1, Pallas kernels, legendre_both(): pl.pallas_call(legendre_kernel, out_shape=jax.ShapeDtypeStruct((DEVS, 32,...  8.53 us
    pallas_call x2, Pallas kernels, spread_half(): pl.pallas_call(other_kernel if with_lists else own_spread_kernel, grid=(H...  6.7 us
    pallas_call x1, Pallas kernels, forward(): pl.pallas_call(forward_kernel, out_shape=jax.ShapeDtypeStruct((DEVS, 32,...  5.64 us
    pallas_call x1, Pallas kernels, inverse(): pl.pallas_call(inverse_kernel, out_shape=(jax.ShapeDtypeStruct((HALF_BLK,...  5.08 us
  transfers between devices with their start and end apart: 6, of which 3 were waited for; matrix products, arithmetic and copies ran while one was open for 0% of the time, Pallas kernels for 4%

profile of v2, /device:TPU:1, one launch (start us, length us, event | category | flops | bytes accessed | tf_op | source)
XLA Modules:
  0.0 115.9 jit_solution(16107318652077281105)
XLA Ops:
  0.0 0.0 copy-start
  0.0 1.2 %copy-done = f32[64,16,256]{2,1,0:T(8,128)S(1)} copy-done((f32[64,16,256]{2,1,0:T(8,128)S(1)}, f32[64,16,256]{2,1,0:T(8,128)}, u32[]{:S(2)}) %copy-start) | copy-done | bytes 1048600
  1.2 0.0 copy-start.2
  1.2 0.9 copy-done.2
  2.2 0.0 copy-start.4
  2.2 0.9 copy-done.4
  3.1 0.0 copy-start.8
  3.1 0.7 copy-done.8
  3.8 0.0 copy-start.9
  3.8 0.7 copy-done.9
  4.4 0.0 copy-start.1
  4.4 0.0 copy-start.3
  4.4 0.0 copy-start.5
  4.4 3.7 %shard_map.109 = (s32[224]{0:T(256)S(1)}, bf16[32,256,256]{2,1,0:T(8,128)(2,1)S(1)}, bf16[32,16,256]{2,1,0:T(8,128)(2,1)S(1)}) custom-call(s32[64]{0:T(128)S(1)} %copy-done.8, s32[64]{0:T(128)S(1)} %copy-done.9, f32[64,16,256]{2,1,0:T(8,128)S(1)} %copy-done, s32[64,4,256]{2,1,0:T(4,128)S(1)} %copy-done.2, f32[64,4,256]{2,1,0:T(4,128)S(1)} %copy-done.4), custom_call_target="tpu_custom_call" | custom-call | flops 5000000000 | bytes 4194304 | tf_op jit(solution)/shard_map/pallas_call | solution.py:234
  8.2 7.4 %collective-permute-start.1 = (s32[224]{0:T(256)S(1)}, s32[224]{0:T(256)S(1)}, u32[]{:S(2)}, u32[]{:S(2)}) collective-permute-start(s32[224]{0:T(256)S(1)} %get-tuple-element.13.lists), channel_id=1, source_target_pairs={{0,127},{1,0},{2,1},{3,2},{4,3},{5,4},{6,5},{7,6},{8,7},{9,8},{10,... | collective-permute-start | bytes 2696 | tf_op jit(solution)/shard_map/ppermute | solution.py:500
  15.6 0.0 collective-permute-start
  15.6 0.0 copy-start.10
  15.6 0.0 copy-start.11
  15.6 0.0 copy-start.12
  15.6 5.1 %collective-permute-start.3 = (bf16[32,16,256]{2,1,0:T(8,128)(2,1)S(1)}, bf16[32,16,256]{2,1,0:T(8,128)(2,1)S(1)}, u32[]{:S(2)}, u32[]{:S(2)}) collective-permute-start(bf16[32,16,256]{2,1,0:T(8,128)(2,1)S(1)} %get-tuple-element.15), channel_id=1, source_target_pairs={{0,127},{1,0},{2,1},{3,2},{4,3},{5,4},{6,5},{7,6},{8,7},{9,8},{10,... | collective-permute-start | bytes 786440 | tf_op jit(solution)/shard_map/ppermute | solution.py:500
  20.7 0.0 collective-permute-start.2
  20.7 0.0 copy-done.1
  20.7 0.0 copy-done.3
  20.7 0.0 copy-done.5
  20.7 0.0 slice-start
  20.7 0.0 slice-start.1
  20.7 3.0 %shard_map.110 = (bf16[32,256,256]{2,1,0:T(8,128)(2,1)S(1)}, f32[32,16,256]{2,1,0:T(8,128)S(1)}) custom-call(s32[224]{0:T(256)S(1)} %get-tuple-element.13.lists, f32[64,16,256]{2,1,0:T(8,128)S(1)} %copy-done.1, s32[64,4,256]{2,1,0:T(4,128)S(1)} %copy-done.3, f32[64,4,256]{2,1,0:T(4,128)S(1)} %copy-done.5), custom_call_target="tpu_custom_call" | custom-call | flops 5000000000 | bytes 4194304 | tf_op jit(solution)/shard_map/pallas_call | solution.py:234
  23.7 0.0 collective-permute-done.1.upp_t
  23.7 0.0 collective-permute-done.low_t
  23.7 0.3 collective-permute-done.3.upp
  24.0 7.7 %collective-permute-done.2.low = bf16[32,16,256]{2,1,0:T(8,128)(2,1)S(1)} collective-permute-done((bf16[32,16,256]{2,1,0:T(8,128)(2,1)S(1)}, bf16[32,16,256]{2,1,0:T(8,128)(2,1)S(1)}, u32[]{:S(2)}, u32[]{:S(2)}) %collective-permute-start.2) | collective-permute-done | bytes 262176 | tf_op jit(solution)/shard_map/ppermute | solution.py:500
  31.7 0.0 copy-done.10
  31.7 0.0 copy-done.11
  31.7 0.0 copy-done.12
  31.7 0.0 slice-start.2
  31.7 0.0 slice-start.3
  31.7 0.0 copy-start.6
  31.7 0.0 copy-start.7
  31.7 5.6 %shard_map.111 = bf16[128,32,128]{2,1,0:T(8,128)(2,1)S(1)} custom-call(s32[224]{0:T(256)S(1)} %get-tuple-element.13.lists, s32[224]{0:T(256)S(1)} %collective-permute-done.low_t, s32[224]{0:T(256)S(1)} %collective-permute-done.1.upp_t, f32[32,16,256]{2,1,0:T(8,128)S(1)} %get-tuple-element.14.own, bf16[32,16,256]{2,1,0:T(8,128)(2,1)S(1)} %collective-permute-done.2.low, ...), custom_call_target="tpu_custom_call" | custom-call | flops 8000000000 | bytes 4194304 | tf_op jit(solution)/shard_map/pallas_call | solution.py:306
  37.4 26.9 %all_to_all.10.data = bf16[128,32,128]{2,1,0:T(8,128)(2,1)S(1)} all-to-all(bf16[128,32,128]{2,1,0:T(8,128)(2,1)S(1)} %shard_map.111), channel_id=1, replica_groups=mesh['dom'=8,'order'=16] {'dom','order'}, dimensions={0} | all-to-all | bytes 2097152 | tf_op jit(solution)/shard_map/all_to_all | solution.py:515
  64.2 0.0 slice-done
  64.2 0.0 slice-done.1
  64.2 0.0 slice-done.2
  64.2 0.0 slice-done.3
  64.3 0.0 copy-done.6
  64.3 0.0 copy-done.7
  64.3 8.5 %shard_map.112 = bf16[128,32,128]{2,1,0:T(8,128)(2,1)S(1)} custom-call(bf16[8,1024,1024]{2,1,0:T(8,128)(2,1)S(1)} %bitcast.3, bf16[128,32,128]{2,1,0:T(8,128)(2,1)S(1)} %all_to_all.10.data, f32[1,1024]{1,0:T(1,128)S(1)} %bitcast.4, f32[1,1024]{1,0:T(1,128)S(1)} %bitcast.5), custom_call_target="tpu_custom_call" | custom-call | flops 11000000512 | bytes 4194304 | tf_op jit(solution)/shard_map/pallas_call | solution.py:361
  72.8 23.0 %all_to_all.11.data = bf16[128,32,128]{2,1,0:T(8,128)(2,1)S(1)} all-to-all(bf16[128,32,128]{2,1,0:T(8,128)(2,1)S(1)} %shard_map.112), channel_id=1, replica_groups=mesh['dom'=8,'order'=16] {'dom','order'}, dimensions={0} | all-to-all | bytes 2097152 | tf_op jit(solution)/shard_map/all_to_all | solution.py:517
  95.9 5.1 %shard_map.113 = (f32[32,16,256]{2,1,0:T(8,128)S(1)}, bf16[32,16,256]{2,1,0:T(8,128)(2,1)S(1)}, bf16[32,16,256]{2,1,0:T(8,128)(2,1)S(1)}) custom-call(s32[224]{0:T(256)S(1)} %get-tuple-element.13.lists, s32[224]{0:T(256)S(1)} %collective-permute-done.low_t, s32[224]{0:T(256)S(1)} %collective-permute-done.1.upp_t, bf16[128,32,128]{2,1,0:T(8,128)(2,1)S(1)} %all_to_all.11.data, ...), custom_call_target="tpu_custom_call" | custom-call | flops 7000000000 | bytes 4194304 | tf_op jit(solution)/shard_map/pallas_call | solution.py:422
  101.0 0.5 collective-permute-start.4
  101.5 4.6 %collective-permute-start.5 = (bf16[32,16,256]{2,1,0:T(8,128)(2,1)S(1)}, bf16[32,16,256]{2,1,0:T(8,128)(2,1)S(1)}, u32[]{:S(2)}, u32[]{:S(2)}) collective-permute-start(bf16[32,16,256]{2,1,0:T(8,128)(2,1)S(1)} %get-tuple-element.19), channel_id=1, source_target_pairs={{0,127},{1,0},{2,1},{3,2},{4,3},{5,4},{6,5},{7,6},{8,7},{9,8},{10,... | collective-permute-start | bytes 786440 | tf_op jit(solution)/shard_map/ppermute | solution.py:500
  106.1 1.2 %shard_map.114.own = f32[32,16,256]{2,1,0:T(8,128)S(1)} custom-call(f32[32,16,256]{2,1,0:T(8,128)S(1)} %get-tuple-element.16.values, bf16[32,256,256]{2,1,0:T(8,128)(2,1)S(1)} %get-tuple-element.17.wt), custom_call_target="tpu_custom_call" | custom-call | flops 2000000000 | bytes 4194304 | tf_op jit(solution)/shard_map/pallas_call | solution.py:451
  107.3 6.0 %collective-permute-done.4.low = bf16[32,16,256]{2,1,0:T(8,128)(2,1)S(1)} collective-permute-done((bf16[32,16,256]{2,1,0:T(8,128)(2,1)S(1)}, bf16[32,16,256]{2,1,0:T(8,128)(2,1)S(1)}, u32[]{:S(2)}, u32[]{:S(2)}) %collective-permute-start.4) | collective-permute-done | bytes 262176 | tf_op jit(solution)/shard_map/ppermute | solution.py:500
  113.2 0.0 collective-permute-done.5.upp
  113.2 2.7 %shard_map.115 = f32[64,16,256]{2,1,0:T(8,128)} custom-call(s32[224]{0:T(256)S(1)} %get-tuple-element.13.lists, f32[32,16,256]{2,1,0:T(8,128)S(1)} %shard_map.114.own, bf16[32,16,256]{2,1,0:T(8,128)(2,1)S(1)} %collective-permute-done.4.low, bf16[32,16,256]{2,1,0:T(8,128)(2,1)S(1)} %collective-permute-done.5.upp, bf16[32,256,256]{2,1,0:T(8,128)(2,1)S(1)} %get-tuple-element.20.wt), custom_call_target="tpu_custom_call" | custom-call | flops 4000000000 | bytes 4194304 | tf_op jit(solution)/shard_map/pallas_call | solution.py:485
  (1 shorter events, 0.0 us)
Async XLA Ops:
  0.0 1.2 %copy-start = (f32[64,16,256]{2,1,0:T(8,128)S(1)}, f32[64,16,256]{2,1,0:T(8,128)}, u32[]{:S(2)}) copy-start(f32[64,16,256]{2,1,0:T(8,128)} %ssh.1) | copy-start | bytes 3145732
  1.2 0.9 copy-start.2
  2.2 0.9 copy-start.4
  3.1 0.7 copy-start.8
  3.8 0.7 copy-start.9
  4.4 16.2 %copy-start.1 = (f32[64,16,256]{2,1,0:T(8,128)S(1)}, f32[64,16,256]{2,1,0:T(8,128)}, u32[]{:S(2)}) copy-start(f32[64,16,256]{2,1,0:T(8,128)} %ssh.1) | copy-start | bytes 3145732
  4.4 16.2 %copy-start.3 = (s32[64,4,256]{2,1,0:T(4,128)S(1)}, s32[64,4,256]{2,1,0:T(4,128)}, u32[]{:S(2)}) copy-start(s32[64,4,256]{2,1,0:T(4,128)} %index.1) | copy-start | bytes 786436
  4.4 16.2 %copy-start.5 = (f32[64,4,256]{2,1,0:T(4,128)S(1)}, f32[64,4,256]{2,1,0:T(4,128)}, u32[]{:S(2)}) copy-start(f32[64,4,256]{2,1,0:T(4,128)} %weight.1) | copy-start | bytes 786436
  8.2 15.5 %collective-permute-start.1 = (s32[224]{0:T(256)S(1)}, s32[224]{0:T(256)S(1)}, u32[]{:S(2)}, u32[]{:S(2)}) collective-permute-start(s32[224]{0:T(256)S(1)} %get-tuple-element.13.lists), channel_id=1, source_target_pairs={{0,127},{1,0},{2,1},{3,2},{4,3},{5,4},{6,5},{7,6},{8,7},{9,8},{10,... | collective-permute-start | bytes 2696 | tf_op jit(solution)/shard_map/ppermute | solution.py:500
  15.6 8.1 %collective-permute-start = (s32[224]{0:T(256)S(1)}, s32[224]{0:T(256)S(1)}, u32[]{:S(2)}, u32[]{:S(2)}) collective-permute-start(s32[224]{0:T(256)S(1)} %get-tuple-element.13.lists), channel_id=1, source_target_pairs={{0,1},{1,2},{2,3},{3,4},{4,5},{5,6},{6,7},{7,8},{8,9},{9,10},{10,1... | collective-permute-start | bytes 2696 | tf_op jit(solution)/shard_map/ppermute | solution.py:500
  15.6 16.1 %copy-start.10 = (bf16[256,512]{1,0:T(8,128)(2,1)S(1)}, bf16[256,512]{1,0:T(8,128)(2,1)}, u32[]{:S(2)}) copy-start(bf16[256,512]{1,0:T(8,128)(2,1)} %constant.6.clone.second) | copy-start | bytes 786436
  15.6 16.1 %copy-start.11 = (f32[16,256]{1,0:T(8,128)S(1)}, f32[16,256]{1,0:T(8,128)}, u32[]{:S(2)}) copy-start(f32[16,256]{1,0:T(8,128)} %constant.8.clone.tws) | copy-start | bytes 49156
  15.6 16.1 %copy-start.12 = (f32[16,256]{1,0:T(8,128)S(1)}, f32[16,256]{1,0:T(8,128)}, u32[]{:S(2)}) copy-start(f32[16,256]{1,0:T(8,128)} %constant.7.clone.twc) | copy-start | bytes 49156
  15.6 8.4 %collective-permute-start.3 = (bf16[32,16,256]{2,1,0:T(8,128)(2,1)S(1)}, bf16[32,16,256]{2,1,0:T(8,128)(2,1)S(1)}, u32[]{:S(2)}, u32[]{:S(2)}) collective-permute-start(bf16[32,16,256]{2,1,0:T(8,128)(2,1)S(1)} %get-tuple-element.15), channel_id=1, source_target_pairs={{0,127},{1,0},{2,1},{3,2},{4,3},{5,4},{6,5},{7,6},{8,7},{9,8},{10,... | collective-permute-start | bytes 786440 | tf_op jit(solution)/shard_map/ppermute | solution.py:500
  20.7 11.0 %collective-permute-start.2 = (bf16[32,16,256]{2,1,0:T(8,128)(2,1)S(1)}, bf16[32,16,256]{2,1,0:T(8,128)(2,1)S(1)}, u32[]{:S(2)}, u32[]{:S(2)}) collective-permute-start(bf16[32,16,256]{2,1,0:T(8,128)(2,1)S(1)} %get-tuple-element.15), channel_id=1, source_target_pairs={{0,1},{1,2},{2,3},{3,4},{4,5},{5,6},{6,7},{7,8},{8,9},{9,10},{10,1... | collective-permute-start | bytes 786440 | tf_op jit(solution)/shard_map/ppermute | solution.py:500
  20.7 43.5 %slice-start = ((s8[16777216]{0:T(1024)(128)(4,1)}), s8[4194304]{0:T(1024)(128)(4,1)S(1)}, s32[]{:S(2)}) async-start(s8[16777216]{0:T(1024)(128)(4,1)} %bitcast.2), calls=%async_computation.2 | async-start | bytes 8388608
  20.7 43.5 %slice-start.1 = ((s8[16777216]{0:T(1024)(128)(4,1)}), s8[4194304]{0:T(1024)(128)(4,1)S(1)}, s32[]{:S(2)}) async-start(s8[16777216]{0:T(1024)(128)(4,1)} %bitcast.2), calls=%async_computation.3 | async-start | bytes 8388608
  31.7 32.6 %slice-start.2 = ((s8[16777216]{0:T(1024)(128)(4,1)}), s8[4194304]{0:T(1024)(128)(4,1)S(1)}, s32[]{:S(2)}) async-start(s8[16777216]{0:T(1024)(128)(4,1)} %bitcast.2), calls=%async_computation.4 | async-start | bytes 8388608
  31.7 32.6 %slice-start.3 = ((s8[16777216]{0:T(1024)(128)(4,1)}), s8[4194304]{0:T(1024)(128)(4,1)S(1)}, s32[]{:S(2)}) async-start(s8[16777216]{0:T(1024)(128)(4,1)} %bitcast.2), calls=%async_computation.5 | async-start | bytes 8388608
  31.7 32.6 %copy-start.6 = (f32[1024]{0:T(1024)S(1)}, f32[1024]{0:T(1024)}, u32[]{:S(2)}) copy-start(f32[1024]{0:T(1024)} %param.16) | copy-start | bytes 12292
  31.7 32.6 %copy-start.7 = (f32[1024]{0:T(1024)S(1)}, f32[1024]{0:T(1024)}, u32[]{:S(2)}) copy-start(f32[1024]{0:T(1024)} %param.17) | copy-start | bytes 12292
  101.0 12.3 %collective-permute-start.4 = (bf16[32,16,256]{2,1,0:T(8,128)(2,1)S(1)}, bf16[32,16,256]{2,1,0:T(8,128)(2,1)S(1)}, u32[]{:S(2)}, u32[]{:S(2)}) collective-permute-start(bf16[32,16,256]{2,1,0:T(8,128)(2,1)S(1)} %get-tuple-element.18), channel_id=1, source_target_pairs={{0,1},{1,2},{2,3},{3,4},{4,5},{5,6},{6,7},{7,8},{8,9},{9,10},{10,1... | collective-permute-start | bytes 786440 | tf_op jit(solution)/shard_map/ppermute | solution.py:500
  101.5 11.7 %collective-permute-start.5 = (bf16[32,16,256]{2,1,0:T(8,128)(2,1)S(1)}, bf16[32,16,256]{2,1,0:T(8,128)(2,1)S(1)}, u32[]{:S(2)}, u32[]{:S(2)}) collective-permute-start(bf16[32,16,256]{2,1,0:T(8,128)(2,1)S(1)} %get-tuple-element.19), channel_id=1, source_target_pairs={{0,127},{1,0},{2,1},{3,2},{4,3},{5,4},{6,5},{7,6},{8,7},{9,8},{10,... | collective-permute-start | bytes 786440 | tf_op jit(solution)/shard_map/ppermute | solution.py:500

commit v3 on v2

--- a/solution.py
+++ b/solution.py
@@ -144,36 +144,37 @@
     lax.fori_loop(0, BLK, step, (jnp.int32(0), jnp.int32(0)), unroll=4)
 
 
-def spread_blocks(first, lists, ssh, index, weight, wt_out, out):
-    base = pl.program_id(0) * STEP
+def cell_matrix(b, lists, index, weight):
     lanes = lax.broadcasted_iota(jnp.int32, (4, BLOCK), 1)
     points = lax.broadcasted_iota(jnp.int32, (BLOCK, BLOCK), 0).astype(F32).astype(BF16)
     zero = jnp.bfloat16(0)
-    for i in range(STEP):
-        b = lists[first + base + i]
-        idx = index[b].astype(F32).astype(BF16)
-        wgt = jnp.where(lanes < lists[COUNT + b], weight[b], 0.0).astype(BF16)
-        mat = jnp.where(points == idx[0:1], wgt[0:1], zero)
-        for k in range(1, 4):
-            mat = mat + jnp.where(points == idx[k : k + 1], wgt[k : k + 1], zero)
-        wt_out[i] = mat
-        heights = ssh[b]
-        hi = heights.astype(BF16)
-        lo = (heights - hi.astype(F32)).astype(BF16)
-        both = lax.dot_general(
-            jnp.concatenate([hi, lo], axis=0),
-            mat,
-            (((1,), (1,)), ((), ())),
-            preferred_element_type=F32,
-        )
-        out[i] = (both[:NF] + both[NF:]).astype(out.dtype)
+    idx = index[b].astype(F32).astype(BF16)
+    wgt = jnp.where(lanes < lists[COUNT + b], weight[b], 0.0).astype(BF16)
+    mat = jnp.where(points == idx[0:1], wgt[0:1], zero)
+    for k in range(1, 4):
+        mat = mat + jnp.where(points == idx[k : k + 1], wgt[k : k + 1], zero)
+    return mat
+
+
+def spread_block(heights, mat):
+    hi = heights.astype(BF16)
+    lo = (heights - hi.astype(F32)).astype(BF16)
+    both = lax.dot_general(
+        jnp.concatenate([hi, lo], axis=0),
+        mat,
+        (((1,), (1,)), ((), ())),
+        preferred_element_type=F32,
+    )
+    return both[:NF] + both[NF:]
 
 
 def other_kernel(
     tile_hbm, count_hbm, ssh_hbm, index_hbm, weight_hbm, lists, wt_out, out,
     tile_ref, count_ref, ssh, index, weight, sems
 ):
-    @pl.when(pl.program_id(0) == 0)
+    step = pl.program_id(0)
+
+    @pl.when(step == 0)
     def _():
         pairs = [
             (tile_hbm, tile_ref),
@@ -188,85 +189,107 @@
         copies[0].wait()
         copies[1].wait()
         make_lists(tile_ref, count_ref, lists)
+        me = lax.axis_index(AXES)
+        lane = lax.broadcasted_iota(jnp.int32, (NF, BLOCK), 1)
+        row = lax.broadcasted_iota(jnp.int32, (NF, BLOCK), 0)
+        codes = jnp.zeros((NF, BLOCK), jnp.int32)
+        for i in range(HALF_BLK):
+            tile = lists[OTH_T + i]
+            code = jnp.where(row == 0, tile & 255, lax.shift_right_logical(tile, 8) - me)
+            codes = jnp.where((lane == i) & (row < 2), code, codes)
+        out[HALF_BLK] = codes.astype(F32).astype(BF16)
         for copy in copies[2:]:
             copy.wait()
 
-    spread_blocks(OTH_B, lists, ssh, index, weight, wt_out, out)
-
-
-def own_spread_kernel(lists, ssh, index, weight, wt_out, out):
-    spread_blocks(OWN_B, lists, ssh, index, weight, wt_out, out)
-
-
-def whole(shape):
-    return pl.BlockSpec(shape, lambda i: (0,) * len(shape))
-
-
-def spread_half(scalars, ssh, index, weight, dtype, with_lists):
-    shapes = (
-        jax.ShapeDtypeStruct((HALF_BLK, BLOCK, BLOCK), BF16),
-        jax.ShapeDtypeStruct((HALF_BLK, NF, BLOCK), dtype),
-    )
-    specs = (
-        pl.BlockSpec((STEP, BLOCK, BLOCK), lambda i: (i, 0, 0)),
-        pl.BlockSpec((STEP, NF, BLOCK), lambda i: (i, 0, 0)),
-    )
-    if with_lists:
-        shapes = (jax.ShapeDtypeStruct((LISTS,), jnp.int32),) + shapes
-        specs = (smem_spec(),) + specs
-        in_specs = [pl.BlockSpec(memory_space=pltpu.HBM)] * 5
-        scratch = [
+    for i in range(STEP):
+        b = lists[OTH_B + step * STEP + i]
+        mat = cell_matrix(b, lists, index, weight)
+        wt_out[i] = mat
+        out[step * STEP + i] = spread_block(ssh[b], mat).astype(BF16)
+
+
+def spread_other(block_tile, cell_count, ssh, index, weight):
+    return pl.pallas_call(
+        other_kernel,
+        grid=(HALF_BLK // STEP,),
+        out_shape=(
+            jax.ShapeDtypeStruct((LISTS,), jnp.int32),
+            jax.ShapeDtypeStruct((HALF_BLK, BLOCK, BLOCK), BF16),
+            jax.ShapeDtypeStruct((HALF_BLK + 1, NF, BLOCK), BF16),
+        ),
+        in_specs=[pl.BlockSpec(memory_space=pltpu.HBM)] * 5,
+        out_specs=(
+            smem_spec(),
+            pl.BlockSpec((STEP, BLOCK, BLOCK), lambda i: (i, 0, 0)),
+            pl.BlockSpec((HALF_BLK + 1, NF, BLOCK), lambda i: (0, 0, 0)),
+        ),
+        scratch_shapes=[
             SMEM((BLK,), jnp.int32),
             SMEM((BLK,), jnp.int32),
             VMEM((BLK, NF, BLOCK), F32),
             VMEM((BLK, 4, BLOCK), jnp.int32),
             VMEM((BLK, 4, BLOCK), F32),
             pltpu.SemaphoreType.DMA((5,)),
-        ]
-    else:
-        in_specs = [
-            smem_spec(),
-            whole((BLK, NF, BLOCK)),
-            whole((BLK, 4, BLOCK)),
-            whole((BLK, 4, BLOCK)),
-        ]
-        scratch = []
+        ],
+        compiler_params=params(60),
+        cost_estimate=cost(5),
+    )(block_tile, cell_count, ssh, index, weight)
+
+
+def own_kernel(lists, ssh, index, weight, wt_out, grid):
+    flip = jnp.where(lax.axis_index(AXES) >= DEVS // 2, 0xF0, 0)
+    grid[...] = jnp.zeros_like(grid)
+
+    def step(j, carry):
+        for i in range(STEP):
+            slot = j * STEP + i
+            b = lists[OWN_B + slot]
+            mat = cell_matrix(b, lists, index, weight)
+            wt_out[slot] = mat
+            tile = (lists[OWN_T + slot] & 255) ^ flip
+            grid[tile] = grid[tile] + spread_block(ssh[b], mat)
+        return carry
+
+    lax.fori_loop(0, HALF_BLK // STEP, step, 0)
+
+
+def spread_own(lists, ssh, index, weight):
     return pl.pallas_call(
-        other_kernel if with_lists else own_spread_kernel,
-        grid=(HALF_BLK // STEP,),
-        out_shape=shapes,
-        in_specs=in_specs,
-        out_specs=specs,
-        scratch_shapes=scratch,
-        compiler_params=params(14),
+        own_kernel,
+        out_shape=(
+            jax.ShapeDtypeStruct((HALF_BLK, BLOCK, BLOCK), BF16),
+            jax.ShapeDtypeStruct((TILES + 1, NF, BLOCK), F32),
+        ),
+        in_specs=[smem_spec()] + [plain_spec()] * 3,
+        out_specs=(vmem_spec(),) * 2,
+        compiler_params=params(8),
         cost_estimate=cost(5),
-    )(*scalars, ssh, index, weight)
-
-
-def forward_kernel(lists, low_t, upp_t, own, low, upp, second, twc, tws, out, grid, mid, wide):
+    )(lists, ssh, index, weight)
+
+
+def forward_kernel(
+    start_grid, far, near, second, twc, tws, out, spots, grid, mid, wide, codes, sem
+):
+    del start_grid
     me = lax.axis_index(AXES)
     flip = jnp.where(me >= DEVS // 2, 0xF0, 0)
-    grid[...] = jnp.zeros_like(grid)
-
-    def add_own(i, carry):
-        tile = (lists[OWN_T + i] & 255) ^ flip
-        grid[tile] = grid[tile] + own[i]
+    rows = []
+    from_below = jnp.where((me & 1) == 0, 1, -1)
+    for values, direction in ((far, from_below), (near, -from_below)):
+        code = values[HALF_BLK].astype(F32).astype(jnp.int32)
+        rows.append(jnp.where(code[1:2] == direction, code[0:1] ^ flip, TILES))
+    codes[0:2] = jnp.concatenate(rows, axis=0)[:, 0:128]
+    copy = pltpu.make_async_copy(codes, spots, sem)
+    copy.start()
+    copy.wait()
+
+    def add_other(i, carry):
+        for side, values in enumerate((far, near)):
+            spot = spots[side, i]
+            grid[spot] = grid[spot] + values[i].astype(F32)
         return carry
 
-    lax.fori_loop(0, HALF_BLK, add_own, 0, unroll=4)
-
-    def add_other(tiles, values):
-        def body(i, carry):
-            tile = tiles[OTH_T + i]
-            mine = lax.shift_right_logical(tile, 8) == me
-            spot = jnp.where(mine, (tile & 255) ^ flip, TILES)
-            grid[spot] = grid[spot] + values[i].astype(F32)
-            return carry
-
-        lax.fori_loop(0, HALF_BLK, body, 0, unroll=4)
-
-    add_other(low_t, low)
-    add_other(upp_t, upp)
+    lax.fori_loop(0, HALF_BLK, add_other, 0, unroll=4)
 
     def circle(r, carry):
         for h in range(2):
@@ -302,20 +325,27 @@
     out[...] = wide[...].astype(BF16).reshape(out.shape)
 
 
-def forward(lists, low_t, upp_t, own, low, upp, tables):
-    return pl.pallas_call(
+def forward(grid, far, near, tables):
+    fourier, spots, _ = pl.pallas_call(
         forward_kernel,
-        out_shape=jax.ShapeDtypeStruct((DEVS, 32, 128), BF16),
-        in_specs=[smem_spec()] * 3 + [vmem_spec()] * 3 + [plain_spec()] * 3,
-        out_specs=vmem_spec(),
+        out_shape=(
+            jax.ShapeDtypeStruct((DEVS, 32, 128), BF16),
+            jax.ShapeDtypeStruct((8, 128), jnp.int32),
+            jax.ShapeDtypeStruct((TILES + 1, NF, BLOCK), F32),
+        ),
+        in_specs=[vmem_spec()] * 3 + [plain_spec()] * 3,
+        out_specs=(vmem_spec(), smem_spec(), vmem_spec()),
         scratch_shapes=[
-            VMEM((TILES + 1, NF, BLOCK), F32),
             VMEM((LAT, RADIX * NF, 2 * BLOCK), BF16),
             VMEM((DEVS * 32, 128), F32),
+            VMEM((8, 128), jnp.int32),
+            pltpu.SemaphoreType.DMA,
         ],
-        compiler_params=params(18),
+        input_output_aliases={0: 2},
+        compiler_params=params(14),
         cost_estimate=cost(8),
-    )(lists, low_t, upp_t, own, low, upp, tables["second"], tables["twc"], tables["tws"])
+    )(grid, far, near, tables["second"], tables["twc"], tables["tws"])
+    return fourier, spots
 
 
 def legendre_kernel(table, data, gauss, love, out, ins, outs):
@@ -370,7 +400,7 @@
 
 
 def inverse_kernel(
-    lists, low_t, upp_t, data, second, twc, tws, own, low, upp, wide, tiles, waves
+    lists, spots, data, second, twc, tws, own, far, near, wide, tiles, waves
 ):
     me = lax.axis_index(AXES)
     flip = jnp.where(me >= DEVS // 2, 0xF0, 0)
@@ -411,14 +441,14 @@
 
     def gather(i, carry):
         own[i] = tiles[(lists[OWN_T + i] & 255) ^ flip]
-        low[i] = tiles[(low_t[OTH_T + i] & 255) ^ flip].astype(BF16)
-        upp[i] = tiles[(upp_t[OTH_T + i] & 255) ^ flip].astype(BF16)
+        far[i] = tiles[spots[0, i] & 255].astype(BF16)
+        near[i] = tiles[spots[1, i] & 255].astype(BF16)
         return carry
 
     lax.fori_loop(0, HALF_BLK, gather, 0, unroll=4)
 
 
-def inverse(lists, low_t, upp_t, data, tables):
+def inverse(lists, spots, data, tables):
     return pl.pallas_call(
         inverse_kernel,
         out_shape=(
@@ -426,7 +456,7 @@
             jax.ShapeDtypeStruct((HALF_BLK, NF, BLOCK), BF16),
             jax.ShapeDtypeStruct((HALF_BLK, NF, BLOCK), BF16),
         ),
-        in_specs=[smem_spec()] * 3 + [vmem_spec()] + [plain_spec()] * 3,
+        in_specs=[smem_spec()] * 2 + [vmem_spec()] + [plain_spec()] * 3,
         out_specs=(vmem_spec(),) * 3,
         scratch_shapes=[
             VMEM((DEVS * 32, 128), F32),
@@ -435,11 +465,11 @@
         ],
         compiler_params=params(20),
         cost_estimate=cost(7),
-    )(lists, low_t, upp_t, data, tables["second"], tables["twc"], tables["tws"])
-
-
-def own_kernel(values, wt, out):
-    for i in range(STEP):
+    )(lists, spots, data, tables["second"], tables["twc"], tables["tws"])
+
+
+def own_cells_kernel(values, wt, out):
+    for i in range(HALF_BLK):
         val = values[i]
         hi = val.astype(BF16)
         lo = (val - hi.astype(F32)).astype(BF16)
@@ -449,77 +479,73 @@
 
 def own_cells(values, wt):
     return pl.pallas_call(
-        own_kernel,
-        grid=(HALF_BLK // STEP,),
+        own_cells_kernel,
         out_shape=jax.ShapeDtypeStruct((HALF_BLK, NF, BLOCK), F32),
-        in_specs=[
-            pl.BlockSpec((STEP, NF, BLOCK), lambda i: (i, 0, 0)),
-            pl.BlockSpec((STEP, BLOCK, BLOCK), lambda i: (i, 0, 0)),
-        ],
-        out_specs=pl.BlockSpec((STEP, NF, BLOCK), lambda i: (i, 0, 0)),
-        compiler_params=params(8),
+        in_specs=[vmem_spec()] * 2,
+        out_specs=vmem_spec(),
+        compiler_params=params(6),
         cost_estimate=cost(2),
     )(values, wt)
 
 
-def cells_kernel(lists, own, low, upp, wt, out):
+def cells_kernel(lists, own, far, near, wt, out, res, sems):
     me = lax.axis_index(AXES)
-    step_id = pl.program_id(0)
-
-    @pl.when(step_id == 0)
-    def _():
-        def copy(i, carry):
-            out[lists[OWN_B + i]] = own[i]
-            return carry
-
-        lax.fori_loop(0, HALF_BLK, copy, 0, unroll=2)
-
-    for i in range(STEP):
-        slot = step_id * STEP + i
-        above = lax.shift_right_logical(lists[OTH_T + slot], 8) > me
-        val = jnp.where(above, upp[slot], low[slot])
-        out[lists[OTH_B + slot]] = jnp.dot(val, wt[i], preferred_element_type=F32)
-
-
-def all_cells(lists, own, low, upp, wt):
+    odd = (me & 1) == 1
+    own_copies = [
+        pltpu.make_async_copy(own.at[i], out.at[lists[OWN_B + i]], sems.at[i])
+        for i in range(HALF_BLK)
+    ]
+    for copy in own_copies:
+        copy.start()
+    copies = []
+    for i in range(HALF_BLK):
+        above = lax.shift_right_logical(lists[OTH_T + i], 8) > me
+        val = jnp.where(above == odd, far[i], near[i])
+        res[i] = jnp.dot(val, wt[i], preferred_element_type=F32)
+        copy = pltpu.make_async_copy(
+            res.at[i], out.at[lists[OTH_B + i]], sems.at[HALF_BLK + i]
+        )
+        copy.start()
+        copies.append(copy)
+    for copy in own_copies + copies:
+        copy.wait()
+
+
+def all_cells(lists, own, far, near, wt):
     return pl.pallas_call(
         cells_kernel,
-        grid=(HALF_BLK // STEP,),
         out_shape=jax.ShapeDtypeStruct((BLK, NF, BLOCK), F32),
-        in_specs=[smem_spec()]
-        + [vmem_spec()] * 3
-        + [pl.BlockSpec((STEP, BLOCK, BLOCK), lambda i: (i, 0, 0))],
-        out_specs=pl.BlockSpec((BLK, NF, BLOCK), lambda i: (0, 0, 0)),
+        in_specs=[smem_spec()] + [vmem_spec()] * 3 + [plain_spec()],
+        out_specs=pl.BlockSpec(memory_space=pltpu.HBM),
+        scratch_shapes=[VMEM((HALF_BLK, NF, BLOCK), F32), pltpu.SemaphoreType.DMA((BLK,))],
         compiler_params=params(8),
         cost_estimate=cost(4),
-    )(lists, own, low, upp, wt)
-
-
-def shift(value, steps):
-    pairs = [(source, (source + steps) % DEVS) for source in range(DEVS)]
+    )(lists, own, far, near, wt)
+
+
+def swap(value, first):
+    pairs = []
+    for i in range(first, DEVS - 1, 2):
+        pairs += [(i, i + 1), (i + 1, i)]
     return lax.ppermute(value, AXES, pairs)
 
 
 def on_device(
     tables, ssh, cell_count, remap_index, remap_weight, block_tile, gauss_weight, love, legendre
 ):
-    lists, wt_oth, oth = spread_half(
-        (block_tile, cell_count), ssh, remap_index, remap_weight, BF16, True
-    )
-    low_t = shift(lists, 1)
-    upp_t = shift(lists, -1)
-    low = shift(oth, 1)
-    upp = shift(oth, -1)
-    wt_own, own = spread_half((lists,), ssh, remap_index, remap_weight, F32, False)
-    fourier = forward(lists, low_t, upp_t, own, low, upp, tables)
+    lists, wt_oth, oth = spread_other(block_tile, cell_count, ssh, remap_index, remap_weight)
+    far = swap(oth, 1)
+    near = swap(oth, 0)
+    wt_own, grid = spread_own(lists, ssh, remap_index, remap_weight)
+    fourier, spots = forward(grid, far, near, tables)
     by_order = lax.all_to_all(fourier, AXES, split_axis=0, concat_axis=0, tiled=True)
     synth = legendre_both(legendre, by_order, gauss_weight, love)
     by_lat = lax.all_to_all(synth, AXES, split_axis=0, concat_axis=0, tiled=True)
-    own_v, low_v, upp_v = inverse(lists, low_t, upp_t, by_lat, tables)
-    from_low = shift(upp_v, 1)
-    from_upp = shift(low_v, -1)
+    own_v, far_v, near_v = inverse(lists, spots, by_lat, tables)
+    from_far = swap(far_v, 1)
+    from_near = swap(near_v, 0)
     own_cell = own_cells(own_v, wt_own)
-    return all_cells(lists, own_cell, from_low, from_upp, wt_oth)
+    return all_cells(lists, own_cell, from_far, from_near, wt_oth)
 
 
 def solution(mesh):

time: 116 us -> 109 us (0.940)
  local copies, waits for them, and re-layouts: 4.49 us -> 0.73 us
  starting transfers between devices: 17.6 us -> 14.4 us
  waiting for transfers between devices: 13.9 us -> 11.9 us
  blocking collectives: 49.9 us -> 51.3 us
    unnamed x34 -> x28, local copies, waits for them, and re-layouts: 4.49 us -> 0.73 us
    ppermute x6 -> x4, starting transfers between devices: 17.6 us -> 14.4 us  [swap(): return lax.ppermute(value, AXES, pairs)]
    ppermute x6 -> x4, waiting for transfers between devices: 13.9 us -> 11.9 us  [swap(): return lax.ppermute(value, AXES, pairs)]
    all_to_all x1, blocking collectives: 26.9 us -> 28.2 us  [on_device(): lax.all_to_all(fourier, AXES, split_axis=0, concat_axis=0, tiled=True)]
  transfers between devices with their start and end apart: 6 -> 4, of which waited for: 3 -> 2; matrix products, arithmetic and copies ran while one was open for 0% -> 0% of each run, Pallas kernels for 4% -> 4%
where the time goes in v3:
time: 109 us
  blocking collectives  51.3 us (47%)
  Pallas kernels  30.4 us (28%)
  starting transfers between devices  14.4 us (13%)
  waiting for transfers between devices  11.9 us (11%)
    all_to_all x1, blocking collectives, on_device(): lax.all_to_all(fourier, AXES, split_axis=0, concat_axis=0, tiled=True)  28.2 us
    all_to_all x1, blocking collectives, on_device(): lax.all_to_all(synth, AXES, split_axis=0, concat_axis=0, tiled=True)  23 us
    ppermute x4, starting transfers between devices, swap(): return lax.ppermute(value, AXES, pairs)  14.4 us
    ppermute x4, waiting for transfers between devices, swap(): return lax.ppermute(value, AXES, pairs)  11.9 us
    pallas_call x1, Pallas kernels, legendre_both(): pl.pallas_call(legendre_kernel, out_shape=jax.ShapeDtypeStruct((DEVS, 32,...  8.53 us
    pallas_call x1, Pallas kernels, spread_other(): pl.pallas_call(other_kernel, grid=(HALF_BLK // STEP,), out_shape=(jax.Sha...  5.23 us
    pallas_call x1, Pallas kernels, forward(): pl.pallas_call(forward_kernel, out_shape=(jax.ShapeDtypeStruct((DEVS, 32,...  5.2 us
    pallas_call x1, Pallas kernels, inverse(): pl.pallas_call(inverse_kernel, out_shape=(jax.ShapeDtypeStruct((HALF_BLK,...  5.01 us
  transfers between devices with their start and end apart: 4, of which 2 were waited for; matrix products, arithmetic and copies ran while one was open for 0% of the time, Pallas kernels for 4%

profile of v3, /device:TPU:1, one launch (start us, length us, event | category | flops | bytes accessed | tf_op | source)
XLA Modules:
  0.0 109.1 jit_solution(16872409469812801354)
XLA Ops:
  0.0 0.0 copy-start.2
  0.0 0.0 copy-start.1
  0.0 0.0 copy-start
  0.0 5.2 %shard_map.109 = (s32[224]{0:T(256)}, bf16[32,256,256]{2,1,0:T(8,128)(2,1)}, bf16[33,16,256]{2,1,0:T(8,128)(2,1)}) custom-call(s32[64]{0:T(128)} %tile_hbm.1, s32[64]{0:T(128)} %count_hbm.1, f32[64,16,256]{2,1,0:T(8,128)} %ssh.1, s32[64,4,256]{2,1,0:T(4,128)} %index.1, f32[64,4,256]{2,1,0:T(4,128)} %weight.1), custom_call_target="tpu_custom_call" | custom-call | flops 5000000000 | bytes 4194304 | tf_op jit(solution)/shard_map/pallas_call | solution.py:212
  5.2 2.1 %collective-permute-start.1 = (bf16[33,16,256]{2,1,0:T(8,128)(2,1)}, bf16[33,16,256]{2,1,0:T(8,128)(2,1)S(1)}, u32[]{:S(2)}, u32[]{:S(2)}) collective-permute-start(bf16[33,16,256]{2,1,0:T(8,128)(2,1)} %get-tuple-element.17), channel_id=1, source_target_pairs={{0,1},{1,0},{2,3},{3,2},{4,5},{5,4},{6,7},{7,6},{8,9},{9,8},{10,11... | collective-permute-start | bytes 811016 | tf_op jit(solution)/shard_map/ppermute | solution.py:530
  7.4 8.0 %collective-permute-start = (bf16[33,16,256]{2,1,0:T(8,128)(2,1)}, bf16[33,16,256]{2,1,0:T(8,128)(2,1)S(1)}, u32[]{:S(2)}, u32[]{:S(2)}) collective-permute-start(bf16[33,16,256]{2,1,0:T(8,128)(2,1)} %get-tuple-element.17), channel_id=1, source_target_pairs={{1,2},{2,1},{3,4},{4,3},{5,6},{6,5},{7,8},{8,7},{9,10},{10,9},{11,... | collective-permute-start | bytes 811016 | tf_op jit(solution)/shard_map/ppermute | solution.py:530
  15.4 0.0 copy-done.2
  15.4 0.0 copy-done.1
  15.4 0.0 copy-done
  15.4 0.0 copy-start.9
  15.4 0.7 copy-done.9
  16.1 0.0 copy-start.5
  16.1 0.0 copy-start.6
  16.1 0.0 copy-start.7
  16.1 0.0 slice-start
  16.1 0.0 slice-start.1
  16.1 3.2 %shard_map.110 = (bf16[32,256,256]{2,1,0:T(8,128)(2,1)S(1)}, f32[257,16,256]{2,1,0:T(8,128)S(1)}) custom-call(s32[224]{0:T(256)S(1)} %copy-done.9, f32[64,16,256]{2,1,0:T(8,128)S(1)} %copy-done, s32[64,4,256]{2,1,0:T(4,128)S(1)} %copy-done.1, f32[64,4,256]{2,1,0:T(4,128)S(1)} %copy-done.2), custom_call_target="tpu_custom_call" | custom-call | flops 5000000000 | bytes 4194304 | tf_op jit(solution)/shard_map/pallas_call | solution.py:257
  19.4 0.0 collective-permute-done.1.near
  19.4 3.1 %collective-permute-done.far = bf16[33,16,256]{2,1,0:T(8,128)(2,1)S(1)} collective-permute-done((bf16[33,16,256]{2,1,0:T(8,128)(2,1)}, bf16[33,16,256]{2,1,0:T(8,128)(2,1)S(1)}, u32[]{:S(2)}, u32[]{:S(2)}) %collective-permute-start) | collective-permute-done | bytes 270368 | tf_op jit(solution)/shard_map/ppermute | solution.py:530
  22.4 0.0 copy-done.5
  22.4 0.0 copy-done.6
  22.4 0.0 copy-done.7
  22.4 0.0 slice-start.2
  22.5 0.0 slice-start.3
  22.5 0.0 copy-start.3
  22.5 0.0 copy-start.4
  22.5 5.2 %shard_map.111 = (bf16[128,32,128]{2,1,0:T(8,128)(2,1)S(1)}, s32[8,128]{1,0:T(8,128)S(1)}, f32[257,16,256]{2,1,0:T(8,128)S(1)}) custom-call(f32[257,16,256]{2,1,0:T(8,128)S(1)} %get-tuple-element.16.start_grid, bf16[33,16,256]{2,1,0:T(8,128)(2,1)S(1)} %collective-permute-done.far, ...), custom_call_target="tpu_custom_call", output_to_operand_aliasing={{2}: (0, {})} | custom-call | flops 8000000000 | bytes 4194304 | tf_op jit(solution)/shard_map/pallas_call | solution.py:329
  27.7 28.2 %all_to_all.10.data = bf16[128,32,128]{2,1,0:T(8,128)(2,1)S(1)} all-to-all(bf16[128,32,128]{2,1,0:T(8,128)(2,1)S(1)} %get-tuple-element.19), channel_id=1, replica_groups=mesh['dom'=8,'order'=16] {'dom','order'}, dimensions={0} | all-to-all | bytes 2097152 | tf_op jit(solution)/shard_map/all_to_all | solution.py:541
  55.9 0.0 slice-done
  55.9 0.0 slice-done.1
  55.9 0.0 slice-done.2
  55.9 0.0 slice-done.3
  56.0 0.0 copy-done.3
  56.0 0.0 copy-done.4
  56.0 8.5 %shard_map.112 = bf16[128,32,128]{2,1,0:T(8,128)(2,1)S(1)} custom-call(bf16[8,1024,1024]{2,1,0:T(8,128)(2,1)S(1)} %bitcast.3, bf16[128,32,128]{2,1,0:T(8,128)(2,1)S(1)} %all_to_all.10.data, f32[1,1024]{1,0:T(1,128)S(1)} %bitcast.4, f32[1,1024]{1,0:T(1,128)S(1)} %bitcast.5), custom_call_target="tpu_custom_call" | custom-call | flops 11000000512 | bytes 4194304 | tf_op jit(solution)/shard_map/pallas_call | solution.py:391
  64.5 23.0 %all_to_all.11.data = bf16[128,32,128]{2,1,0:T(8,128)(2,1)S(1)} all-to-all(bf16[128,32,128]{2,1,0:T(8,128)(2,1)S(1)} %shard_map.112), channel_id=1, replica_groups=mesh['dom'=8,'order'=16] {'dom','order'}, dimensions={0} | all-to-all | bytes 2097152 | tf_op jit(solution)/shard_map/all_to_all | solution.py:543
  87.6 5.0 %shard_map.113 = (f32[32,16,256]{2,1,0:T(8,128)S(1)}, bf16[32,16,256]{2,1,0:T(8,128)(2,1)S(1)}, bf16[32,16,256]{2,1,0:T(8,128)(2,1)S(1)}) custom-call(s32[224]{0:T(256)S(1)} %copy-done.9, s32[8,128]{1,0:T(8,128)S(1)} %get-tuple-element.18.spots, bf16[128,32,128]{2,1,0:T(8,128)(2,1)S(1)} %all_to_all.11.data, bf16[256,512]{1,0:T(8,128)(2,1)S(1)} %copy-done.5, ...), custom_call_target="tpu_custom_call" | custom-call | flops 7000000000 | bytes 4194304 | tf_op jit(solution)/shard_map/pallas_call | solution.py:452
  92.6 0.0 copy-start.8
  92.6 4.2 %collective-permute-start.2 = (bf16[32,16,256]{2,1,0:T(8,128)(2,1)S(1)}, bf16[32,16,256]{2,1,0:T(8,128)(2,1)S(1)}, u32[]{:S(2)}, u32[]{:S(2)}) collective-permute-start(bf16[32,16,256]{2,1,0:T(8,128)(2,1)S(1)} %get-tuple-element.22), channel_id=1, source_target_pairs={{1,2},{2,1},{3,4},{4,3},{5,6},{6,5},{7,8},{8,7},{9,10},{10,9},{11,... | collective-permute-start | bytes 786440 | tf_op jit(solution)/shard_map/ppermute | solution.py:530
  96.8 0.1 collective-permute-start.3
  96.9 0.8 shard_map.114.own
  97.7 8.8 %collective-permute-done.2.far = bf16[32,16,256]{2,1,0:T(8,128)(2,1)S(1)} collective-permute-done((bf16[32,16,256]{2,1,0:T(8,128)(2,1)S(1)}, bf16[32,16,256]{2,1,0:T(8,128)(2,1)S(1)}, u32[]{:S(2)}, u32[]{:S(2)}) %collective-permute-start.2) | collective-permute-done | bytes 262176 | tf_op jit(solution)/shard_map/ppermute | solution.py:530
  106.5 0.0 collective-permute-done.3.near
  106.5 0.0 copy-done.8
  106.5 2.4 %shard_map.115 = f32[64,16,256]{2,1,0:T(8,128)} custom-call(s32[224]{0:T(256)S(1)} %copy-done.9, f32[32,16,256]{2,1,0:T(8,128)S(1)} %shard_map.114.own, bf16[32,16,256]{2,1,0:T(8,128)(2,1)S(1)} %collective-permute-done.2.far, bf16[32,16,256]{2,1,0:T(8,128)(2,1)S(1)} %collective-permute-done.3.near, bf16[32,256,256]{2,1,0:T(8,128)(2,1)S(1)} %copy-done.8), custom_call_target="tpu_custom_call" | custom-call | flops 4000000000 | bytes 4194304 | tf_op jit(solution)/shard_map/pallas_call | solution.py:515
  (1 shorter events, 0.0 us)
Async XLA Ops:
  0.0 15.4 %copy-start.2 = (f32[64,4,256]{2,1,0:T(4,128)S(1)}, f32[64,4,256]{2,1,0:T(4,128)}, u32[]{:S(2)}) copy-start(f32[64,4,256]{2,1,0:T(4,128)} %weight.1) | copy-start | bytes 786436
  0.0 15.4 %copy-start.1 = (s32[64,4,256]{2,1,0:T(4,128)S(1)}, s32[64,4,256]{2,1,0:T(4,128)}, u32[]{:S(2)}) copy-start(s32[64,4,256]{2,1,0:T(4,128)} %index.1) | copy-start | bytes 786436
  0.0 15.4 %copy-start = (f32[64,16,256]{2,1,0:T(8,128)S(1)}, f32[64,16,256]{2,1,0:T(8,128)}, u32[]{:S(2)}) copy-start(f32[64,16,256]{2,1,0:T(8,128)} %ssh.1) | copy-start | bytes 3145732
  5.2 14.1 %collective-permute-start.1 = (bf16[33,16,256]{2,1,0:T(8,128)(2,1)}, bf16[33,16,256]{2,1,0:T(8,128)(2,1)S(1)}, u32[]{:S(2)}, u32[]{:S(2)}) collective-permute-start(bf16[33,16,256]{2,1,0:T(8,128)(2,1)} %get-tuple-element.17), channel_id=1, source_target_pairs={{0,1},{1,0},{2,3},{3,2},{4,5},{5,4},{6,7},{7,6},{8,9},{9,8},{10,11... | collective-permute-start | bytes 811016 | tf_op jit(solution)/shard_map/ppermute | solution.py:530
  7.4 15.1 %collective-permute-start = (bf16[33,16,256]{2,1,0:T(8,128)(2,1)}, bf16[33,16,256]{2,1,0:T(8,128)(2,1)S(1)}, u32[]{:S(2)}, u32[]{:S(2)}) collective-permute-start(bf16[33,16,256]{2,1,0:T(8,128)(2,1)} %get-tuple-element.17), channel_id=1, source_target_pairs={{1,2},{2,1},{3,4},{4,3},{5,6},{6,5},{7,8},{8,7},{9,10},{10,9},{11,... | collective-permute-start | bytes 811016 | tf_op jit(solution)/shard_map/ppermute | solution.py:530
  15.4 0.7 copy-start.9
  16.1 6.3 %copy-start.5 = (bf16[256,512]{1,0:T(8,128)(2,1)S(1)}, bf16[256,512]{1,0:T(8,128)(2,1)}, u32[]{:S(2)}) copy-start(bf16[256,512]{1,0:T(8,128)(2,1)} %constant.6.clone.second) | copy-start | bytes 786436
  16.1 6.3 %copy-start.6 = (f32[16,256]{1,0:T(8,128)S(1)}, f32[16,256]{1,0:T(8,128)}, u32[]{:S(2)}) copy-start(f32[16,256]{1,0:T(8,128)} %constant.8.clone.tws) | copy-start | bytes 49156
  16.1 6.3 %copy-start.7 = (f32[16,256]{1,0:T(8,128)S(1)}, f32[16,256]{1,0:T(8,128)}, u32[]{:S(2)}) copy-start(f32[16,256]{1,0:T(8,128)} %constant.7.clone.twc) | copy-start | bytes 49156
  16.1 39.8 %slice-start = ((s8[16777216]{0:T(1024)(128)(4,1)}), s8[4194304]{0:T(1024)(128)(4,1)S(1)}, s32[]{:S(2)}) async-start(s8[16777216]{0:T(1024)(128)(4,1)} %bitcast.2), calls=%async_computation.2 | async-start | bytes 8388608
  16.1 39.8 %slice-start.1 = ((s8[16777216]{0:T(1024)(128)(4,1)}), s8[4194304]{0:T(1024)(128)(4,1)S(1)}, s32[]{:S(2)}) async-start(s8[16777216]{0:T(1024)(128)(4,1)} %bitcast.2), calls=%async_computation.3 | async-start | bytes 8388608
  22.4 33.5 %slice-start.2 = ((s8[16777216]{0:T(1024)(128)(4,1)}), s8[4194304]{0:T(1024)(128)(4,1)S(1)}, s32[]{:S(2)}) async-start(s8[16777216]{0:T(1024)(128)(4,1)} %bitcast.2), calls=%async_computation.4 | async-start | bytes 8388608
  22.5 33.5 %slice-start.3 = ((s8[16777216]{0:T(1024)(128)(4,1)}), s8[4194304]{0:T(1024)(128)(4,1)S(1)}, s32[]{:S(2)}) async-start(s8[16777216]{0:T(1024)(128)(4,1)} %bitcast.2), calls=%async_computation.5 | async-start | bytes 8388608
  22.5 33.5 %copy-start.3 = (f32[1024]{0:T(1024)S(1)}, f32[1024]{0:T(1024)}, u32[]{:S(2)}) copy-start(f32[1024]{0:T(1024)} %param.16) | copy-start | bytes 12292
  22.5 33.5 %copy-start.4 = (f32[1024]{0:T(1024)S(1)}, f32[1024]{0:T(1024)}, u32[]{:S(2)}) copy-start(f32[1024]{0:T(1024)} %param.17) | copy-start | bytes 12292
  92.6 13.9 %copy-start.8 = (bf16[32,256,256]{2,1,0:T(8,128)(2,1)S(1)}, bf16[32,256,256]{2,1,0:T(8,128)(2,1)}, u32[]{:S(2)}) copy-start(bf16[32,256,256]{2,1,0:T(8,128)(2,1)} %get-tuple-element.24.wt) | copy-start | bytes 12582916
  92.6 13.9 %collective-permute-start.2 = (bf16[32,16,256]{2,1,0:T(8,128)(2,1)S(1)}, bf16[32,16,256]{2,1,0:T(8,128)(2,1)S(1)}, u32[]{:S(2)}, u32[]{:S(2)}) collective-permute-start(bf16[32,16,256]{2,1,0:T(8,128)(2,1)S(1)} %get-tuple-element.22), channel_id=1, source_target_pairs={{1,2},{2,1},{3,4},{4,3},{5,6},{6,5},{7,8},{8,7},{9,10},{10,9},{11,... | collective-permute-start | bytes 786440 | tf_op jit(solution)/shard_map/ppermute | solution.py:530
  96.8 9.7 %collective-permute-start.3 = (bf16[32,16,256]{2,1,0:T(8,128)(2,1)S(1)}, bf16[32,16,256]{2,1,0:T(8,128)(2,1)S(1)}, u32[]{:S(2)}, u32[]{:S(2)}) collective-permute-start(bf16[32,16,256]{2,1,0:T(8,128)(2,1)S(1)} %get-tuple-element.23), channel_id=1, source_target_pairs={{0,1},{1,0},{2,3},{3,2},{4,5},{5,4},{6,7},{7,6},{8,9},{9,8},{10,11... | collective-permute-start | bytes 786440 | tf_op jit(solution)/shard_map/ppermute | solution.py:530

commit v4 on v3

--- a/solution.py
+++ b/solution.py
@@ -147,12 +147,19 @@
 def cell_matrix(b, lists, index, weight):
     lanes = lax.broadcasted_iota(jnp.int32, (4, BLOCK), 1)
     points = lax.broadcasted_iota(jnp.int32, (BLOCK, BLOCK), 0).astype(F32).astype(BF16)
-    zero = jnp.bfloat16(0)
-    idx = index[b].astype(F32).astype(BF16)
-    wgt = jnp.where(lanes < lists[COUNT + b], weight[b], 0.0).astype(BF16)
-    mat = jnp.where(points == idx[0:1], wgt[0:1], zero)
-    for k in range(1, 4):
-        mat = mat + jnp.where(points == idx[k : k + 1], wgt[k : k + 1], zero)
+    raw = index[b]
+    wgt = jnp.where(lanes < lists[COUNT + b], weight[b], 0.0)
+    sums = []
+    for k in range(4):
+        total = wgt[k : k + 1]
+        for j in range(k + 1, 4):
+            same = raw[j : j + 1] == raw[k : k + 1]
+            total = total + jnp.where(same, wgt[j : j + 1], 0.0)
+        sums.append(total.astype(BF16))
+    idx = raw.astype(F32).astype(BF16)
+    mat = jnp.where(points == idx[3:4], sums[3], jnp.bfloat16(0))
+    for k in (2, 1, 0):
+        mat = jnp.where(points == idx[k : k + 1], sums[k], mat)
     return mat
 
 
@@ -208,6 +215,21 @@
         out[step * STEP + i] = spread_block(ssh[b], mat).astype(BF16)
 
 
+def copy_kernel(source, out):
+    out[...] = source[...]
+
+
+def later_copy(value):
+    return pl.pallas_call(
+        copy_kernel,
+        out_shape=jax.ShapeDtypeStruct(value.shape, value.dtype),
+        in_specs=[vmem_spec()],
+        out_specs=vmem_spec(),
+        compiler_params=params(2),
+        cost_estimate=cost(3),
+    )(value)
+
+
 def spread_other(block_tile, cell_count, ssh, index, weight):
     return pl.pallas_call(
         other_kernel,
@@ -291,7 +313,7 @@
 
     lax.fori_loop(0, HALF_BLK, add_other, 0, unroll=4)
 
-    def circle(r, carry):
+    def circle(r):
         for h in range(2):
             lanes = slice(h * 128, h * 128 + 128)
             re, im = real_dft16([grid[r * RADIX + s, :, lanes] for s in range(RADIX)])
@@ -309,10 +331,8 @@
                 rows = slice(u * NF, u * NF + NF)
                 mid[r, rows, h * 128 : h * 128 + 128] = x.astype(BF16)
                 mid[r, rows, 256 + h * 128 : 256 + h * 128 + 128] = y.astype(BF16)
-        return carry
-
-    lax.fori_loop(0, LAT, circle, 0, unroll=2)
-    for r in range(LAT):
+
+    def waves(r):
         res = lax.dot_general(
             second[...], mid[r], (((1,), (1,)), ((), ())), preferred_element_type=F32
         )
@@ -322,6 +342,12 @@
                 wide[pl.ds(uh * 32 + c * 16 + r, NQ, stride=64), :] = res[
                     c * NQ : c * NQ + NQ, uh * 128 : uh * 128 + 128
                 ]
+
+    circle(0)
+    for r in range(1, LAT):
+        waves(r - 1)
+        circle(r)
+    waves(LAT - 1)
     out[...] = wide[...].astype(BF16).reshape(out.shape)
 
 
@@ -348,7 +374,7 @@
     return fourier, spots
 
 
-def legendre_kernel(table, data, gauss, love, out, ins, outs):
+def legendre_kernel(table, data, gauss, love, out, ins, coefs):
     first_order = lax.axis_index(AXES) * ORD
     gw = gauss[...]
     for c in range(2):
@@ -361,30 +387,31 @@
         ins[:, c * 16 : c * 16 + 16, :] = even.reshape(ORD, NF, NLAT)
         ins[:, 32 + c * 16 : 32 + c * 16 + 16, :] = odd.reshape(ORD, NF, NLAT)
     degree = lax.broadcasted_iota(jnp.int32, (32, NDEG), 1)
-    for k in range(ORD):
-        both = jnp.dot(ins[k], table[k], preferred_element_type=F32)
-        order = first_order + k
-        is_even = ((degree + order) & 1) == 0
-        coef = jnp.where(is_even, both[:32], both[32:])
-        coef = jnp.where(degree < order, 0.0, coef)
-        coef = coef * love[...]
-        parts = jnp.concatenate(
-            [jnp.where(is_even, coef, 0.0), jnp.where(is_even, 0.0, coef)], axis=0
-        ).astype(BF16)
-        res = lax.dot_general(
-            parts, table[k], (((1,), (1,)), ((), ())), preferred_element_type=F32
-        )
-        upper = res[:32] + res[32:]
-        lower = res[:32] - res[32:]
-        for c in range(2):
-            outs[c, 0, k * NF : k * NF + NF, :] = upper[c * 16 : c * 16 + 16]
-            outs[c, 1, k * NF : k * NF + NF, :] = lower[c * 16 : c * 16 + 16]
-    for c in range(2):
-        up = outs[c, 0].T.astype(BF16)
-        dn = outs[c, 1].T.astype(BF16)
+    lane_order = lax.shift_right_logical(lax.broadcasted_iota(jnp.int32, (NLAT, 256), 1), 4) & 3
+    for high in range(2):
+        for low in range(4):
+            k = high * 4 + low
+            both = jnp.dot(ins[k], table[k], preferred_element_type=F32)
+            order = first_order + k
+            is_even = ((degree + order) & 1) == 0
+            coef = jnp.where(is_even, both[:32], both[32:])
+            coef = jnp.where(degree < order, 0.0, coef)
+            coef = coef * love[...]
+            mirror = jnp.where(is_even, coef, -coef)
+            for side, values in enumerate((coef, mirror)):
+                for c in range(2):
+                    spot = side * 128 + c * 64 + low * NF
+                    coefs[high, spot : spot + NF, :] = values[c * NF : c * NF + NF].astype(BF16)
+        columns = coefs[high].T
+        total = jnp.zeros((NLAT, 256), F32)
+        for low in range(4):
+            res = jnp.dot(table[high * 4 + low], columns, preferred_element_type=F32)
+            total = jnp.where(lane_order == low, res, total)
+        total = total.astype(BF16)
         for i in range(64):
-            out[i, c * 16 : c * 16 + 16] = up[i * 16 : i * 16 + 16]
-            out[127 - i, c * 16 : c * 16 + 16] = dn[i * 16 : i * 16 + 16]
+            rows = slice(i * 16, i * 16 + 16)
+            out[i, high * 16 : high * 16 + 16] = total[rows, 0:128]
+            out[127 - i, high * 16 : high * 16 + 16] = total[rows, 128:256]
 
 
 def legendre_both(table, data, gauss, love):
@@ -393,7 +420,7 @@
         out_shape=jax.ShapeDtypeStruct((DEVS, 32, 128), BF16),
         in_specs=[plain_spec(), vmem_spec(), plain_spec(), plain_spec()],
         out_specs=vmem_spec(),
-        scratch_shapes=[VMEM((ORD, 64, NLAT), BF16), VMEM((2, 2, 128, NLAT), F32)],
+        scratch_shapes=[VMEM((ORD, 64, NLAT), BF16), VMEM((2, 256, NDEG), BF16)],
         compiler_params=params(12),
         cost_estimate=cost(11),
     )(table, data, gauss.reshape(1, NLAT), love.reshape(1, NDEG))
@@ -407,18 +434,22 @@
     wide[...] = data[...].astype(F32).reshape(wide.shape)
     row = lax.broadcasted_iota(jnp.int32, (NQ, 128), 0)
     lane = lax.broadcasted_iota(jnp.int32, (NQ, 128), 1)
-    zonal = jnp.where((row == 0) & (lane < NF), 1.0, 2.0)
-    for r in range(LAT):
-        parts = []
-        for c in range(2):
-            left = wide[pl.ds(c * 16 + r, NQ, stride=64), :] * zonal
-            right = wide[pl.ds(32 + c * 16 + r, NQ, stride=64), :] * 2.0
-            parts.append(jnp.concatenate([left, right], axis=1))
+    zonal = jnp.where((row == 0) & ((lane & 63) < NF), 1.0, 2.0)
+    left = lane < 64
+
+    def spread_waves(r):
+        parts = [[], []]
+        for uh in range(2):
+            first = wide[pl.ds(uh * 32 + r, NQ, stride=64), :] * (2.0 if uh else zonal)
+            second_half = wide[pl.ds(uh * 32 + 16 + r, NQ, stride=64), :] * 2.0
+            parts[0].append(jnp.where(left, first, pltpu.roll(second_half, 64, 1)))
+            parts[1].append(jnp.where(left, pltpu.roll(first, 64, 1), second_half))
+        parts = [jnp.concatenate(part, axis=1) for part in parts]
         spectrum = jnp.concatenate(parts, axis=0).T.astype(BF16)
         spectrum = jnp.concatenate([spectrum, spectrum], axis=1)
         waves[r] = jnp.dot(spectrum, second[...], preferred_element_type=F32)
 
-    def circle(r, carry):
+    def circle(r):
         for h in range(2):
             lanes = slice(h * 128, h * 128 + 128)
             re, im = {}, {}
@@ -435,9 +466,12 @@
             values = real_idft16(a, b)
             for s in range(RADIX):
                 tiles[r * RADIX + s, :, lanes] = values[s]
-        return carry
-
-    lax.fori_loop(0, LAT, circle, 0)
+
+    spread_waves(0)
+    for r in range(1, LAT):
+        spread_waves(r)
+        circle(r - 1)
+    circle(LAT - 1)
 
     def gather(i, carry):
         own[i] = tiles[(lists[OWN_T + i] & 255) ^ flip]
@@ -468,46 +502,46 @@
     )(lists, spots, data, tables["second"], tables["twc"], tables["tws"])
 
 
-def own_cells_kernel(values, wt, out):
+def own_cells_kernel(lists, values, wt, out, res, sems):
+    copies = []
     for i in range(HALF_BLK):
         val = values[i]
         hi = val.astype(BF16)
         lo = (val - hi.astype(F32)).astype(BF16)
         both = jnp.dot(jnp.concatenate([hi, lo], axis=0), wt[i], preferred_element_type=F32)
-        out[i] = both[:NF] + both[NF:]
-
-
-def own_cells(values, wt):
+        res[i] = both[:NF] + both[NF:]
+        copy = pltpu.make_async_copy(res.at[i], out.at[lists[OWN_B + i]], sems.at[i])
+        copy.start()
+        copies.append(copy)
+    for copy in copies:
+        copy.wait()
+
+
+def own_cells(lists, values, wt):
     return pl.pallas_call(
         own_cells_kernel,
-        out_shape=jax.ShapeDtypeStruct((HALF_BLK, NF, BLOCK), F32),
-        in_specs=[vmem_spec()] * 2,
-        out_specs=vmem_spec(),
+        out_shape=jax.ShapeDtypeStruct((BLK, NF, BLOCK), F32),
+        in_specs=[smem_spec()] + [vmem_spec()] * 2,
+        out_specs=pl.BlockSpec(memory_space=pltpu.HBM),
+        scratch_shapes=[VMEM((HALF_BLK, NF, BLOCK), F32), pltpu.SemaphoreType.DMA((HALF_BLK,))],
         compiler_params=params(6),
         cost_estimate=cost(2),
-    )(values, wt)
+    )(lists, values, wt)
 
 
 def cells_kernel(lists, own, far, near, wt, out, res, sems):
+    del own
     me = lax.axis_index(AXES)
     odd = (me & 1) == 1
-    own_copies = [
-        pltpu.make_async_copy(own.at[i], out.at[lists[OWN_B + i]], sems.at[i])
-        for i in range(HALF_BLK)
-    ]
-    for copy in own_copies:
-        copy.start()
     copies = []
     for i in range(HALF_BLK):
         above = lax.shift_right_logical(lists[OTH_T + i], 8) > me
         val = jnp.where(above == odd, far[i], near[i])
         res[i] = jnp.dot(val, wt[i], preferred_element_type=F32)
-        copy = pltpu.make_async_copy(
-            res.at[i], out.at[lists[OTH_B + i]], sems.at[HALF_BLK + i]
-        )
+        copy = pltpu.make_async_copy(res.at[i], out.at[lists[OTH_B + i]], sems.at[i])
         copy.start()
         copies.append(copy)
-    for copy in own_copies + copies:
+    for copy in copies:
         copy.wait()
 
 
@@ -515,9 +549,12 @@
     return pl.pallas_call(
         cells_kernel,
         out_shape=jax.ShapeDtypeStruct((BLK, NF, BLOCK), F32),
-        in_specs=[smem_spec()] + [vmem_spec()] * 3 + [plain_spec()],
+        in_specs=[smem_spec(), pl.BlockSpec(memory_space=pltpu.HBM)]
+        + [vmem_spec()] * 2
+        + [plain_spec()],
         out_specs=pl.BlockSpec(memory_space=pltpu.HBM),
-        scratch_shapes=[VMEM((HALF_BLK, NF, BLOCK), F32), pltpu.SemaphoreType.DMA((BLK,))],
+        scratch_shapes=[VMEM((HALF_BLK, NF, BLOCK), F32), pltpu.SemaphoreType.DMA((HALF_BLK,))],
+        input_output_aliases={1: 0},
         compiler_params=params(8),
         cost_estimate=cost(4),
     )(lists, own, far, near, wt)
@@ -535,7 +572,7 @@
 ):
     lists, wt_oth, oth = spread_other(block_tile, cell_count, ssh, remap_index, remap_weight)
     far = swap(oth, 1)
-    near = swap(oth, 0)
+    near = swap(later_copy(oth), 0)
     wt_own, grid = spread_own(lists, ssh, remap_index, remap_weight)
     fourier, spots = forward(grid, far, near, tables)
     by_order = lax.all_to_all(fourier, AXES, split_axis=0, concat_axis=0, tiled=True)
@@ -544,7 +581,7 @@
     own_v, far_v, near_v = inverse(lists, spots, by_lat, tables)
     from_far = swap(far_v, 1)
     from_near = swap(near_v, 0)
-    own_cell = own_cells(own_v, wt_own)
+    own_cell = own_cells(lists, own_v, wt_own)
     return all_cells(lists, own_cell, from_far, from_near, wt_oth)
 
 

time: 109 us -> 108 us (level)
  waiting for transfers between devices: 11.9 us -> 8.97 us
  local copies, waits for them, and re-layouts: 0.73 us -> 1.92 us
    ppermute x4, waiting for transfers between devices: 11.9 us -> 8.97 us  [swap(): return lax.ppermute(value, AXES, pairs)]
    pallas_call x1 -> x2, Pallas kernels: 0.83 us -> 2.3 us  [the longest x1 2.28 us: own_cells(): pl.pallas_call(own_cells_kernel, out_shape=jax.ShapeDtypeStruct((BLK, NF,...]
    unnamed x28 -> x30, local copies, waits for them, and re-layouts: 0.73 us -> 1.92 us
  transfers between devices with their start and end apart: 4 -> 4, of which waited for: 2 -> 3; matrix products, arithmetic and copies ran while one was open for 0% -> 0% of each run, Pallas kernels for 4% -> 5%
where the time goes in v4:
time: 108 us; the launch traced here: 107 us
  blocking collectives  51.7 us (48%)
  Pallas kernels  30.6 us (28%)
  starting transfers between devices  13.8 us (13%)
  waiting for transfers between devices  8.97 us (8%)
  local copies, waits for them, and re-layouts  1.92 us (2%)
    all_to_all x1, blocking collectives, on_device(): lax.all_to_all(fourier, AXES, split_axis=0, concat_axis=0, tiled=True)  28.7 us
    all_to_all x1, blocking collectives, on_device(): lax.all_to_all(synth, AXES, split_axis=0, concat_axis=0, tiled=True)  23 us
    ppermute x4, starting transfers between devices, swap(): return lax.ppermute(value, AXES, pairs)  13.8 us
    ppermute x4, waiting for transfers between devices, swap(): return lax.ppermute(value, AXES, pairs)  8.97 us
    pallas_call x1, Pallas kernels, legendre_both(): pl.pallas_call(legendre_kernel, out_shape=jax.ShapeDtypeStruct((DEVS, 32,...  7.83 us
    pallas_call x1, Pallas kernels, forward(): pl.pallas_call(forward_kernel, out_shape=(jax.ShapeDtypeStruct((DEVS, 32,...  5.29 us
    pallas_call x1, Pallas kernels, spread_other(): pl.pallas_call(other_kernel, grid=(HALF_BLK // STEP,), out_shape=(jax.Sha...  4.99 us
    pallas_call x1, Pallas kernels, inverse(): pl.pallas_call(inverse_kernel, out_shape=(jax.ShapeDtypeStruct((HALF_BLK,...  4.98 us
  transfers between devices with their start and end apart: 4, of which 3 were waited for; matrix products, arithmetic and copies ran while one was open for 0% of the time, Pallas kernels for 5%

profile of v4, /device:TPU:1, one launch (start us, length us, event | category | flops | bytes accessed | tf_op | source)
XLA Modules:
  0.0 107.3 jit_solution(13599695489736719602)
XLA Ops:
  0.0 5.0 %shard_map.109 = (s32[224]{0:T(256)}, bf16[32,256,256]{2,1,0:T(8,128)(2,1)}, bf16[33,16,256]{2,1,0:T(8,128)(2,1)}) custom-call(s32[64]{0:T(128)} %tile_hbm.1, s32[64]{0:T(128)} %count_hbm.1, f32[64,16,256]{2,1,0:T(8,128)} %ssh.1, s32[64,4,256]{2,1,0:T(4,128)} %index.1, f32[64,4,256]{2,1,0:T(4,128)} %weight.1), custom_call_target="tpu_custom_call" | custom-call | flops 5000000000 | bytes 4194304 | tf_op jit(solution)/shard_map/pallas_call | solution.py:234
  5.0 0.0 copy-start
  5.0 9.4 %collective-permute-start = (bf16[33,16,256]{2,1,0:T(8,128)(2,1)}, bf16[33,16,256]{2,1,0:T(8,128)(2,1)S(1)}, u32[]{:S(2)}, u32[]{:S(2)}) collective-permute-start(bf16[33,16,256]{2,1,0:T(8,128)(2,1)} %get-tuple-element.17.source), channel_id=1, source_target_pairs={{1,2},{2,1},{3,4},{4,3},{5,6},{6,5},{7,8},{8,7},{9,10},{10,9},{11,... | collective-permute-start | bytes 811016 | tf_op jit(solution)/shard_map/ppermute | solution.py:567
  14.4 0.0 copy-start.1
  14.4 1.0 copy-done.1
  15.4 0.0 copy-start.2
  15.4 0.0 copy-start.3
  15.4 0.0 copy-start.10
  15.4 0.1 collective-permute-start.1
  15.5 0.0 copy-done
  15.5 0.8 copy-done.2
  16.3 0.1 copy-done.3
  16.4 0.0 copy-done.10
  16.4 0.0 copy-start.6
  16.4 0.0 copy-start.7
  16.4 0.0 copy-start.8
  16.4 0.0 slice-start
  16.4 0.0 slice-start.1
  16.4 3.1 %shard_map.110 = (bf16[32,256,256]{2,1,0:T(8,128)(2,1)S(1)}, f32[257,16,256]{2,1,0:T(8,128)S(1)}) custom-call(s32[224]{0:T(256)S(1)} %copy-done.10, f32[64,16,256]{2,1,0:T(8,128)S(1)} %copy-done, s32[64,4,256]{2,1,0:T(4,128)S(1)} %copy-done.2, f32[64,4,256]{2,1,0:T(4,128)S(1)} %copy-done.3), custom_call_target="tpu_custom_call" | custom-call | flops 5000000000 | bytes 4194304 | tf_op jit(solution)/shard_map/pallas_call | solution.py:279
  19.5 1.3 %collective-permute-done.1.near = bf16[33,16,256]{2,1,0:T(8,128)(2,1)S(1)} collective-permute-done((bf16[33,16,256]{2,1,0:T(8,128)(2,1)S(1)}, bf16[33,16,256]{2,1,0:T(8,128)(2,1)S(1)}, u32[]{:S(2)}, u32[]{:S(2)}) %collective-permute-start.1) | collective-permute-done | bytes 270368 | tf_op jit(solution)/shard_map/ppermute | solution.py:567
  20.8 0.4 collective-permute-done.far
  21.2 0.0 copy-done.6
  21.2 0.0 copy-done.7
  21.2 0.0 copy-done.8
  21.2 0.0 slice-start.2
  21.2 0.0 slice-start.3
  21.2 0.0 copy-start.4
  21.2 0.0 copy-start.5
  21.2 5.3 %shard_map.112 = (bf16[128,32,128]{2,1,0:T(8,128)(2,1)S(1)}, s32[8,128]{1,0:T(8,128)S(1)}, f32[257,16,256]{2,1,0:T(8,128)S(1)}) custom-call(f32[257,16,256]{2,1,0:T(8,128)S(1)} %get-tuple-element.16.start_grid, bf16[33,16,256]{2,1,0:T(8,128)(2,1)S(1)} %collective-permute-done.far, ...), custom_call_target="tpu_custom_call", output_to_operand_aliasing={{2}: (0, {})} | custom-call | flops 8000000000 | bytes 4194304 | tf_op jit(solution)/shard_map/pallas_call | solution.py:355
  26.5 28.7 %all_to_all.10.data = bf16[128,32,128]{2,1,0:T(8,128)(2,1)S(1)} all-to-all(bf16[128,32,128]{2,1,0:T(8,128)(2,1)S(1)} %get-tuple-element.19), channel_id=1, replica_groups=mesh['dom'=8,'order'=16] {'dom','order'}, dimensions={0} | all-to-all | bytes 2097152 | tf_op jit(solution)/shard_map/all_to_all | solution.py:578
  55.2 0.0 slice-done
  55.2 0.0 slice-done.1
  55.2 0.0 slice-done.2
  55.3 0.0 slice-done.3
  55.3 0.0 copy-done.4
  55.3 0.0 copy-done.5
  55.3 7.8 %shard_map.113 = bf16[128,32,128]{2,1,0:T(8,128)(2,1)S(1)} custom-call(bf16[8,1024,1024]{2,1,0:T(8,128)(2,1)S(1)} %bitcast.3, bf16[128,32,128]{2,1,0:T(8,128)(2,1)S(1)} %all_to_all.10.data, f32[1,1024]{1,0:T(1,128)S(1)} %bitcast.4, f32[1,1024]{1,0:T(1,128)S(1)} %bitcast.5), custom_call_target="tpu_custom_call" | custom-call | flops 11000000512 | bytes 4194304 | tf_op jit(solution)/shard_map/pallas_call | solution.py:418
  63.1 23.0 %all_to_all.11.data = bf16[128,32,128]{2,1,0:T(8,128)(2,1)S(1)} all-to-all(bf16[128,32,128]{2,1,0:T(8,128)(2,1)S(1)} %shard_map.113), channel_id=1, replica_groups=mesh['dom'=8,'order'=16] {'dom','order'}, dimensions={0} | all-to-all | bytes 2097152 | tf_op jit(solution)/shard_map/all_to_all | solution.py:580
  86.2 5.0 %shard_map.114 = (f32[32,16,256]{2,1,0:T(8,128)S(1)}, bf16[32,16,256]{2,1,0:T(8,128)(2,1)S(1)}, bf16[32,16,256]{2,1,0:T(8,128)(2,1)S(1)}) custom-call(s32[224]{0:T(256)S(1)} %copy-done.10, s32[8,128]{1,0:T(8,128)S(1)} %get-tuple-element.18.spots, bf16[128,32,128]{2,1,0:T(8,128)(2,1)S(1)} %all_to_all.11.data, bf16[256,512]{1,0:T(8,128)(2,1)S(1)} %copy-done.6, ...), custom_call_target="tpu_custom_call" | custom-call | flops 7000000000 | bytes 4194304 | tf_op jit(solution)/shard_map/pallas_call | solution.py:486
  91.2 0.0 copy-start.9
  91.2 4.2 %collective-permute-start.2 = (bf16[32,16,256]{2,1,0:T(8,128)(2,1)S(1)}, bf16[32,16,256]{2,1,0:T(8,128)(2,1)S(1)}, u32[]{:S(2)}, u32[]{:S(2)}) collective-permute-start(bf16[32,16,256]{2,1,0:T(8,128)(2,1)S(1)} %get-tuple-element.22), channel_id=1, source_target_pairs={{1,2},{2,1},{3,4},{4,3},{5,6},{6,5},{7,8},{8,7},{9,10},{10,9},{11,... | collective-permute-start | bytes 786440 | tf_op jit(solution)/shard_map/ppermute | solution.py:567
  95.4 0.1 collective-permute-start.3
  95.5 2.3 %shard_map.115.own = f32[64,16,256]{2,1,0:T(8,128)} custom-call(s32[224]{0:T(256)S(1)} %copy-done.10, f32[32,16,256]{2,1,0:T(8,128)S(1)} %get-tuple-element.20.values, bf16[32,256,256]{2,1,0:T(8,128)(2,1)S(1)} %get-tuple-element.21.wt), custom_call_target="tpu_custom_call" | custom-call | flops 2000000000 | bytes 4194304 | tf_op jit(solution)/shard_map/pallas_call | solution.py:521
  97.8 7.3 %collective-permute-done.2.far = bf16[32,16,256]{2,1,0:T(8,128)(2,1)S(1)} collective-permute-done((bf16[32,16,256]{2,1,0:T(8,128)(2,1)S(1)}, bf16[32,16,256]{2,1,0:T(8,128)(2,1)S(1)}, u32[]{:S(2)}, u32[]{:S(2)}) %collective-permute-start.2) | collective-permute-done | bytes 262176 | tf_op jit(solution)/shard_map/ppermute | solution.py:567
  105.0 0.0 collective-permute-done.3.near
  105.1 0.0 copy-done.9
  105.1 2.1 %shard_map.116 = f32[64,16,256]{2,1,0:T(8,128)} custom-call(s32[224]{0:T(256)S(1)} %copy-done.10, f32[64,16,256]{2,1,0:T(8,128)} %shard_map.115.own, bf16[32,16,256]{2,1,0:T(8,128)(2,1)S(1)} %collective-permute-done.2.far, bf16[32,16,256]{2,1,0:T(8,128)(2,1)S(1)} %collective-permute-done.3.near, ...), custom_call_target="tpu_custom_call", output_to_operand_aliasing={{}: (1, {})} | custom-call | flops 4000000000 | bytes 4194304 | tf_op jit(solution)/shard_map/pallas_call | solution.py:549
  (2 shorter events, 0.0 us)
Async XLA Ops:
  5.0 10.5 %copy-start = (f32[64,16,256]{2,1,0:T(8,128)S(1)}, f32[64,16,256]{2,1,0:T(8,128)}, u32[]{:S(2)}) copy-start(f32[64,16,256]{2,1,0:T(8,128)} %ssh.1) | copy-start | bytes 3145732
  5.0 16.2 %collective-permute-start = (bf16[33,16,256]{2,1,0:T(8,128)(2,1)}, bf16[33,16,256]{2,1,0:T(8,128)(2,1)S(1)}, u32[]{:S(2)}, u32[]{:S(2)}) collective-permute-start(bf16[33,16,256]{2,1,0:T(8,128)(2,1)} %get-tuple-element.17.source), channel_id=1, source_target_pairs={{1,2},{2,1},{3,4},{4,3},{5,6},{6,5},{7,8},{8,7},{9,10},{10,9},{11,... | collective-permute-start | bytes 811016 | tf_op jit(solution)/shard_map/ppermute | solution.py:567
  14.4 1.0 copy-start.1
  15.4 0.9 copy-start.2
  15.4 1.0 copy-start.3
  15.4 1.0 copy-start.10
  15.4 5.4 %collective-permute-start.1 = (bf16[33,16,256]{2,1,0:T(8,128)(2,1)S(1)}, bf16[33,16,256]{2,1,0:T(8,128)(2,1)S(1)}, u32[]{:S(2)}, u32[]{:S(2)}) collective-permute-start(bf16[33,16,256]{2,1,0:T(8,128)(2,1)S(1)} %shard_map.111), channel_id=1, source_target_pairs={{0,1},{1,0},{2,3},{3,2},{4,5},{5,4},{6,7},{7,6},{8,9},{9,8},{10,11... | collective-permute-start | bytes 811016 | tf_op jit(solution)/shard_map/ppermute | solution.py:567
  16.4 4.8 %copy-start.6 = (bf16[256,512]{1,0:T(8,128)(2,1)S(1)}, bf16[256,512]{1,0:T(8,128)(2,1)}, u32[]{:S(2)}) copy-start(bf16[256,512]{1,0:T(8,128)(2,1)} %constant.6.clone.second) | copy-start | bytes 786436
  16.4 4.8 %copy-start.7 = (f32[16,256]{1,0:T(8,128)S(1)}, f32[16,256]{1,0:T(8,128)}, u32[]{:S(2)}) copy-start(f32[16,256]{1,0:T(8,128)} %constant.8.clone.tws) | copy-start | bytes 49156
  16.4 4.8 %copy-start.8 = (f32[16,256]{1,0:T(8,128)S(1)}, f32[16,256]{1,0:T(8,128)}, u32[]{:S(2)}) copy-start(f32[16,256]{1,0:T(8,128)} %constant.7.clone.twc) | copy-start | bytes 49156
  16.4 38.8 %slice-start = ((s8[16777216]{0:T(1024)(128)(4,1)}), s8[4194304]{0:T(1024)(128)(4,1)S(1)}, s32[]{:S(2)}) async-start(s8[16777216]{0:T(1024)(128)(4,1)} %bitcast.2), calls=%async_computation.2 | async-start | bytes 8388608
  16.4 38.8 %slice-start.1 = ((s8[16777216]{0:T(1024)(128)(4,1)}), s8[4194304]{0:T(1024)(128)(4,1)S(1)}, s32[]{:S(2)}) async-start(s8[16777216]{0:T(1024)(128)(4,1)} %bitcast.2), calls=%async_computation.3 | async-start | bytes 8388608
  21.2 34.1 %slice-start.2 = ((s8[16777216]{0:T(1024)(128)(4,1)}), s8[4194304]{0:T(1024)(128)(4,1)S(1)}, s32[]{:S(2)}) async-start(s8[16777216]{0:T(1024)(128)(4,1)} %bitcast.2), calls=%async_computation.4 | async-start | bytes 8388608
  21.2 34.1 %slice-start.3 = ((s8[16777216]{0:T(1024)(128)(4,1)}), s8[4194304]{0:T(1024)(128)(4,1)S(1)}, s32[]{:S(2)}) async-start(s8[16777216]{0:T(1024)(128)(4,1)} %bitcast.2), calls=%async_computation.5 | async-start | bytes 8388608
  21.2 34.1 %copy-start.4 = (f32[1024]{0:T(1024)S(1)}, f32[1024]{0:T(1024)}, u32[]{:S(2)}) copy-start(f32[1024]{0:T(1024)} %param.16) | copy-start | bytes 12292
  21.2 34.1 %copy-start.5 = (f32[1024]{0:T(1024)S(1)}, f32[1024]{0:T(1024)}, u32[]{:S(2)}) copy-start(f32[1024]{0:T(1024)} %param.17) | copy-start | bytes 12292
  91.2 13.9 %copy-start.9 = (bf16[32,256,256]{2,1,0:T(8,128)(2,1)S(1)}, bf16[32,256,256]{2,1,0:T(8,128)(2,1)}, u32[]{:S(2)}) copy-start(bf16[32,256,256]{2,1,0:T(8,128)(2,1)} %get-tuple-element.24.wt) | copy-start | bytes 12582916
  91.2 13.9 %collective-permute-start.2 = (bf16[32,16,256]{2,1,0:T(8,128)(2,1)S(1)}, bf16[32,16,256]{2,1,0:T(8,128)(2,1)S(1)}, u32[]{:S(2)}, u32[]{:S(2)}) collective-permute-start(bf16[32,16,256]{2,1,0:T(8,128)(2,1)S(1)} %get-tuple-element.22), channel_id=1, source_target_pairs={{1,2},{2,1},{3,4},{4,3},{5,6},{6,5},{7,8},{8,7},{9,10},{10,9},{11,... | collective-permute-start | bytes 786440 | tf_op jit(solution)/shard_map/ppermute | solution.py:567
  95.4 9.7 %collective-permute-start.3 = (bf16[32,16,256]{2,1,0:T(8,128)(2,1)S(1)}, bf16[32,16,256]{2,1,0:T(8,128)(2,1)S(1)}, u32[]{:S(2)}, u32[]{:S(2)}) collective-permute-start(bf16[32,16,256]{2,1,0:T(8,128)(2,1)S(1)} %get-tuple-element.23), channel_id=1, source_target_pairs={{0,1},{1,0},{2,3},{3,2},{4,5},{5,4},{6,7},{7,6},{8,9},{9,8},{10,11... | collective-permute-start | bytes 786440 | tf_op jit(solution)/shard_map/ppermute | solution.py:567

commit v5 on v4

--- a/solution.py
+++ b/solution.py
@@ -215,21 +215,6 @@
         out[step * STEP + i] = spread_block(ssh[b], mat).astype(BF16)
 
 
-def copy_kernel(source, out):
-    out[...] = source[...]
-
-
-def later_copy(value):
-    return pl.pallas_call(
-        copy_kernel,
-        out_shape=jax.ShapeDtypeStruct(value.shape, value.dtype),
-        in_specs=[vmem_spec()],
-        out_specs=vmem_spec(),
-        compiler_params=params(2),
-        cost_estimate=cost(3),
-    )(value)
-
-
 def spread_other(block_tile, cell_count, ssh, index, weight):
     return pl.pallas_call(
         other_kernel,
@@ -243,7 +228,7 @@
         out_specs=(
             smem_spec(),
             pl.BlockSpec((STEP, BLOCK, BLOCK), lambda i: (i, 0, 0)),
-            pl.BlockSpec((HALF_BLK + 1, NF, BLOCK), lambda i: (0, 0, 0)),
+            vmem_spec(),
         ),
         scratch_shapes=[
             SMEM((BLK,), jnp.int32),
@@ -253,7 +238,7 @@
             VMEM((BLK, 4, BLOCK), F32),
             pltpu.SemaphoreType.DMA((5,)),
         ],
-        compiler_params=params(60),
+        compiler_params=params(63),
         cost_estimate=cost(5),
     )(block_tile, cell_count, ssh, index, weight)
 
@@ -290,7 +275,7 @@
 
 
 def forward_kernel(
-    start_grid, far, near, second, twc, tws, out, spots, grid, mid, wide, codes, sem
+    start_grid, near, far, second, twc, tws, out, spots, grid, mid, wide, codes, sem
 ):
     del start_grid
     me = lax.axis_index(AXES)
@@ -370,7 +355,7 @@
         input_output_aliases={0: 2},
         compiler_params=params(14),
         cost_estimate=cost(8),
-    )(grid, far, near, tables["second"], tables["twc"], tables["tws"])
+    )(grid, near, far, tables["second"], tables["twc"], tables["tws"])
     return fourier, spots
 
 
@@ -442,8 +427,9 @@
         for uh in range(2):
             first = wide[pl.ds(uh * 32 + r, NQ, stride=64), :] * (2.0 if uh else zonal)
             second_half = wide[pl.ds(uh * 32 + 16 + r, NQ, stride=64), :] * 2.0
-            parts[0].append(jnp.where(left, first, pltpu.roll(second_half, 64, 1)))
-            parts[1].append(jnp.where(left, pltpu.roll(first, 64, 1), second_half))
+            turned = pltpu.roll(jnp.where(left, second_half, first), 64, 1)
+            parts[0].append(jnp.where(left, first, turned))
+            parts[1].append(jnp.where(left, turned, second_half))
         parts = [jnp.concatenate(part, axis=1) for part in parts]
         spectrum = jnp.concatenate(parts, axis=0).T.astype(BF16)
         spectrum = jnp.concatenate([spectrum, spectrum], axis=1)
@@ -572,7 +558,7 @@
 ):
     lists, wt_oth, oth = spread_other(block_tile, cell_count, ssh, remap_index, remap_weight)
     far = swap(oth, 1)
-    near = swap(later_copy(oth), 0)
+    near = swap(oth, 0)
     wt_own, grid = spread_own(lists, ssh, remap_index, remap_weight)
     fourier, spots = forward(grid, far, near, tables)
     by_order = lax.all_to_all(fourier, AXES, split_axis=0, concat_axis=0, tiled=True)

time: 108 us -> 107 us (level)
  transfers between devices with their start and end apart: 4 -> 4, of which waited for: 3 -> 2; matrix products, arithmetic and copies ran while one was open for 0% -> 0% of each run, Pallas kernels for 5% -> 5%
where the time goes in v5:
time: 107 us
  blocking collectives  51.7 us (48%)
  Pallas kernels  30.3 us (28%)
  starting transfers between devices  13.6 us (13%)
  waiting for transfers between devices  8.95 us (8%)
  local copies, waits for them, and re-layouts  1.95 us (2%)
    all_to_all x1, blocking collectives, on_device(): lax.all_to_all(fourier, AXES, split_axis=0, concat_axis=0, tiled=True)  28.7 us
    all_to_all x1, blocking collectives, on_device(): lax.all_to_all(synth, AXES, split_axis=0, concat_axis=0, tiled=True)  23 us
    ppermute x4, starting transfers between devices, swap(): return lax.ppermute(value, AXES, pairs)  13.6 us
    ppermute x4, waiting for transfers between devices, swap(): return lax.ppermute(value, AXES, pairs)  8.95 us
    pallas_call x1, Pallas kernels, legendre_both(): pl.pallas_call(legendre_kernel, out_shape=jax.ShapeDtypeStruct((DEVS, 32,...  7.84 us
    pallas_call x1, Pallas kernels, forward(): pl.pallas_call(forward_kernel, out_shape=(jax.ShapeDtypeStruct((DEVS, 32,...  5.3 us
    pallas_call x1, Pallas kernels, spread_other(): pl.pallas_call(other_kernel, grid=(HALF_BLK // STEP,), out_shape=(jax.Sha...  5.03 us
    pallas_call x1, Pallas kernels, inverse(): pl.pallas_call(inverse_kernel, out_shape=(jax.ShapeDtypeStruct((HALF_BLK,...  4.73 us
  transfers between devices with their start and end apart: 4, of which 2 were waited for; matrix products, arithmetic and copies ran while one was open for 0% of the time, Pallas kernels for 5%

profile of v5, /device:TPU:1, one launch (start us, length us, event | category | flops | bytes accessed | tf_op | source)
XLA Modules:
  0.0 107.0 jit_solution(4446498254517765550)
XLA Ops:
  0.0 0.0 copy-start.2
  0.0 0.0 copy-start.1
  0.0 5.0 %shard_map.109 = (s32[224]{0:T(256)}, bf16[32,256,256]{2,1,0:T(8,128)(2,1)}, bf16[33,16,256]{2,1,0:T(8,128)(2,1)}) custom-call(s32[64]{0:T(128)} %tile_hbm.1, s32[64]{0:T(128)} %count_hbm.1, f32[64,16,256]{2,1,0:T(8,128)} %ssh.1, s32[64,4,256]{2,1,0:T(4,128)} %index.1, f32[64,4,256]{2,1,0:T(4,128)} %weight.1), custom_call_target="tpu_custom_call" | custom-call | flops 5000000000 | bytes 4194304 | tf_op jit(solution)/shard_map/pallas_call | solution.py:219
  5.0 9.2 %collective-permute-start.1 = (bf16[33,16,256]{2,1,0:T(8,128)(2,1)}, bf16[33,16,256]{2,1,0:T(8,128)(2,1)S(1)}, u32[]{:S(2)}, u32[]{:S(2)}) collective-permute-start(bf16[33,16,256]{2,1,0:T(8,128)(2,1)} %get-tuple-element.17), channel_id=1, source_target_pairs={{1,2},{2,1},{3,4},{4,3},{5,6},{6,5},{7,8},{8,7},{9,10},{10,9},{11,... | collective-permute-start | bytes 811016 | tf_op jit(solution)/shard_map/ppermute | solution.py:553
  14.3 0.1 collective-permute-start
  14.4 0.0 copy-done.2
  14.4 0.0 copy-done.1
  14.4 0.0 copy-start
  14.4 1.2 %copy-done = f32[64,16,256]{2,1,0:T(8,128)S(1)} copy-done((f32[64,16,256]{2,1,0:T(8,128)S(1)}, f32[64,16,256]{2,1,0:T(8,128)}, u32[]{:S(2)}) %copy-start) | copy-done | bytes 1048600
  15.6 0.0 copy-start.9
  15.6 0.7 copy-done.9
  16.3 0.0 copy-start.5
  16.3 0.0 copy-start.6
  16.3 0.0 copy-start.7
  16.3 0.0 slice-start
  16.3 0.0 slice-start.1
  16.3 3.1 %shard_map.110 = (bf16[32,256,256]{2,1,0:T(8,128)(2,1)S(1)}, f32[257,16,256]{2,1,0:T(8,128)S(1)}) custom-call(s32[224]{0:T(256)S(1)} %copy-done.9, f32[64,16,256]{2,1,0:T(8,128)S(1)} %copy-done, s32[64,4,256]{2,1,0:T(4,128)S(1)} %copy-done.1, f32[64,4,256]{2,1,0:T(4,128)S(1)} %copy-done.2), custom_call_target="tpu_custom_call" | custom-call | flops 5000000000 | bytes 4194304 | tf_op jit(solution)/shard_map/pallas_call | solution.py:264
  19.4 1.7 %collective-permute-done.1.far = bf16[33,16,256]{2,1,0:T(8,128)(2,1)S(1)} collective-permute-done((bf16[33,16,256]{2,1,0:T(8,128)(2,1)}, bf16[33,16,256]{2,1,0:T(8,128)(2,1)S(1)}, u32[]{:S(2)}, u32[]{:S(2)}) %collective-permute-start.1) | collective-permute-done | bytes 270368 | tf_op jit(solution)/shard_map/ppermute | solution.py:553
  21.1 0.0 collective-permute-done.near
  21.1 0.0 copy-done.5
  21.1 0.0 copy-done.6
  21.1 0.0 copy-done.7
  21.1 0.0 slice-start.2
  21.1 0.0 slice-start.3
  21.1 0.0 copy-start.3
  21.1 0.0 copy-start.4
  21.1 5.3 %shard_map.111 = (bf16[128,32,128]{2,1,0:T(8,128)(2,1)S(1)}, s32[8,128]{1,0:T(8,128)S(1)}, f32[257,16,256]{2,1,0:T(8,128)S(1)}) custom-call(f32[257,16,256]{2,1,0:T(8,128)S(1)} %get-tuple-element.16.start_grid, bf16[33,16,256]{2,1,0:T(8,128)(2,1)S(1)} %collective-permute-done.near, ...), custom_call_target="tpu_custom_call", output_to_operand_aliasing={{2}: (0, {})} | custom-call | flops 8000000000 | bytes 4194304 | tf_op jit(solution)/shard_map/pallas_call | solution.py:340
  26.5 28.7 %all_to_all.10.data = bf16[128,32,128]{2,1,0:T(8,128)(2,1)S(1)} all-to-all(bf16[128,32,128]{2,1,0:T(8,128)(2,1)S(1)} %get-tuple-element.19), channel_id=1, replica_groups=mesh['dom'=8,'order'=16] {'dom','order'}, dimensions={0} | all-to-all | bytes 2097152 | tf_op jit(solution)/shard_map/all_to_all | solution.py:564
  55.1 0.0 slice-done
  55.1 0.0 slice-done.1
  55.1 0.0 slice-done.2
  55.2 0.0 slice-done.3
  55.2 0.0 copy-done.3
  55.2 0.0 copy-done.4
  55.2 7.8 %shard_map.112 = bf16[128,32,128]{2,1,0:T(8,128)(2,1)S(1)} custom-call(bf16[8,1024,1024]{2,1,0:T(8,128)(2,1)S(1)} %bitcast.3, bf16[128,32,128]{2,1,0:T(8,128)(2,1)S(1)} %all_to_all.10.data, f32[1,1024]{1,0:T(1,128)S(1)} %bitcast.4, f32[1,1024]{1,0:T(1,128)S(1)} %bitcast.5), custom_call_target="tpu_custom_call" | custom-call | flops 11000000512 | bytes 4194304 | tf_op jit(solution)/shard_map/pallas_call | solution.py:403
  63.0 23.0 %all_to_all.11.data = bf16[128,32,128]{2,1,0:T(8,128)(2,1)S(1)} all-to-all(bf16[128,32,128]{2,1,0:T(8,128)(2,1)S(1)} %shard_map.112), channel_id=1, replica_groups=mesh['dom'=8,'order'=16] {'dom','order'}, dimensions={0} | all-to-all | bytes 2097152 | tf_op jit(solution)/shard_map/all_to_all | solution.py:566
  86.1 4.7 %shard_map.113 = (f32[32,16,256]{2,1,0:T(8,128)S(1)}, bf16[32,16,256]{2,1,0:T(8,128)(2,1)S(1)}, bf16[32,16,256]{2,1,0:T(8,128)(2,1)S(1)}) custom-call(s32[224]{0:T(256)S(1)} %copy-done.9, s32[8,128]{1,0:T(8,128)S(1)} %get-tuple-element.18.spots, bf16[128,32,128]{2,1,0:T(8,128)(2,1)S(1)} %all_to_all.11.data, bf16[256,512]{1,0:T(8,128)(2,1)S(1)} %copy-done.5, ...), custom_call_target="tpu_custom_call" | custom-call | flops 7000000000 | bytes 4194304 | tf_op jit(solution)/shard_map/pallas_call | solution.py:472
  90.8 0.0 copy-start.8
  90.8 4.2 %collective-permute-start.2 = (bf16[32,16,256]{2,1,0:T(8,128)(2,1)S(1)}, bf16[32,16,256]{2,1,0:T(8,128)(2,1)S(1)}, u32[]{:S(2)}, u32[]{:S(2)}) collective-permute-start(bf16[32,16,256]{2,1,0:T(8,128)(2,1)S(1)} %get-tuple-element.22), channel_id=1, source_target_pairs={{1,2},{2,1},{3,4},{4,3},{5,6},{6,5},{7,8},{8,7},{9,10},{10,9},{11,... | collective-permute-start | bytes 786440 | tf_op jit(solution)/shard_map/ppermute | solution.py:553
  95.1 0.1 collective-permute-start.3
  95.1 2.3 %shard_map.114.own = f32[64,16,256]{2,1,0:T(8,128)} custom-call(s32[224]{0:T(256)S(1)} %copy-done.9, f32[32,16,256]{2,1,0:T(8,128)S(1)} %get-tuple-element.20.values, bf16[32,256,256]{2,1,0:T(8,128)(2,1)S(1)} %get-tuple-element.21.wt), custom_call_target="tpu_custom_call" | custom-call | flops 2000000000 | bytes 4194304 | tf_op jit(solution)/shard_map/pallas_call | solution.py:507
  97.4 7.3 %collective-permute-done.2.far = bf16[32,16,256]{2,1,0:T(8,128)(2,1)S(1)} collective-permute-done((bf16[32,16,256]{2,1,0:T(8,128)(2,1)S(1)}, bf16[32,16,256]{2,1,0:T(8,128)(2,1)S(1)}, u32[]{:S(2)}, u32[]{:S(2)}) %collective-permute-start.2) | collective-permute-done | bytes 262176 | tf_op jit(solution)/shard_map/ppermute | solution.py:553
  104.7 0.0 collective-permute-done.3.near
  104.7 0.0 copy-done.8
  104.7 2.1 %shard_map.115 = f32[64,16,256]{2,1,0:T(8,128)} custom-call(s32[224]{0:T(256)S(1)} %copy-done.9, f32[64,16,256]{2,1,0:T(8,128)} %shard_map.114.own, bf16[32,16,256]{2,1,0:T(8,128)(2,1)S(1)} %collective-permute-done.2.far, bf16[32,16,256]{2,1,0:T(8,128)(2,1)S(1)} %collective-permute-done.3.near, ...), custom_call_target="tpu_custom_call", output_to_operand_aliasing={{}: (1, {})} | custom-call | flops 4000000000 | bytes 4194304 | tf_op jit(solution)/shard_map/pallas_call | solution.py:535
  (1 shorter events, 0.0 us)
Async XLA Ops:
  0.0 14.4 %copy-start.2 = (f32[64,4,256]{2,1,0:T(4,128)S(1)}, f32[64,4,256]{2,1,0:T(4,128)}, u32[]{:S(2)}) copy-start(f32[64,4,256]{2,1,0:T(4,128)} %weight.1) | copy-start | bytes 786436
  0.0 14.4 %copy-start.1 = (s32[64,4,256]{2,1,0:T(4,128)S(1)}, s32[64,4,256]{2,1,0:T(4,128)}, u32[]{:S(2)}) copy-start(s32[64,4,256]{2,1,0:T(4,128)} %index.1) | copy-start | bytes 786436
  5.0 16.0 %collective-permute-start.1 = (bf16[33,16,256]{2,1,0:T(8,128)(2,1)}, bf16[33,16,256]{2,1,0:T(8,128)(2,1)S(1)}, u32[]{:S(2)}, u32[]{:S(2)}) collective-permute-start(bf16[33,16,256]{2,1,0:T(8,128)(2,1)} %get-tuple-element.17), channel_id=1, source_target_pairs={{1,2},{2,1},{3,4},{4,3},{5,6},{6,5},{7,8},{8,7},{9,10},{10,9},{11,... | collective-permute-start | bytes 811016 | tf_op jit(solution)/shard_map/ppermute | solution.py:553
  14.3 6.8 %collective-permute-start = (bf16[33,16,256]{2,1,0:T(8,128)(2,1)}, bf16[33,16,256]{2,1,0:T(8,128)(2,1)S(1)}, u32[]{:S(2)}, u32[]{:S(2)}) collective-permute-start(bf16[33,16,256]{2,1,0:T(8,128)(2,1)} %get-tuple-element.17), channel_id=1, source_target_pairs={{0,1},{1,0},{2,3},{3,2},{4,5},{5,4},{6,7},{7,6},{8,9},{9,8},{10,11... | collective-permute-start | bytes 811016 | tf_op jit(solution)/shard_map/ppermute | solution.py:553
  14.4 1.2 %copy-start = (f32[64,16,256]{2,1,0:T(8,128)S(1)}, f32[64,16,256]{2,1,0:T(8,128)}, u32[]{:S(2)}) copy-start(f32[64,16,256]{2,1,0:T(8,128)} %ssh.1) | copy-start | bytes 3145732
  15.6 0.7 copy-start.9
  16.3 4.8 %copy-start.5 = (bf16[256,512]{1,0:T(8,128)(2,1)S(1)}, bf16[256,512]{1,0:T(8,128)(2,1)}, u32[]{:S(2)}) copy-start(bf16[256,512]{1,0:T(8,128)(2,1)} %constant.6.clone.second) | copy-start | bytes 786436
  16.3 4.8 %copy-start.6 = (f32[16,256]{1,0:T(8,128)S(1)}, f32[16,256]{1,0:T(8,128)}, u32[]{:S(2)}) copy-start(f32[16,256]{1,0:T(8,128)} %constant.8.clone.tws) | copy-start | bytes 49156
  16.3 4.8 %copy-start.7 = (f32[16,256]{1,0:T(8,128)S(1)}, f32[16,256]{1,0:T(8,128)}, u32[]{:S(2)}) copy-start(f32[16,256]{1,0:T(8,128)} %constant.7.clone.twc) | copy-start | bytes 49156
  16.3 38.8 %slice-start = ((s8[16777216]{0:T(1024)(128)(4,1)}), s8[4194304]{0:T(1024)(128)(4,1)S(1)}, s32[]{:S(2)}) async-start(s8[16777216]{0:T(1024)(128)(4,1)} %bitcast.2), calls=%async_computation.2 | async-start | bytes 8388608
  16.3 38.8 %slice-start.1 = ((s8[16777216]{0:T(1024)(128)(4,1)}), s8[4194304]{0:T(1024)(128)(4,1)S(1)}, s32[]{:S(2)}) async-start(s8[16777216]{0:T(1024)(128)(4,1)} %bitcast.2), calls=%async_computation.3 | async-start | bytes 8388608
  21.1 34.0 %slice-start.2 = ((s8[16777216]{0:T(1024)(128)(4,1)}), s8[4194304]{0:T(1024)(128)(4,1)S(1)}, s32[]{:S(2)}) async-start(s8[16777216]{0:T(1024)(128)(4,1)} %bitcast.2), calls=%async_computation.4 | async-start | bytes 8388608
  21.1 34.0 %slice-start.3 = ((s8[16777216]{0:T(1024)(128)(4,1)}), s8[4194304]{0:T(1024)(128)(4,1)S(1)}, s32[]{:S(2)}) async-start(s8[16777216]{0:T(1024)(128)(4,1)} %bitcast.2), calls=%async_computation.5 | async-start | bytes 8388608
  21.1 34.0 %copy-start.3 = (f32[1024]{0:T(1024)S(1)}, f32[1024]{0:T(1024)}, u32[]{:S(2)}) copy-start(f32[1024]{0:T(1024)} %param.16) | copy-start | bytes 12292
  21.1 34.0 %copy-start.4 = (f32[1024]{0:T(1024)S(1)}, f32[1024]{0:T(1024)}, u32[]{:S(2)}) copy-start(f32[1024]{0:T(1024)} %param.17) | copy-start | bytes 12292
  90.8 13.9 %copy-start.8 = (bf16[32,256,256]{2,1,0:T(8,128)(2,1)S(1)}, bf16[32,256,256]{2,1,0:T(8,128)(2,1)}, u32[]{:S(2)}) copy-start(bf16[32,256,256]{2,1,0:T(8,128)(2,1)} %get-tuple-element.24.wt) | copy-start | bytes 12582916
  90.8 13.9 %collective-permute-start.2 = (bf16[32,16,256]{2,1,0:T(8,128)(2,1)S(1)}, bf16[32,16,256]{2,1,0:T(8,128)(2,1)S(1)}, u32[]{:S(2)}, u32[]{:S(2)}) collective-permute-start(bf16[32,16,256]{2,1,0:T(8,128)(2,1)S(1)} %get-tuple-element.22), channel_id=1, source_target_pairs={{1,2},{2,1},{3,4},{4,3},{5,6},{6,5},{7,8},{8,7},{9,10},{10,9},{11,... | collective-permute-start | bytes 786440 | tf_op jit(solution)/shard_map/ppermute | solution.py:553
  95.1 9.7 %collective-permute-start.3 = (bf16[32,16,256]{2,1,0:T(8,128)(2,1)S(1)}, bf16[32,16,256]{2,1,0:T(8,128)(2,1)S(1)}, u32[]{:S(2)}, u32[]{:S(2)}) collective-permute-start(bf16[32,16,256]{2,1,0:T(8,128)(2,1)S(1)} %get-tuple-element.23), channel_id=1, source_target_pairs={{0,1},{1,0},{2,3},{3,2},{4,5},{5,4},{6,7},{7,6},{8,9},{9,8},{10,11... | collective-permute-start | bytes 786440 | tf_op jit(solution)/shard_map/ppermute | solution.py:553

commit v6 on v5

--- a/solution.py
+++ b/solution.py
@@ -45,7 +45,7 @@
     second = np.concatenate(
         [np.concatenate([cos, sin], axis=1), np.concatenate([-sin, cos], axis=1)], axis=0
     )
-    s_hi, s_lo = hi_lo(second)
+    s_hi, s_lo = hi_lo(2.0 * second)
     twist = 2 * np.pi * (np.arange(RADIX)[:, None] * points[None, :]) / 4096.0
     return dict(
         second=np.concatenate([s_hi, s_lo], axis=0),
@@ -321,7 +321,7 @@
         res = lax.dot_general(
             second[...], mid[r], (((1,), (1,)), ((), ())), preferred_element_type=F32
         )
-        res = (res[:128] + res[128:]) * (1.0 / 4096.0)
+        res = (res[:128] + res[128:]) * (1.0 / 8192.0)
         for c in range(2):
             for uh in range(2):
                 wide[pl.ds(uh * 32 + c * 16 + r, NQ, stride=64), :] = res[
@@ -419,14 +419,15 @@
     wide[...] = data[...].astype(F32).reshape(wide.shape)
     row = lax.broadcasted_iota(jnp.int32, (NQ, 128), 0)
     lane = lax.broadcasted_iota(jnp.int32, (NQ, 128), 1)
-    zonal = jnp.where((row == 0) & ((lane & 63) < NF), 1.0, 2.0)
+    zonal = jnp.where((row == 0) & ((lane & 63) < NF), 0.5, 1.0)
     left = lane < 64
 
     def spread_waves(r):
         parts = [[], []]
         for uh in range(2):
-            first = wide[pl.ds(uh * 32 + r, NQ, stride=64), :] * (2.0 if uh else zonal)
-            second_half = wide[pl.ds(uh * 32 + 16 + r, NQ, stride=64), :] * 2.0
+            first = wide[pl.ds(uh * 32 + r, NQ, stride=64), :]
+            first = first if uh else first * zonal
+            second_half = wide[pl.ds(uh * 32 + 16 + r, NQ, stride=64), :]
             turned = pltpu.roll(jnp.where(left, second_half, first), 64, 1)
             parts[0].append(jnp.where(left, first, turned))
             parts[1].append(jnp.where(left, turned, second_half))

time: 107 us -> 107 us (level)
  no operation moved by 1% of the time
where the time goes in v6:
time: 107 us
  blocking collectives  51.7 us (48%)
  Pallas kernels  30.3 us (28%)
  starting transfers between devices  13.6 us (13%)
  waiting for transfers between devices  8.96 us (8%)
  local copies, waits for them, and re-layouts  1.95 us (2%)
    all_to_all x1, blocking collectives, on_device(): lax.all_to_all(fourier, AXES, split_axis=0, concat_axis=0, tiled=True)  28.6 us
    all_to_all x1, blocking collectives, on_device(): lax.all_to_all(synth, AXES, split_axis=0, concat_axis=0, tiled=True)  23 us
    ppermute x4, starting transfers between devices, swap(): return lax.ppermute(value, AXES, pairs)  13.6 us
    ppermute x4, waiting for transfers between devices, swap(): return lax.ppermute(value, AXES, pairs)  8.96 us
    pallas_call x1, Pallas kernels, legendre_both(): pl.pallas_call(legendre_kernel, out_shape=jax.ShapeDtypeStruct((DEVS, 32,...  7.83 us
    pallas_call x1, Pallas kernels, forward(): pl.pallas_call(forward_kernel, out_shape=(jax.ShapeDtypeStruct((DEVS, 32,...  5.31 us
    pallas_call x1, Pallas kernels, spread_other(): pl.pallas_call(other_kernel, grid=(HALF_BLK // STEP,), out_shape=(jax.Sha...  5.03 us
    pallas_call x1, Pallas kernels, inverse(): pl.pallas_call(inverse_kernel, out_shape=(jax.ShapeDtypeStruct((HALF_BLK,...  4.65 us
  transfers between devices with their start and end apart: 4, of which 2 were waited for; matrix products, arithmetic and copies ran while one was open for 0% of the time, Pallas kernels for 5%

profile of v6, /device:TPU:1, one launch (start us, length us, event | category | flops | bytes accessed | tf_op | source)
XLA Modules:
  0.0 106.8 jit_solution(17967235977107967187)
XLA Ops:
  0.0 0.0 copy-start.2
  0.0 0.0 copy-start.1
  0.0 5.0 %shard_map.109 = (s32[224]{0:T(256)}, bf16[32,256,256]{2,1,0:T(8,128)(2,1)}, bf16[33,16,256]{2,1,0:T(8,128)(2,1)}) custom-call(s32[64]{0:T(128)} %tile_hbm.1, s32[64]{0:T(128)} %count_hbm.1, f32[64,16,256]{2,1,0:T(8,128)} %ssh.1, s32[64,4,256]{2,1,0:T(4,128)} %index.1, f32[64,4,256]{2,1,0:T(4,128)} %weight.1), custom_call_target="tpu_custom_call" | custom-call | flops 5000000000 | bytes 4194304 | tf_op jit(solution)/shard_map/pallas_call | solution.py:219
  5.0 9.2 %collective-permute-start.1 = (bf16[33,16,256]{2,1,0:T(8,128)(2,1)}, bf16[33,16,256]{2,1,0:T(8,128)(2,1)S(1)}, u32[]{:S(2)}, u32[]{:S(2)}) collective-permute-start(bf16[33,16,256]{2,1,0:T(8,128)(2,1)} %get-tuple-element.17), channel_id=1, source_target_pairs={{1,2},{2,1},{3,4},{4,3},{5,6},{6,5},{7,8},{8,7},{9,10},{10,9},{11,... | collective-permute-start | bytes 811016 | tf_op jit(solution)/shard_map/ppermute | solution.py:554
  14.3 0.1 collective-permute-start
  14.4 0.0 copy-done.2
  14.4 0.0 copy-done.1
  14.4 0.0 copy-start
  14.4 1.2 %copy-done = f32[64,16,256]{2,1,0:T(8,128)S(1)} copy-done((f32[64,16,256]{2,1,0:T(8,128)S(1)}, f32[64,16,256]{2,1,0:T(8,128)}, u32[]{:S(2)}) %copy-start) | copy-done | bytes 1048600
  15.6 0.0 copy-start.9
  15.6 0.7 copy-done.9
  16.3 0.0 copy-start.5
  16.3 0.0 copy-start.6
  16.3 0.0 copy-start.7
  16.3 0.0 slice-start
  16.3 0.0 slice-start.1
  16.3 3.1 %shard_map.110 = (bf16[32,256,256]{2,1,0:T(8,128)(2,1)S(1)}, f32[257,16,256]{2,1,0:T(8,128)S(1)}) custom-call(s32[224]{0:T(256)S(1)} %copy-done.9, f32[64,16,256]{2,1,0:T(8,128)S(1)} %copy-done, s32[64,4,256]{2,1,0:T(4,128)S(1)} %copy-done.1, f32[64,4,256]{2,1,0:T(4,128)S(1)} %copy-done.2), custom_call_target="tpu_custom_call" | custom-call | flops 5000000000 | bytes 4194304 | tf_op jit(solution)/shard_map/pallas_call | solution.py:264
  19.4 1.7 %collective-permute-done.1.far = bf16[33,16,256]{2,1,0:T(8,128)(2,1)S(1)} collective-permute-done((bf16[33,16,256]{2,1,0:T(8,128)(2,1)}, bf16[33,16,256]{2,1,0:T(8,128)(2,1)S(1)}, u32[]{:S(2)}, u32[]{:S(2)}) %collective-permute-start.1) | collective-permute-done | bytes 270368 | tf_op jit(solution)/shard_map/ppermute | solution.py:554
  21.1 0.0 collective-permute-done.near
  21.1 0.0 copy-done.5
  21.1 0.0 copy-done.6
  21.1 0.0 copy-done.7
  21.1 0.0 slice-start.2
  21.1 0.0 slice-start.3
  21.1 0.0 copy-start.3
  21.1 0.0 copy-start.4
  21.1 5.3 %shard_map.111 = (bf16[128,32,128]{2,1,0:T(8,128)(2,1)S(1)}, s32[8,128]{1,0:T(8,128)S(1)}, f32[257,16,256]{2,1,0:T(8,128)S(1)}) custom-call(f32[257,16,256]{2,1,0:T(8,128)S(1)} %get-tuple-element.16.start_grid, bf16[33,16,256]{2,1,0:T(8,128)(2,1)S(1)} %collective-permute-done.near, ...), custom_call_target="tpu_custom_call", output_to_operand_aliasing={{2}: (0, {})} | custom-call | flops 8000000000 | bytes 4194304 | tf_op jit(solution)/shard_map/pallas_call | solution.py:340
  26.5 28.6 %all_to_all.10.data = bf16[128,32,128]{2,1,0:T(8,128)(2,1)S(1)} all-to-all(bf16[128,32,128]{2,1,0:T(8,128)(2,1)S(1)} %get-tuple-element.19), channel_id=1, replica_groups=mesh['dom'=8,'order'=16] {'dom','order'}, dimensions={0} | all-to-all | bytes 2097152 | tf_op jit(solution)/shard_map/all_to_all | solution.py:565
  55.1 0.0 slice-done
  55.1 0.0 slice-done.1
  55.1 0.0 slice-done.2
  55.1 0.0 slice-done.3
  55.1 0.0 copy-done.3
  55.1 0.0 copy-done.4
  55.1 7.8 %shard_map.112 = bf16[128,32,128]{2,1,0:T(8,128)(2,1)S(1)} custom-call(bf16[8,1024,1024]{2,1,0:T(8,128)(2,1)S(1)} %bitcast.3, bf16[128,32,128]{2,1,0:T(8,128)(2,1)S(1)} %all_to_all.10.data, f32[1,1024]{1,0:T(1,128)S(1)} %bitcast.4, f32[1,1024]{1,0:T(1,128)S(1)} %bitcast.5), custom_call_target="tpu_custom_call" | custom-call | flops 11000000512 | bytes 4194304 | tf_op jit(solution)/shard_map/pallas_call | solution.py:403
  63.0 23.0 %all_to_all.11.data = bf16[128,32,128]{2,1,0:T(8,128)(2,1)S(1)} all-to-all(bf16[128,32,128]{2,1,0:T(8,128)(2,1)S(1)} %shard_map.112), channel_id=1, replica_groups=mesh['dom'=8,'order'=16] {'dom','order'}, dimensions={0} | all-to-all | bytes 2097152 | tf_op jit(solution)/shard_map/all_to_all | solution.py:567
  86.0 4.7 %shard_map.113 = (f32[32,16,256]{2,1,0:T(8,128)S(1)}, bf16[32,16,256]{2,1,0:T(8,128)(2,1)S(1)}, bf16[32,16,256]{2,1,0:T(8,128)(2,1)S(1)}) custom-call(s32[224]{0:T(256)S(1)} %copy-done.9, s32[8,128]{1,0:T(8,128)S(1)} %get-tuple-element.18.spots, bf16[128,32,128]{2,1,0:T(8,128)(2,1)S(1)} %all_to_all.11.data, bf16[256,512]{1,0:T(8,128)(2,1)S(1)} %copy-done.5, ...), custom_call_target="tpu_custom_call" | custom-call | flops 7000000000 | bytes 4194304 | tf_op jit(solution)/shard_map/pallas_call | solution.py:473
  90.7 0.0 copy-start.8
  90.7 4.2 %collective-permute-start.2 = (bf16[32,16,256]{2,1,0:T(8,128)(2,1)S(1)}, bf16[32,16,256]{2,1,0:T(8,128)(2,1)S(1)}, u32[]{:S(2)}, u32[]{:S(2)}) collective-permute-start(bf16[32,16,256]{2,1,0:T(8,128)(2,1)S(1)} %get-tuple-element.22), channel_id=1, source_target_pairs={{1,2},{2,1},{3,4},{4,3},{5,6},{6,5},{7,8},{8,7},{9,10},{10,9},{11,... | collective-permute-start | bytes 786440 | tf_op jit(solution)/shard_map/ppermute | solution.py:554
  94.9 0.1 collective-permute-start.3
  95.0 2.3 %shard_map.114.own = f32[64,16,256]{2,1,0:T(8,128)} custom-call(s32[224]{0:T(256)S(1)} %copy-done.9, f32[32,16,256]{2,1,0:T(8,128)S(1)} %get-tuple-element.20.values, bf16[32,256,256]{2,1,0:T(8,128)(2,1)S(1)} %get-tuple-element.21.wt), custom_call_target="tpu_custom_call" | custom-call | flops 2000000000 | bytes 4194304 | tf_op jit(solution)/shard_map/pallas_call | solution.py:508
  97.3 7.3 %collective-permute-done.2.far = bf16[32,16,256]{2,1,0:T(8,128)(2,1)S(1)} collective-permute-done((bf16[32,16,256]{2,1,0:T(8,128)(2,1)S(1)}, bf16[32,16,256]{2,1,0:T(8,128)(2,1)S(1)}, u32[]{:S(2)}, u32[]{:S(2)}) %collective-permute-start.2) | collective-permute-done | bytes 262176 | tf_op jit(solution)/shard_map/ppermute | solution.py:554
  104.6 0.0 collective-permute-done.3.near
  104.6 0.0 copy-done.8
  104.6 2.1 %shard_map.115 = f32[64,16,256]{2,1,0:T(8,128)} custom-call(s32[224]{0:T(256)S(1)} %copy-done.9, f32[64,16,256]{2,1,0:T(8,128)} %shard_map.114.own, bf16[32,16,256]{2,1,0:T(8,128)(2,1)S(1)} %collective-permute-done.2.far, bf16[32,16,256]{2,1,0:T(8,128)(2,1)S(1)} %collective-permute-done.3.near, ...), custom_call_target="tpu_custom_call", output_to_operand_aliasing={{}: (1, {})} | custom-call | flops 4000000000 | bytes 4194304 | tf_op jit(solution)/shard_map/pallas_call | solution.py:536
  (1 shorter events, 0.0 us)
Async XLA Ops:
  0.0 14.4 %copy-start.2 = (f32[64,4,256]{2,1,0:T(4,128)S(1)}, f32[64,4,256]{2,1,0:T(4,128)}, u32[]{:S(2)}) copy-start(f32[64,4,256]{2,1,0:T(4,128)} %weight.1) | copy-start | bytes 786436
  0.0 14.4 %copy-start.1 = (s32[64,4,256]{2,1,0:T(4,128)S(1)}, s32[64,4,256]{2,1,0:T(4,128)}, u32[]{:S(2)}) copy-start(s32[64,4,256]{2,1,0:T(4,128)} %index.1) | copy-start | bytes 786436
  5.0 16.0 %collective-permute-start.1 = (bf16[33,16,256]{2,1,0:T(8,128)(2,1)}, bf16[33,16,256]{2,1,0:T(8,128)(2,1)S(1)}, u32[]{:S(2)}, u32[]{:S(2)}) collective-permute-start(bf16[33,16,256]{2,1,0:T(8,128)(2,1)} %get-tuple-element.17), channel_id=1, source_target_pairs={{1,2},{2,1},{3,4},{4,3},{5,6},{6,5},{7,8},{8,7},{9,10},{10,9},{11,... | collective-permute-start | bytes 811016 | tf_op jit(solution)/shard_map/ppermute | solution.py:554
  14.3 6.8 %collective-permute-start = (bf16[33,16,256]{2,1,0:T(8,128)(2,1)}, bf16[33,16,256]{2,1,0:T(8,128)(2,1)S(1)}, u32[]{:S(2)}, u32[]{:S(2)}) collective-permute-start(bf16[33,16,256]{2,1,0:T(8,128)(2,1)} %get-tuple-element.17), channel_id=1, source_target_pairs={{0,1},{1,0},{2,3},{3,2},{4,5},{5,4},{6,7},{7,6},{8,9},{9,8},{10,11... | collective-permute-start | bytes 811016 | tf_op jit(solution)/shard_map/ppermute | solution.py:554
  14.4 1.2 %copy-start = (f32[64,16,256]{2,1,0:T(8,128)S(1)}, f32[64,16,256]{2,1,0:T(8,128)}, u32[]{:S(2)}) copy-start(f32[64,16,256]{2,1,0:T(8,128)} %ssh.1) | copy-start | bytes 3145732
  15.6 0.7 copy-start.9
  16.3 4.8 %copy-start.5 = (bf16[256,512]{1,0:T(8,128)(2,1)S(1)}, bf16[256,512]{1,0:T(8,128)(2,1)}, u32[]{:S(2)}) copy-start(bf16[256,512]{1,0:T(8,128)(2,1)} %constant.6.clone.second) | copy-start | bytes 786436
  16.3 4.8 %copy-start.6 = (f32[16,256]{1,0:T(8,128)S(1)}, f32[16,256]{1,0:T(8,128)}, u32[]{:S(2)}) copy-start(f32[16,256]{1,0:T(8,128)} %constant.8.clone.tws) | copy-start | bytes 49156
  16.3 4.8 %copy-start.7 = (f32[16,256]{1,0:T(8,128)S(1)}, f32[16,256]{1,0:T(8,128)}, u32[]{:S(2)}) copy-start(f32[16,256]{1,0:T(8,128)} %constant.7.clone.twc) | copy-start | bytes 49156
  16.3 38.8 %slice-start = ((s8[16777216]{0:T(1024)(128)(4,1)}), s8[4194304]{0:T(1024)(128)(4,1)S(1)}, s32[]{:S(2)}) async-start(s8[16777216]{0:T(1024)(128)(4,1)} %bitcast.2), calls=%async_computation.2 | async-start | bytes 8388608
  16.3 38.8 %slice-start.1 = ((s8[16777216]{0:T(1024)(128)(4,1)}), s8[4194304]{0:T(1024)(128)(4,1)S(1)}, s32[]{:S(2)}) async-start(s8[16777216]{0:T(1024)(128)(4,1)} %bitcast.2), calls=%async_computation.3 | async-start | bytes 8388608
  21.1 34.0 %slice-start.2 = ((s8[16777216]{0:T(1024)(128)(4,1)}), s8[4194304]{0:T(1024)(128)(4,1)S(1)}, s32[]{:S(2)}) async-start(s8[16777216]{0:T(1024)(128)(4,1)} %bitcast.2), calls=%async_computation.4 | async-start | bytes 8388608
  21.1 34.0 %slice-start.3 = ((s8[16777216]{0:T(1024)(128)(4,1)}), s8[4194304]{0:T(1024)(128)(4,1)S(1)}, s32[]{:S(2)}) async-start(s8[16777216]{0:T(1024)(128)(4,1)} %bitcast.2), calls=%async_computation.5 | async-start | bytes 8388608
  21.1 34.0 %copy-start.3 = (f32[1024]{0:T(1024)S(1)}, f32[1024]{0:T(1024)}, u32[]{:S(2)}) copy-start(f32[1024]{0:T(1024)} %param.16) | copy-start | bytes 12292
  21.1 34.0 %copy-start.4 = (f32[1024]{0:T(1024)S(1)}, f32[1024]{0:T(1024)}, u32[]{:S(2)}) copy-start(f32[1024]{0:T(1024)} %param.17) | copy-start | bytes 12292
  90.7 13.9 %copy-start.8 = (bf16[32,256,256]{2,1,0:T(8,128)(2,1)S(1)}, bf16[32,256,256]{2,1,0:T(8,128)(2,1)}, u32[]{:S(2)}) copy-start(bf16[32,256,256]{2,1,0:T(8,128)(2,1)} %get-tuple-element.24.wt) | copy-start | bytes 12582916
  90.7 13.9 %collective-permute-start.2 = (bf16[32,16,256]{2,1,0:T(8,128)(2,1)S(1)}, bf16[32,16,256]{2,1,0:T(8,128)(2,1)S(1)}, u32[]{:S(2)}, u32[]{:S(2)}) collective-permute-start(bf16[32,16,256]{2,1,0:T(8,128)(2,1)S(1)} %get-tuple-element.22), channel_id=1, source_target_pairs={{1,2},{2,1},{3,4},{4,3},{5,6},{6,5},{7,8},{8,7},{9,10},{10,9},{11,... | collective-permute-start | bytes 786440 | tf_op jit(solution)/shard_map/ppermute | solution.py:554
  94.9 9.7 %collective-permute-start.3 = (bf16[32,16,256]{2,1,0:T(8,128)(2,1)S(1)}, bf16[32,16,256]{2,1,0:T(8,128)(2,1)S(1)}, u32[]{:S(2)}, u32[]{:S(2)}) collective-permute-start(bf16[32,16,256]{2,1,0:T(8,128)(2,1)S(1)} %get-tuple-element.23), channel_id=1, source_target_pairs={{0,1},{1,0},{2,3},{3,2},{4,5},{5,4},{6,7},{7,6},{8,9},{9,8},{10,11... | collective-permute-start | bytes 786440 | tf_op jit(solution)/shard_map/ppermute | solution.py:554
